TPU v7x, 32 devices: a whole 2x2x4 slice. The times are simulated.
32 devices in a mesh: ctx: 8 (over y, x, core), tp: 4 (over z).
Axes of the slice: x: 2, y: 2, z: 4, core: 2. Of those that a mesh axis runs over, the one named last changes fastest.
Arguments:
- queries: bfloat16 [4096, 8192], P('ctx', 'tp'), may hold values from -1.796875 to 1.796875
- keys: bfloat16 [4096, 8192], P('ctx', 'tp'), may hold values from -1.796875 to 1.796875
- values: bfloat16 [4096, 8192], P('ctx', 'tp'), may hold values from -12 to 12
- log_decay: float32 [64, 4096], P('tp', 'ctx'), may hold values from -2 to 0
- gain: float32 [8192], P('tp'), may hold values from 0.1 to 1.9
- grad_out: bfloat16 [4096, 8192], P('ctx', 'tp'), may hold values from -5 to 5
Outputs:
- normed: bfloat16 [4096, 8192], P('ctx', 'tp')
- grad_queries: bfloat16 [4096, 8192], P('ctx', 'tp')
- grad_keys: bfloat16 [4096, 8192], P('ctx', 'tp')
- grad_values: bfloat16 [4096, 8192], P('ctx', 'tp')
All inputs are finite; a program needn't handle non-finite values.
Results may differ from a plain program's by a relative error of at most 0.0069.
Values sent between devices are 32-bit elements; how exact they have to be, the bound alone decides.
No kernel may reach another device: no remote copies, remote signals or barrier semaphores. Data moves between devices by JAX's collectives and lax.ppermute only.
A program may use at most 128 MiB of HBM per device.

v0:
```python
import jax
import jax.numpy as jnp
from jax import lax
from jax.sharding import PartitionSpec as P

ATTENTION_HEADS = 64
E = 128
BLOCK = 512


EPSILON = 1e-05


def prefix(shard, axis, combine, identity, reverse):
    devices, place = (lax.axis_size(axis), lax.axis_index(axis))
    everything = jax.tree.map(lambda part: lax.all_gather(part, axis), shard)
    start = jax.tree.map(
        lambda part, zero: jnp.broadcast_to(jnp.asarray(zero, part.dtype), part.shape),
        shard,
        identity,
    )

    def lap(k, before):
        at = devices - 1 - k if reverse else k
        reached = at > place if reverse else at < place
        new = combine(before, jax.tree.map(lambda part: part[at], everything))
        return jax.tree.map(lambda a, b: jnp.where(reached, a, b), new, before)

    return lax.fori_loop(0, devices, lap, start)


def chain_states(earlier, later):
    return (earlier[0] * later[0], later[0][:, None, None] * earlier[1] + later[1])


def per_device(queries, keys, values, log_decay, gain, grad_out):
    heads = log_decay.shape[0]
    tok_rows = log_decay.shape[1]
    blocks = tok_rows // BLOCK
    shape_four = (blocks, BLOCK, heads, E)
    query_blk = queries.reshape(shape_four)
    key_blk = keys.reshape(shape_four)
    value_blk = values.reshape(shape_four)
    decay_blk = log_decay.reshape(heads, blocks, BLOCK).transpose(1, 0, 2)
    cumulative = jnp.cumsum(decay_blk, axis=2)
    totals = cumulative[:, :, -1]
    factors = jnp.exp(totals)
    row_pos = lax.broadcasted_iota(jnp.int32, (BLOCK, BLOCK), 0)
    col_pos = lax.broadcasted_iota(jnp.int32, (BLOCK, BLOCK), 1)
    causal = row_pos >= col_pos
    spread = cumulative[:, :, :, None] - cumulative[:, :, None, :]
    weights = jnp.exp(jnp.where(causal, spread, -1e30))
    scores = jnp.einsum("nthe,nshe->nhts", query_blk, key_blk, preferred_element_type=jnp.float32)
    probs = (scores * weights).astype(jnp.bfloat16)
    rise = jnp.exp(cumulative).transpose(0, 2, 1)[:, :, :, None]
    fall = jnp.exp(totals[:, :, None] - cumulative).transpose(0, 2, 1)[:, :, :, None]
    query_dec = (query_blk * rise).astype(jnp.bfloat16)
    key_dec = (key_blk * fall).astype(jnp.bfloat16)
    contrib = jnp.einsum("nshe,nshf->nhef", key_dec, value_blk, preferred_element_type=jnp.float32)
    local_state = jnp.zeros((heads, E, E), jnp.float32)
    block_id = 0
    local_state = factors[block_id][:, None, None] * local_state + contrib[block_id]
    device_decay = jnp.prod(factors, axis=0)
    identity = (jnp.ones_like(device_decay), jnp.zeros_like(local_state))
    incoming = prefix((device_decay, local_state), "ctx", chain_states, identity, False)[1]
    current = incoming
    block_id = 0
    entering = [current]
    state_half = jnp.stack(entering).astype(jnp.bfloat16)
    attended = jnp.einsum(
        "nhts,nshe->nthe", probs, value_blk, preferred_element_type=jnp.float32
    ) + jnp.einsum("nthe,nhef->nthf", query_dec, state_half, preferred_element_type=jnp.float32)
    attended = attended.reshape(tok_rows, heads * E)
    squares = jnp.sum(attended * attended, axis=1)
    scaled_grad = gain[None, :] * grad_out.astype(jnp.float32)
    crossed = jnp.sum(scaled_grad * attended, axis=1)
    square_total = lax.psum(squares, "tp")
    inverse = lax.rsqrt(square_total / (ATTENTION_HEADS * E) + EPSILON)
    normed = (gain[None, :] * attended * inverse[:, None]).astype(jnp.bfloat16)
    cross_total = lax.psum(crossed, "tp")
    d_attended = (
        inverse[:, None] * scaled_grad
        - attended * (inverse**3 * cross_total / (ATTENTION_HEADS * E))[:, None]
    ).astype(jnp.bfloat16)
    grad_blk = d_attended.reshape(shape_four)
    state_grad = jnp.einsum(
        "nthe,nthf->nhef", query_dec, grad_blk, preferred_element_type=jnp.float32
    )
    local_grad = jnp.zeros((heads, E, E), jnp.float32)
    for block_id in reversed(range(blocks)):
        local_grad = factors[block_id][:, None, None] * local_grad + state_grad[block_id]
    d_prob = jnp.einsum("nthe,nshe->nhts", grad_blk, value_blk, preferred_element_type=jnp.float32)
    d_scores = (d_prob * weights).astype(jnp.bfloat16)
    intra_q = jnp.einsum("nhts,nshe->nthe", d_scores, key_blk, preferred_element_type=jnp.float32)
    intra_k = jnp.einsum("nhts,nthe->nshe", d_scores, query_blk, preferred_element_type=jnp.float32)
    intra_v = jnp.einsum("nhts,nthe->nshe", probs, grad_blk, preferred_element_type=jnp.float32)
    grad_q = intra_q + rise * jnp.einsum(
        "nthf,nhef->nthe", grad_blk, state_half, preferred_element_type=jnp.float32
    )
    identity = (jnp.ones_like(device_decay), jnp.zeros_like(local_grad))
    outgoing = prefix((device_decay, local_grad), "ctx", chain_states, identity, True)[1]
    leaving = [outgoing] * blocks
    current = outgoing
    for block_id in reversed(range(blocks)):
        leaving[block_id] = current
        current = factors[block_id][:, None, None] * current + state_grad[block_id]
    leave_half = jnp.stack(leaving).astype(jnp.bfloat16)
    grad_k = intra_k + fall * jnp.einsum(
        "nshf,nhef->nshe", value_blk, leave_half, preferred_element_type=jnp.float32
    )
    grad_v = intra_v + jnp.einsum(
        "nshe,nhef->nshf", key_dec, leave_half, preferred_element_type=jnp.float32
    )
    return (
        normed,
        grad_q.reshape(tok_rows, heads * E).astype(jnp.bfloat16),
        grad_k.reshape(tok_rows, heads * E).astype(jnp.bfloat16),
        grad_v.reshape(tok_rows, heads * E).astype(jnp.bfloat16),
    )


def solution(mesh):
    in_specs = (
        P("ctx", "tp"),
        P("ctx", "tp"),
        P("ctx", "tp"),
        P("tp", "ctx"),
        P("tp"),
        P("ctx", "tp"),
    )
    out_specs = (P("ctx", "tp"), P("ctx", "tp"), P("ctx", "tp"), P("ctx", "tp"))
    return jax.shard_map(
        per_device, mesh=mesh, in_specs=in_specs, out_specs=out_specs, check_vma=False
    )
```

profile of v0, /device:TPU:0, one launch (start us, length us, event | category | flops | bytes accessed | tf_op | source)
XLA Modules:
  0.0 222.9 jit_solution(16730702211006540905)
XLA Ops:
  7.2 0.9 reshape.285
  8.2 1.2 reduce-window.6
  9.9 4.7 %fusion.19 = f32[16,128,128]{2,1,0:T(8,128)} fusion(f32[512,16]{0,1:T(8,128)S(1)} %copy.136, f32[16]{0:T(128)S(1)} %exponential_multiply_fusion, bf16[512,2048]{1,0:T(8,128)(2,1)S(1)} %copy-done, bf16[512,2048]{1,0:T(8,128)(2,1)} %param.11), kind=kOutput, calls=%fused_computation.37 | convolution fusion | flops 271843328 | bytes 5275712 | tf_op jit(solution)/shard_map/nshe,nshf->nhef/dot_general | solution.py:59
  14.7 0.7 broadcast.66
  15.5 1.0 copy.164
  16.6 3.9 %copy.165 = bf16[512,2048]{0,1:T(8,128)(2,1)} copy(bf16[512,2048]{1,0:T(8,128)(2,1)} %param.10) | data formatting | bytes 4194304 | tf_op jit(solution)/shard_map/reshape.3
  20.5 10.2 %all-gather = f32[8,16,1]{1,2,0:T(1,128)S(1)} all-gather(f32[1,16,1]{1,2,0:T(1,128)S(1)} %get-tuple-element.315), channel_id=2, replica_groups=mesh['ctx'=8,'tp'=4] {'ctx'}, dimensions={0}, use_global_device_ids=true | all-gather | bytes 576 | tf_op jit(solution)/shard_map/all_gather | solution.py:16
  30.8 0.6 copy-done.5
  31.4 9.0 %multiply_convert_fusion.1 = bf16[16,512,512]{2,1,0:T(8,128)(2,1)} fusion(bf16[512,16,128]{0,2,1:T(8,128)(2,1)} %bitcast.157, f32[16,512]{1,0:T(8,128)S(1)} %bitcast_add_fusion.4, pred[512,512]{1,0:T(8,128)(4,1)S(1)} %iota_compare_fusion, bf16[512,2048]{1,0:T(8,128)(2,1)} %param.11), kind=kOutput, calls=%fused_computation.7 | convolution fusion | flops 1090519040 | bytes 12877824 | tf_op jit(solution)/shard_map/nthe,nshe->nhts/dot_general | solution.py:53
  40.5 31.4 %all-gather.6.cloned.1.call-done = f32[128,128,128]{2,1,0:T(8,128)} async-done(((f32[16,128,128]{2,1,0:T(8,128)}), f32[128,128,128]{2,1,0:T(8,128)}) %all-gather.6.cloned.1.call-update) | async-done | bytes 8388624 | tf_op jit(solution)/shard_map/all_gather | solution.py:16
  71.9 12.0 %while.30 = (s32[]{:T(128)}, f32[16,128,128]{2,1,0:T(8,128)S(1)}, s32[]{:T(128)}, f32[8,16]{1,0:T(8,128)S(1)}, f32[8,16,128,128]{3,2,1,0:T(8,128)}, /*index=5*/s32[]{:T(128)}, s32[]{:T(128)}) while((s32[]{:T(128)}, f32[16,128,128]{2,1,0:T(8,128)S(1)}, s32[]{:T(128)}, f32[8,16]{1,0:T(8,128)S(1)}, f32[8,16,128,128]{3,2,1,0:T(8,128)}, ...), condition=%wide.region_3.4_spmd.clone, body=%wide.region_2.3_spmd.clone.sunk | while | flops 1048580 | bytes 3146033 | solution.py:29
  71.9 1.5 fusion.57
  73.4 1.5 fusion.57
  74.9 1.5 fusion.57
  76.4 1.5 fusion.57
  77.9 1.5 fusion.57
  79.4 1.5 fusion.57
  80.9 1.5 fusion.57
  82.4 1.5 fusion.57
  83.9 2.3 %fusion.17 = f32[16,128,512]{2,1,0:T(8,128)S(1)} fusion(bf16[512,16,128]{0,2,1:T(8,128)(2,1)} %bitcast.158, f32[512,16]{0,1:T(8,128)S(1)} %copy.140, f32[16,128,128]{2,1,0:T(8,128)S(1)} %get-tuple-element.230), kind=kOutput, calls=%fused_computation.35 | convolution fusion | flops 271843328 | bytes 7372800 | tf_op jit(solution)/shard_map/nthe,nhef->nthf/dot_general | solution.py:72
  86.2 8.2 %fusion.6 = (f32[512]{0:T(512)S(1)}, f32[16,128,512]{2,1,0:T(8,128)}) fusion(f32[16,128,512]{2,1,0:T(8,128)S(1)} %fusion.17, bf16[16,512,512]{2,1,0:T(8,128)(2,1)} %multiply_convert_fusion.1, bf16[512,2048]{1,0:T(8,128)(2,1)S(1)} %copy-done), kind=kOutput, calls=%fused_computation.16 | convolution fusion | flops 1076887040 | bytes 18876416 | tf_op jit(solution)/shard_map/nhts,nshe->nthe/dot_general | solution.py:70
  94.4 5.5 %copy.143 = f32[512,2048]{1,0:T(8,128)} copy(f32[512,2048]{0,1:T(8,128)} %bitcast.161) | data formatting | bytes 8388608 | tf_op jit(solution)/shard_map/reshape | solution.py:73
  99.9 3.5 %multiply_reduce_fusion = f32[512]{0:T(512)S(1)} fusion(f32[512,2048]{1,0:T(8,128)} %copy.143, bf16[512,2048]{1,0:T(8,128)(2,1)} %param.15, f32[2048]{0:T(1024)S(1)} %copy-done.7), kind=kLoop, calls=%fused_computation.20 | loop fusion | flops 4193792 | bytes 6301696 | tf_op jit(solution)/shard_map/reduce_sum | solution.py:76
  103.4 11.9 %all-reduce = (f32[512]{0:T(512)S(1)}, f32[512]{0:T(512)S(1)}) all-reduce(f32[512]{0:T(512)S(1)} %get-tuple-element.318, f32[512]{0:T(512)S(1)} %multiply_reduce_fusion), channel_id=1, replica_groups=mesh['ctx'=8,'tp'=4] {'tp'}, use_global_device_ids=true, to_apply=%region_5.6 | all-reduce | flops 1024 | bytes 8192 | tf_op jit(solution)/shard_map/psum | solution.py:77
  115.3 6.2 %subtract_convert_fusion = (bf16[512,2048]{1,0:T(8,128)(2,1)}, bf16[512,2048]{1,0:T(8,128)(2,1)}) fusion(f32[512,2048]{1,0:T(8,128)} %copy.143, bf16[512,2048]{1,0:T(8,128)(2,1)} %param.15, f32[512]{0:T(512)S(1)} %get-tuple-element.316, f32[512]{0:T(512)S(1)} %get-tuple-element.317, f32[2048]{0:T(1024)S(1)} %copy-done.7), kind=kLoop, calls=%fused_computation.19 | loop fusion | flops 9437184 | bytes 10498048 | tf_op jit(solution)/shard_map/convert_element_type | solution.py:84
  121.5 3.9 %copy.166 = bf16[512,2048]{0,1:T(8,128)(2,1)} copy(bf16[512,2048]{1,0:T(8,128)(2,1)} %get-tuple-element.312) | data formatting | bytes 4194304 | tf_op jit(solution)/shard_map/reshape.39
  125.4 3.9 %fusion.18 = f32[16,128,128]{2,1,0:T(8,128)} fusion(bf16[512,16,128]{0,2,1:T(8,128)(2,1)} %bitcast.153, bf16[512,16,128]{0,2,1:T(8,128)(2,1)} %bitcast.159, f32[512,16]{0,1:T(8,128)S(1)} %copy.140, f32[16]{0:T(128)S(1)} %exponential_multiply_fusion), kind=kOutput, calls=%fused_computation.36 | convolution fusion | flops 271843328 | bytes 5275712 | tf_op jit(solution)/shard_map/nthe,nthf->nhef/dot_general | solution.py:86
  129.4 6.4 %multiply_convert_fusion = bf16[16,512,512]{2,1,0:T(8,128)(2,1)S(1)} fusion(bf16[512,16,128]{0,2,1:T(8,128)(2,1)} %bitcast.154, f32[16,512]{1,0:T(8,128)S(1)} %copy-done.6, pred[512,512]{1,0:T(8,128)(4,1)S(1)} %iota_compare_fusion, bf16[512,2048]{1,0:T(8,128)(2,1)S(1)} %copy-done), kind=kOutput, calls=%fused_computation.6 | convolution fusion | flops 1090519040 | bytes 12877824 | tf_op jit(solution)/shard_map/nthe,nshe->nhts/dot_general | solution.py:92
  135.8 8.0 %fusion.13 = f32[16,512,128]{1,2,0:T(8,128)} fusion(bf16[16,512,512]{2,1,0:T(8,128)(2,1)S(1)} %multiply_convert_fusion, bf16[512,2048]{1,0:T(8,128)(2,1)} %param.11), kind=kOutput, calls=%fused_computation.31 | convolution fusion | flops 1073741824 | bytes 14680064 | tf_op jit(solution)/shard_map/nhts,nshe->nthe/dot_general | solution.py:94
  143.8 4.8 %fusion.5 = bf16[1,512,16,128]{1,3,2,0:T(8,128)(2,1)} fusion(f32[16,512,128]{1,2,0:T(8,128)} %fusion.13, bf16[512,16,128]{0,2,1:T(8,128)(2,1)} %bitcast.155, f32[512,16]{0,1:T(8,128)S(1)} %copy.140, f32[16,128,128]{2,1,0:T(8,128)S(1)} %get-tuple-element.230), kind=kOutput, calls=%fused_computation.14 | convolution fusion | flops 271843328 | bytes 9469952 | tf_op jit(solution)/shard_map/nthf,nhef->nthe/dot_general | solution.py:97
  148.6 3.9 %copy.157 = bf16[512,2048]{1,0:T(8,128)(2,1)} copy(bf16[512,2048]{0,1:T(8,128)(2,1)} %bitcast.162) | data formatting | bytes 4194304
  152.6 8.7 %fusion.36 = f32[16,128,512]{2,1,0:T(8,128)} fusion(bf16[512,16,128]{0,2,1:T(8,128)(2,1)} %bitcast.156, bf16[16,512,512]{2,1,0:T(8,128)(2,1)} %multiply_convert_fusion.1), kind=kOutput, calls=%fused_computation.64 | convolution fusion | flops 1073741824 | bytes 14680064 | tf_op jit(solution)/shard_map/nhts,nthe->nshe/dot_general | solution.py:96
  161.2 19.9 %all-gather.8.cloned.1.call-done = f32[128,128,128]{2,1,0:T(8,128)} async-done(((f32[16,128,128]{2,1,0:T(8,128)}), f32[128,128,128]{2,1,0:T(8,128)}) %all-gather.8.cloned.1.call-update) | async-done | bytes 8388624 | tf_op jit(solution)/shard_map/all_gather | solution.py:16
  181.1 12.0 %while.31 = (s32[]{:T(128)}, f32[16,128,128]{2,1,0:T(8,128)S(1)}, s32[]{:T(128)}, f32[8,16]{1,0:T(8,128)S(1)}, f32[8,16,128,128]{3,2,1,0:T(8,128)}, /*index=5*/s32[]{:T(128)}, s32[]{:T(128)}, s32[]{:T(128)}, s32[]{:T(128)}) while((s32[]{:T(128)}, f32[16,128,128]{2,1,0:T(8,128)S(1)}, s32[]{:T(128)}, f32[8,16]{1,0:T(8,128)S(1)}, ...), condition=%wide.region_9.10_spmd.clone, body=%wide.region_8.9_spmd.clone.sunk | while | flops 1048584 | bytes 3146095 | solution.py:29
  181.1 1.5 fusion.58
  182.6 1.5 fusion.58
  184.1 1.5 fusion.58
  185.6 1.5 fusion.58
  187.2 1.5 fusion.58
  188.7 1.5 fusion.58
  190.2 1.5 fusion.58
  191.7 1.5 fusion.58
  193.2 2.9 %fusion.8 = f32[16,128,512]{2,1,0:T(8,128)} fusion(f32[16,128,128]{2,1,0:T(8,128)S(1)} %get-tuple-element.231, bf16[512,2048]{1,0:T(8,128)(2,1)S(1)} %copy-done), kind=kOutput, calls=%fused_computation.26 | convolution fusion | flops 268697600 | bytes 7340032 | tf_op jit(solution)/shard_map/nshf,nhef->nshe/dot_general | solution.py:108
  196.6 1.0 copy-done.4
  197.5 2.9 %add_convert_fusion = bf16[16,128,512]{2,1,0:T(8,128)(2,1)} fusion(f32[16,128,512]{2,1,0:T(8,128)S(1)} %copy-done.3, f32[512,16]{0,1:T(8,128)S(1)} %copy.136, f32[16,128,128]{2,1,0:T(8,128)S(1)} %get-tuple-element.231, bf16[512,2048]{1,0:T(8,128)(2,1)S(1)} %copy-done.4), kind=kOutput, calls=%fused_computation.18 | convolution fusion | flops 273940480 | bytes 9469952 | tf_op jit(solution)/shard_map/nshe,nhef->nshf/dot_general | solution.py:111
  200.4 3.9 %copy.159 = bf16[512,2048]{1,0:T(8,128)(2,1)} copy(bf16[512,2048]{0,1:T(8,128)(2,1)} %bitcast.163) | data formatting | bytes 4194304
  204.3 7.8 %fusion.3 = bf16[1,512,16,128]{1,3,2,0:T(8,128)(2,1)} fusion(f32[16,128,512]{2,1,0:T(8,128)} %fusion.8, bf16[512,16,128]{0,2,1:T(8,128)(2,1)} %bitcast.160, bf16[16,512,512]{2,1,0:T(8,128)(2,1)} %copy-done.2, f32[512,16]{0,1:T(8,128)S(1)} %copy.136), kind=kOutput, calls=%fused_computation.11 | convolution fusion | flops 1076887552 | bytes 16809984 | tf_op jit(solution)/shard_map/nhts,nthe->nshe/dot_general | solution.py:95
  212.1 3.9 %copy.158 = bf16[512,2048]{1,0:T(8,128)(2,1)} copy(bf16[512,2048]{0,1:T(8,128)(2,1)} %bitcast.164) | data formatting | bytes 4194304
  (52 shorter events, 1.6 us)
Async XLA Ops:
  7.2 2.7 %copy-start = (bf16[512,2048]{1,0:T(8,128)(2,1)S(1)}, bf16[512,2048]{1,0:T(8,128)(2,1)}, u32[]{:S(2)}) copy-start(bf16[512,2048]{1,0:T(8,128)(2,1)} %param.12) | copy-start | bytes 6291460
  7.2 64.7 %all-gather.6.cloned.1.call-start = ((), (), s32[]{:S(2)}) async-start(), calls=%async_computation | async-start | bytes 9437184 | tf_op jit(solution)/shard_map/all_gather | solution.py:16
  14.6 166.5 %all-gather.8.cloned.1.call-start = ((), (), s32[]{:S(2)}) async-start(), calls=%async_computation.1 | async-start | bytes 9437184 | tf_op jit(solution)/shard_map/all_gather | solution.py:16
  30.8 0.6 copy-start.5
  94.4 5.5 %copy-start.7 = (f32[2048]{0:T(1024)S(1)}, f32[2048]{0:T(1024)}, u32[]{:S(2)}) copy-start(f32[2048]{0:T(1024)} %param.14) | copy-start | bytes 24580
  125.4 4.0 %copy-start.6 = (f32[16,512]{1,0:T(8,128)S(1)}, f32[16,512]{1,0:T(8,128)}, u32[]{:S(2)}) copy-start(f32[16,512]{1,0:T(8,128)} %copy-done.5) | copy-start | bytes 98308
  135.8 8.0 %copy-start.2 = (bf16[16,512,512]{2,1,0:T(8,128)(2,1)}, bf16[16,512,512]{2,1,0:T(8,128)(2,1)S(1)}, u32[]{:S(2)}) copy-start(bf16[16,512,512]{2,1,0:T(8,128)(2,1)S(1)} %multiply_convert_fusion) | copy-start | bytes 25165828
  152.5 28.6 %copy-start.1 = (f32[16,128,128]{2,1,0:T(8,128)S(1)}, f32[16,128,128]{2,1,0:T(8,128)}, u32[]{:S(2)}) copy-start(f32[16,128,128]{2,1,0:T(8,128)} %custom-call.1) | copy-start | bytes 3145732
  193.2 3.4 %copy-start.3 = (f32[16,128,512]{2,1,0:T(8,128)S(1)}, f32[16,128,512]{2,1,0:T(8,128)}, u32[]{:S(2)}) copy-start(f32[16,128,512]{2,1,0:T(8,128)} %fusion.36) | copy-start | bytes 12582916
  193.2 4.4 %copy-start.4 = (bf16[512,2048]{1,0:T(8,128)(2,1)S(1)}, bf16[512,2048]{1,0:T(8,128)(2,1)}, u32[]{:S(2)}) copy-start(bf16[512,2048]{1,0:T(8,128)(2,1)} %param.11) | copy-start | bytes 6291460
Sparse Core Ops, SparseCore 0:
  14.8 57.0 all-gather.5
  129.5 51.5 all-gather.7
where the time goes:
time: 224 us; the launch traced here: 223 us
  matrix products  69.7 us (31%)
  waiting for transfers between devices  51.4 us (23%)
  other arithmetic  34.4 us (15%)
  local copies, waits for them, and re-layouts  30.5 us (14%)
  blocking collectives  22.1 us (10%)
  between operations  14.2 us (6%)
    all_gather x2, waiting for transfers between devices, prefix(): everything = jax.tree.map(lambda part: lax.all_gather(part, axis), shard)  51.3 us
    select_n x16, other arithmetic, lap(): return jax.tree.map(lambda a, b: jnp.where(reached, a, b), new, before)  23.4 us
    unnamed x19, local copies, waits for them, and re-layouts  13.9 us
    psum x1, blocking collectives, per_device(): square_total = lax.psum(squares, 'tp')  11.9 us
    all_gather x1, blocking collectives, prefix(): everything = jax.tree.map(lambda part: lax.all_gather(part, axis), shard)  10.2 us
    another operation x8, local copies, waits for them, and re-layouts  9.78 us
    dot_general x1, matrix products, per_device(): jnp.einsum('nthe,nshe->nhts', query_blk, key_blk, preferred_element_type=...  9.02 us
    dot_general x1, matrix products, per_device(): jnp.einsum('nhts,nthe->nshe', probs, grad_blk, preferred_element_type=jnp...  8.68 us
  transfers between devices with their start and end apart: 2, of which 2 were waited for; matrix products, arithmetic and copies ran while one was open for 21% of the time, Pallas kernels for 0%

commit v1 on v0

v1 whole, which is shorter than its diff:
```python
import functools

import jax
import jax.numpy as jnp
from jax import lax
from jax.experimental import pallas as pl
from jax.experimental.pallas import tpu as pltpu
from jax.sharding import PartitionSpec as P

E = 128
BLOCK = 512
CHUNK = 256
CHUNKS = BLOCK // CHUNK
EPSILON = 1e-05
PARTS = 2

F32 = jnp.float32
BF16 = jnp.bfloat16
IN_VMEM = pl.BlockSpec(memory_space=pltpu.VMEM)
ANY = pl.BlockSpec(memory_space=pl.ANY)
MIB = 1 << 20


def call(kernel, outs, *args, flops=0, anywhere=(), after=(), outs_anywhere=0, scratch=(), alias=None, limit=8):
    args = (*args, *after)
    skip = len(after)

    def body(*refs):
        kept = len(args) - skip
        kernel(*refs[:kept], *refs[len(args) :])

    in_specs = [IN_VMEM] * (len(args) - skip) + [ANY] * skip
    for operand in anywhere:
        in_specs[operand] = ANY
    return pl.pallas_call(
        body,
        out_shape=[
            jax.ShapeDtypeStruct(shape, dtype) if n < outs_anywhere else pltpu.VMEM(shape, dtype)
            for n, (shape, dtype) in enumerate(outs)
        ],
        in_specs=in_specs,
        out_specs=[ANY] * outs_anywhere + [IN_VMEM] * (len(outs) - outs_anywhere),
        scratch_shapes=scratch,
        input_output_aliases=alias or {},
        compiler_params=pltpu.CompilerParams(vmem_limit_bytes=limit * MIB),
        cost_estimate=pl.CostEstimate(flops=flops, bytes_accessed=0, transcendentals=0),
    )(*args)


def dot(a, b, contract):
    return lax.dot_general(a, b, ((contract[:1], contract[1:]), ((), ())), preferred_element_type=F32)


def span(i, n=1):
    return slice(i * E, (i + n) * E)


def chunk(c):
    return slice(c * CHUNK, (c + 1) * CHUNK)


def bits(reverse=False):
    me = lax.axis_index("ctx")
    if reverse:
        me = 7 - me
    return me & 1, (me >> 1) & 1, me >> 2


def columns(half, i, n=1):
    if half is None:
        return span(i, n)
    core = lax.axis_index("ctx") & 1
    base = core if i < half else 1 - core
    return pl.ds(pl.multiple_of(base * (half * E) + (i % half) * E, E), n * E)


def head_rows(half, i, n):
    core = lax.axis_index("ctx") & 1
    base = core if i < half else 1 - core
    return pl.ds(pl.multiple_of(base * half, half), n)


def contribution(half, index, keys, values, fall_row, factor, contrib, early):
    for n, i in enumerate(index):
        cols = columns(half, i)
        dec = (keys[:, cols].T.astype(F32) * fall_row[i : i + 1, :]).astype(BF16)
        v = values[:, cols]
        total = None
        for c in range(CHUNKS):
            new = dot(dec[:, chunk(c)], v[chunk(c)], (1, 0))
            if c > 0:
                total = factor[c][i : i + 1, :] * total + new
            else:
                total = new
            if c < CHUNKS - 1:
                early[span(n), :] = total
        contrib[span(n), :] = total


def start_kernel(half, order, first, heads, log_decay, keys, values, cum_row, rise_row, fall_row, factor, k_out, v_out, contrib, early, rows, sems):
    rows[...] = jnp.zeros_like(rows)
    moves = []
    if half is None:
        moves.append(pltpu.make_async_copy(log_decay, rows.at[0:heads, :], sems.at[0]))
    else:
        for n, i in enumerate((0, half)):
            source = log_decay.at[head_rows(half, i, half), :]
            moves.append(pltpu.make_async_copy(source, rows.at[i : i + half, :], sems.at[n]))
    for move in moves:
        move.start()
    pieces = []
    for n, (i, count) in enumerate(order):
        cols = columns(half, i, count)
        pieces.append(
            [
                pltpu.make_async_copy(keys.at[:, cols], k_out.at[:, cols], sems.at[2 + 2 * n]),
                pltpu.make_async_copy(values.at[:, cols], v_out.at[:, cols], sems.at[3 + 2 * n]),
            ]
        )
        for move in pieces[-1]:
            move.start()
    up_to = (
        lax.broadcasted_iota(jnp.int32, (CHUNK, CHUNK), 0)
        <= lax.broadcasted_iota(jnp.int32, (CHUNK, CHUNK), 1)
    ).astype(F32).astype(BF16)
    for move in moves:
        move.wait()
    for c in range(CHUNKS):
        whole = rows[:, chunk(c)]
        high = whole.astype(BF16)
        rest = whole - high.astype(F32)
        middle = rest.astype(BF16)
        low = (rest - middle.astype(F32)).astype(BF16)
        cum = (dot(low, up_to, (1, 0)) + dot(middle, up_to, (1, 0))) + dot(high, up_to, (1, 0))
        total = cum[:, CHUNK - 1 : CHUNK]
        cum_row[:, chunk(c)] = cum
        rise_row[:, chunk(c)] = jnp.exp(cum)
        fall_row[:, chunk(c)] = jnp.exp(total - cum)
        factor[c] = jnp.broadcast_to(jnp.exp(total), (total.shape[0], E))
    whole = factor[0]
    for c in range(1, CHUNKS):
        whole = whole * factor[c]
    factor[CHUNKS] = whole
    for move in pieces[0]:
        move.wait()
    contribution(half, first, k_out, v_out, fall_row, factor, contrib, early)
    for piece in pieces[1:]:
        for move in piece:
            move.wait()


def contrib_kernel(half, index, keys, values, fall_row, factor, contrib, early):
    contribution(half, index, keys, values, fall_row, factor, contrib, early)


def column_kernel(cum_row, cum_col, rise_col, fall_col, rows):
    rows[...] = jnp.zeros_like(rows)
    rows[0 : cum_row.shape[0], :] = cum_row[...]
    col = rows[...].T
    cum_col[...] = col
    rise_col[...] = jnp.exp(col)
    for c in range(CHUNKS):
        fall_col[chunk(c), :] = jnp.exp(col[(c + 1) * CHUNK - 1 : (c + 1) * CHUNK, :] - col[chunk(c)])


def chip_kernel(count, reverse, kept, got, own_factor, other_factor, *sums):
    lower = bits(reverse)[0] == 0
    for n in range(len(sums) * count):
        mine = jnp.where(lower, other_factor[n : n + 1, :], 1.0)
        theirs = jnp.where(lower, 1.0, own_factor[n : n + 1, :])
        sums[n // count][span(n % count), :] = mine * kept[span(n), :] + theirs * got[span(n), :]


def second_kernel(reverse, got_x, own_x, got_y, own_y, factor, factor_x, factor_d, send_y, send_x):
    _, x, y = bits(reverse)
    right, later = x == 1, y == 1
    count = got_x.shape[0] // E
    for n in range(count):
        f, fx = factor[n : n + 1, :], factor_x[n : n + 1, :]
        p = jnp.where(right, f, 1.0)
        q = jnp.where(right, 1.0, fx)
        send_y[span(n), :] = p * got_x[span(n), :] + q * own_x[span(n), :]
        n2 = count + n
        f, fd = factor[n2 : n2 + 1, :], factor_d[n2 : n2 + 1, :]
        p = jnp.where(later, jnp.where(right, 1.0, f * fd), 0.0)
        q = jnp.where(later, jnp.where(right, 0.0, jnp.ones_like(f)), 1.0)
        send_x[span(n), :] = p * got_y[span(n), :] + q * own_y[span(n), :]


def enter_kernel(reverse, one_x, two_y, one_y, two_x, factor_x, factor_d, own_factor, other_factor, kept, got, mine, send):
    core, x, y = bits(reverse)
    lower, right, later = core == 0, x == 1, y == 1
    count = one_x.shape[0] // E
    for n in range(2 * count):
        fx, fd = factor_x[n : n + 1, :], factor_d[n : n + 1, :]
        one = jnp.ones_like(fx)
        if n < count:
            first, second = one_x[span(n), :], two_y[span(n), :]
            w = jnp.where(right, one, 0.0)
            u = jnp.where(later, jnp.where(right, fx, 1.0), 0.0)
        else:
            first, second = one_y[span(n - count), :], two_x[span(n - count), :]
            w = jnp.where(later, jnp.where(right, fx, fd), 0.0)
            u = jnp.where(later, one, jnp.where(right, one, 0.0))
        low = w * first + u * second
        f = jnp.where(lower, own_factor[n : n + 1, :], other_factor[n : n + 1, :])
        high = f * low + jnp.where(lower, kept[span(n), :], got[span(n), :])
        mine[span(n), :] = jnp.where(lower, low, high)
        send[span(n), :] = jnp.where(lower, high, low)


def intra_kernel(half, index, queries, keys, values, cum_row, rise_row, cum_col, rise_col, fall_col, intra, query_dec, query_dec_t, key_dec, value_dec):
    causal = lax.broadcasted_iota(jnp.int32, (CHUNK, CHUNK), 0) >= lax.broadcasted_iota(
        jnp.int32, (CHUNK, CHUNK), 1
    )
    for n, i in enumerate(index):
        cols = columns(half, i)
        q, k, v = queries[:, cols], keys[:, cols], values[:, cols]
        rise, fall = rise_col[:, i : i + 1], fall_col[:, i : i + 1]
        query_dec[:, span(n)] = (q.astype(F32) * rise).astype(BF16)
        query_dec_t[span(n), :] = (q.T.astype(F32) * rise_row[i : i + 1, :]).astype(BF16)
        key_dec[:, span(n)] = (k.astype(F32) * fall).astype(BF16)
        value_dec[:, span(n)] = (v.astype(F32) * fall).astype(BF16)
        for c in range(CHUNKS):
            at = chunk(c)
            spread = cum_col[at, i : i + 1] - cum_row[i : i + 1, at]
            weight = jnp.exp(jnp.where(causal, spread, -1e30))
            probs = (dot(q[at], k[at], (1, 1)) * weight).astype(BF16)
            intra[at, span(n)] = dot(probs, v[at], (1, 0))


def attend_kernel(half, index, query_dec, intra, entering, early, factor, grad_out, gain, *refs):
    if len(refs) == 6:
        total, cross = refs[0][...], refs[1][...]
    else:
        total = cross = jnp.zeros((BLOCK, E), F32)
    attended, state, squares, crossed = refs[-4:]
    totals, crosses = [], []
    for c in range(CHUNKS):
        at = chunk(c)
        totals.append(total[at])
        crosses.append(cross[at])
    for n, i in enumerate(index):
        cols = columns(half, i)
        now = entering[span(n), :]
        for c in range(CHUNKS):
            at = chunk(c)
            if c > 0:
                now = factor[0, i : i + 1, :] * now + early[span(n), :]
            rounded = now.astype(BF16)
            state[c, span(n), :] = rounded
            out = intra[at, span(n)] + dot(query_dec[at, span(n)], rounded, (1, 0))
            attended[at, span(n)] = out
            totals[c] += out * out
            crosses[c] += (gain[:, cols] * grad_out[at, cols].astype(F32)) * out
    for c in range(CHUNKS):
        squares[chunk(c), :] = totals[c]
        crossed[chunk(c), :] = crosses[c]


def sum_kernel(squares, crossed, sums):
    ones = jnp.ones((8, E), F32)

    def row(x):
        return lax.dot_general(
            ones, x, (((1,), (1,)), ((), ())), precision=lax.Precision.HIGHEST, preferred_element_type=F32
        )

    first = lax.broadcasted_iota(jnp.int32, (8, BLOCK), 0) == 0
    sums[...] = jnp.where(first, row(squares[...]), row(crossed[...]))


def scale_kernel(features, ours, theirs, inverse, coefficient):
    sums = ours[...] + theirs[...]
    inv = lax.rsqrt(sums[0:1, :] / features + EPSILON)
    coef = inv * inv * inv * sums[1:2, :] / features
    inverse[...] = jnp.broadcast_to(inv, (E, BLOCK)).T
    coefficient[...] = jnp.broadcast_to(coef, (E, BLOCK)).T


def outer_kernel(half, index, inverse, coefficient, attended, query_dec_t, factor, grad_out, gain, d_attended, flow, late):
    for n, i in enumerate(index):
        cols = columns(half, i)
        total = None
        for c in reversed(range(CHUNKS)):
            at = chunk(c)
            scaled = gain[:, cols] * grad_out[at, cols].astype(F32)
            grad = (inverse[at] * scaled - attended[at, span(n)] * coefficient[at]).astype(BF16)
            d_attended[at, span(n)] = grad
            new = dot(query_dec_t[span(n), at], grad, (1, 0))
            total = new if total is None else factor[c, i : i + 1, :] * total + new
            if c > 0:
                late[span(n), :] = total
        flow[span(n), :] = total


def copies(staged, outs, sems, n, cols):
    made = []
    for m, out in enumerate(outs):
        copy = pltpu.make_async_copy(staged.at[m, n], out.at[:, cols], sems.at[m, n])
        copy.start()
        made.append(copy)
    return made


def back_kernel(half, index, queries, keys, values, cum_row, cum_col, rise_col, d_attended, state, attended, inverse, gain, *refs):
    normed, grad_q, intra_k, intra_v, staged, sems = refs[-6:]
    causal = lax.broadcasted_iota(jnp.int32, (CHUNK, CHUNK), 0) <= lax.broadcasted_iota(
        jnp.int32, (CHUNK, CHUNK), 1
    )
    made = []
    for n, i in enumerate(index):
        cols = columns(half, i)
        q, k, v, grad = queries[:, cols], keys[:, cols], values[:, cols], d_attended[:, span(n)]
        staged[0, n] = (gain[:, cols] * attended[:, span(n)] * inverse[...]).astype(BF16)
        for c in range(CHUNKS):
            at = chunk(c)
            spread = cum_row[i : i + 1, at] - cum_col[at, i : i + 1]
            weight = jnp.exp(jnp.where(causal, spread, -1e30))
            probs = (dot(k[at], q[at], (1, 1)) * weight).astype(BF16)
            d_scores = (dot(v[at], grad[at], (1, 1)) * weight).astype(BF16)
            intra_v[at, span(n)] = dot(probs, grad[at], (1, 0))
            intra_k[at, span(n)] = dot(d_scores, q[at], (1, 0))
            staged[1, n, at, :] = (
                dot(d_scores, k[at], (0, 0))
                + rise_col[at, i : i + 1] * dot(grad[at], state[c, span(n), :], (1, 1))
            ).astype(BF16)
        made += copies(staged, (normed, grad_q), sems, n, cols)
    for copy in made:
        copy.wait()


def leave_kernel(half, index, value_dec, key_dec, intra_k, intra_v, leaving, late, factor, *refs):
    grad_k, grad_v, staged, sems = refs[-4:]
    made = []
    for n, i in enumerate(index):
        cols = columns(half, i)
        now = leaving[span(n), :]
        for c in reversed(range(CHUNKS)):
            at = chunk(c)
            if c < CHUNKS - 1:
                now = factor[c + 1, i : i + 1, :] * now + late[span(n), :]
            rounded = now.astype(BF16)
            staged[0, n, at, :] = (
                intra_k[at, span(n)] + dot(value_dec[at, span(n)], rounded, (1, 1))
            ).astype(BF16)
            staged[1, n, at, :] = (
                intra_v[at, span(n)] + dot(key_dec[at, span(n)], rounded, (1, 0))
            ).astype(BF16)
        made += copies(staged, (grad_k, grad_v), sems, n, cols)
    for copy in made:
        copy.wait()


def exchange(x, axis, bit):
    return lax.ppermute(x, axis, [(i, i ^ bit) for i in range(lax.axis_size(axis))])


def gathered(contrib, factor, reverse):
    devices, place = lax.axis_size("ctx"), lax.axis_index("ctx")
    all_contrib = lax.all_gather(contrib, "ctx")
    all_factor = lax.all_gather(factor, "ctx")

    def lap(step, state):
        at = devices - 1 - step if reverse else step
        reached = at > place if reverse else at < place
        new = (all_factor[at][:, None, :] * state.reshape(-1, E, E)).reshape(-1, E) + all_contrib[at]
        return jnp.where(reached, new, state)

    return lax.fori_loop(0, devices, lap, jnp.zeros_like(contrib))


def summed(x):
    devices = lax.axis_size("tp")
    if devices == 1 or devices & (devices - 1):
        return lax.psum(x, "tp"), jnp.zeros_like(x)
    bit = 1
    while True:
        other = exchange(x, "tp", bit)
        bit *= 2
        if bit == devices:
            return x, other
        x = x + other


def per_device(queries, keys, values, log_decay, gain, grad_out):
    heads, tokens = log_decay.shape
    assert tokens == BLOCK and CHUNKS == 2
    features = heads * E * lax.axis_size("tp")
    fast = lax.axis_size("ctx") == 8 and heads % 16 == 0
    half = heads // 2 if fast else None
    parts = PARTS if fast else 1
    own = (half or heads) // parts
    group = own // 2
    gain = gain[None, :]
    product = 2 * BLOCK * E * E
    rows = max(16, heads)

    pieces = [(p, side) for p in range(parts) for side in ((1, 0) if fast else (0,))]
    index = {(p, side): [side * (half or 0) + p * own + i for i in range(own)] for p, side in pieces}
    order = [(index[piece][0], own) for piece in pieces]
    tall, flat, wide = (own * E, E), (BLOCK, own * E), (BLOCK, E)

    cum_row, rise_row, fall_row, factor, keys, values, contrib, early = call(
        functools.partial(start_kernel, half, order, index[pieces[0]], heads),
        [((rows, BLOCK), F32)] * 3 + [((CHUNKS + 1, rows, E), F32)] + [(keys.shape, BF16)] * 2 + [(tall, F32)] * 2,
        log_decay, keys, values, anywhere=(0, 1, 2),
        scratch=[pltpu.VMEM((rows, BLOCK), F32), pltpu.SemaphoreType.DMA((2 + 2 * len(order),))],
        flops=4 * product,
    )
    whole_factor = factor[CHUNKS]
    contribs, earlies = {pieces[0]: contrib}, {pieces[0]: early}
    if fast:
        other_factor = exchange(whole_factor, "ctx", 1)[half:]
        own_factor = whole_factor[:half]
        chip_factor = own_factor * other_factor

    def at(p):
        return slice(p * own, (p + 1) * own)

    def first_step(reverse, kept, got, p):
        for_x, for_y = call(
            functools.partial(chip_kernel, group, reverse),
            [((group * E, E), F32)] * 2,
            kept, got, own_factor[at(p)], other_factor[at(p)],
        )
        return kept, got, for_x, for_y, exchange(for_x, "ctx", 2), exchange(for_y, "ctx", 4)

    def second_step(reverse, p, step, after):
        kept, got, for_x, for_y, got_x, got_y = step
        send_y, send_x = call(
            functools.partial(second_kernel, reverse), [((group * E, E), F32)] * 2,
            got_x, for_x, got_y, for_y, chip_factor[at(p)], factor_x[at(p)], factor_d[at(p)], after=after,
        )
        return *step, exchange(send_y, "ctx", 4), exchange(send_x, "ctx", 2)

    def last_step(reverse, p, step, after):
        kept, got, for_x, for_y, got_x, got_y, two_y, two_x = step
        enter, send = call(
            functools.partial(enter_kernel, reverse), [(tall, F32)] * 2,
            got_x, two_y, got_y, two_x, factor_x[at(p)], factor_d[at(p)], own_factor[at(p)], other_factor[at(p)], kept, got,
            after=after,
        )
        return {(p, 0): enter, (p, 1): exchange(send, "ctx", 1)}

    def contribute(piece, after):
        contribs[piece], earlies[piece] = call(
            functools.partial(contrib_kernel, half, index[piece]), [(tall, F32)] * 2,
            keys, values, fall_row, factor, flops=product * own, after=after,
        )

    steps, last = [], ()
    if fast:
        for p in range(parts):
            if p:
                contribute((p, 1), last)
            got = exchange(contribs[p, 1], "ctx", 1)
            contribute((p, 0), last)
            steps.append(first_step(False, contribs[p, 0], got, p))
            last = (steps[-1][2],)
        chip_factor, _ = lax.optimization_barrier((chip_factor, last[0]))
        factor_x = exchange(chip_factor, "ctx", 2)
        factor_d = exchange(chip_factor, "ctx", 6)

    cum_col, rise_col, fall_col = call(
        column_kernel, [(wide, F32)] * 3, cum_row, scratch=[pltpu.VMEM((E, BLOCK), F32)], after=last
    )
    intra, query_dec, query_dec_t, key_dec, value_dec = {}, {}, {}, {}, {}
    for piece in pieces:
        intra[piece], query_dec[piece], query_dec_t[piece], key_dec[piece], value_dec[piece] = call(
            functools.partial(intra_kernel, half, index[piece]),
            [(flat, F32), (flat, BF16), ((own * E, BLOCK), BF16), (flat, BF16), (flat, BF16)],
            queries, keys, values, cum_row, rise_row, cum_col, rise_col, fall_col, flops=own * 8 * product, after=last,
        )
    entering = {}
    if fast:
        for p in range(parts):
            steps[p] = second_step(False, p, steps[p], (intra[pieces[p]],))
        for p in range(parts):
            entering |= last_step(False, p, steps[p], (intra[pieces[parts + p]],))
    else:
        entering[pieces[0]] = gathered(contribs[pieces[0]], whole_factor[:heads], False)

    attended, state, sums = {}, {}, []
    for p in range(parts):
        for side in (0, 1) if fast else (0,):
            piece = p, side
            attended[piece], state[piece], *sums = call(
                functools.partial(attend_kernel, half, index[piece]),
                [(flat, F32), ((CHUNKS, *tall), BF16), (wide, F32), (wide, F32)],
                query_dec[piece], intra[piece], entering[piece], earlies[piece], factor, grad_out, gain, *sums,
                flops=own * product,
            )
    (sums,) = call(sum_kernel, [((8, BLOCK), F32)], *sums)
    inverse, coefficient = call(functools.partial(scale_kernel, features), [(wide, F32)] * 2, *summed(sums))

    d_attended, flow, late = {}, {}, {}

    def outer(piece, after):
        d_attended[piece], flow[piece], late[piece] = call(
            functools.partial(outer_kernel, half, index[piece]), [(flat, BF16), (tall, F32), (tall, F32)],
            inverse, coefficient, attended[piece], query_dec_t[piece], factor, grad_out, gain,
            flops=product * own, after=after,
        )

    steps, last = [], ()
    if fast:
        for p in range(parts):
            outer((p, 1), last)
            got = exchange(flow[p, 1], "ctx", 1)
            outer((p, 0), last)
            steps.append(first_step(True, flow[p, 0], got, p))
            last = (steps[-1][2],)
    else:
        outer(pieces[0], ())

    full = (queries.shape, BF16)
    staging = [pltpu.VMEM((2, own, BLOCK, E), BF16), pltpu.SemaphoreType.DMA((2, own))]
    results, intra_k, intra_v = [], {}, {}
    for piece in pieces:
        args = [
            queries, keys, values, cum_row, cum_col, rise_col,
            d_attended[piece], state[piece], attended[piece], inverse, gain, *results,
        ]
        where = (len(args) - 2, len(args) - 1) if results else ()
        *results, intra_k[piece], intra_v[piece] = call(
            functools.partial(back_kernel, half, index[piece]),
            [full, full, (flat, F32), (flat, F32)],
            *args, flops=own * 20 * product, anywhere=where, alias=dict(zip(where, (0, 1))), outs_anywhere=2,
            scratch=staging, after=last,
        )
    normed, grad_q = results

    leaving = {}
    if fast:
        for p in range(parts):
            steps[p] = second_step(True, p, steps[p], (intra_k[pieces[p]],))
        for p in range(parts):
            leaving |= last_step(True, p, steps[p], (intra_k[pieces[parts + p]],))
    else:
        leaving[pieces[0]] = gathered(flow[pieces[0]], whole_factor[:heads], True)

    results = []
    for p in range(parts):
        for side in (0, 1) if fast else (0,):
            piece = p, side
            args = [
                value_dec[piece], key_dec[piece], intra_k[piece], intra_v[piece],
                leaving[piece], late[piece], factor, *results,
            ]
            where = (len(args) - 2, len(args) - 1) if results else ()
            results = call(
                functools.partial(leave_kernel, half, index[piece]), [full, full],
                *args, flops=2 * own * product, anywhere=where, alias=dict(zip(where, (0, 1))), outs_anywhere=2,
                scratch=staging,
            )
    return normed, grad_q, *results


def solution(mesh):
    in_specs = (
        P("ctx", "tp"),
        P("ctx", "tp"),
        P("ctx", "tp"),
        P("tp", "ctx"),
        P("tp"),
        P("ctx", "tp"),
    )
    out_specs = (P("ctx", "tp"),) * 4
    return jax.shard_map(
        per_device, mesh=mesh, in_specs=in_specs, out_specs=out_specs, check_vma=False
    )
```

time: 224 us -> 75.8 us (0.34)
  matrix products: 69.7 us -> 0 us
  waiting for transfers between devices: 51.4 us -> 7.92 us
  other arithmetic: 34.4 us -> 0.01 us
  Pallas kernels: 0 us -> 34.2 us
  starting transfers between devices: 0.08 us -> 27.3 us
  local copies, waits for them, and re-layouts: 30.5 us -> 4.85 us
  blocking collectives: 22.1 us -> 0 us
  between operations: 14.2 us -> 1.28 us
    dot_general x12 -> x0, matrix products: 69.7 us -> none  [the longest x1 9.02 us: per_device(): jnp.einsum('nthe,nshe->nhts', query_blk, key_blk, preferred_element_type=...]
    all_gather x2 -> x0, waiting for transfers between devices: 51.3 us -> none  [prefix(): everything = jax.tree.map(lambda part: lax.all_gather(part, axis), shard)]
    pallas_call x0 -> x39, Pallas kernels: none -> 34.2 us  [call(): pl.pallas_call(body, out_shape=[jax.ShapeDtypeStruct(shape, dtype) if n <...]
    ppermute x0 -> x29, starting transfers between devices: none -> 27.3 us  [exchange(): lax.ppermute(x, axis, [(i, i ^ bit) for i in range(lax.axis_size(axis))])]
    select_n x16 -> x0, other arithmetic: 23.4 us -> none  [lap(): return jax.tree.map(lambda a, b: jnp.where(reached, a, b), new, before)]
    psum x1 -> x0, blocking collectives: 11.9 us -> none  [per_device(): square_total = lax.psum(squares, 'tp')]
    all_gather x1 -> x0, blocking collectives: 10.2 us -> none  [prefix(): everything = jax.tree.map(lambda part: lax.all_gather(part, axis), shard)]
    another operation x8 -> x0, local copies, waits for them, and re-layouts: 9.78 us -> none
  transfers between devices with their start and end apart: 2 -> 29, of which waited for: 2 -> 8; matrix products, arithmetic and copies ran while one was open for 21% -> 0% of each run, Pallas kernels for 0% -> 38%
where the time goes in v1:
time: 75.8 us; the launch traced here: 75.5 us
  Pallas kernels  34.2 us (45%)
  starting transfers between devices  27.3 us (36%)
  waiting for transfers between devices  7.92 us (10%)
  local copies, waits for them, and re-layouts  4.85 us (6%)
  between operations  1.28 us (2%)
    pallas_call x39, Pallas kernels, call(): pl.pallas_call(body, out_shape=[jax.ShapeDtypeStruct(shape, dtype) if n <...  34.2 us
    ppermute x29, starting transfers between devices, exchange(): lax.ppermute(x, axis, [(i, i ^ bit) for i in range(lax.axis_size(axis))])  27.3 us
    ppermute x29, waiting for transfers between devices, exchange(): lax.ppermute(x, axis, [(i, i ^ bit) for i in range(lax.axis_size(axis))])  7.92 us
    unnamed x12, local copies, waits for them, and re-layouts  4.82 us
  transfers between devices with their start and end apart: 29, of which 8 were waited for; matrix products, arithmetic and copies ran while one was open for 0% of the time, Pallas kernels for 38%

profile of v1, /device:TPU:0, one launch (start us, length us, event | category | flops | bytes accessed | tf_op | source)
XLA Modules:
  0.0 75.5 jit_solution(17292407599969515586)
XLA Ops:
  0.6 1.6 %copy-done.2 = bf16[512,2048]{1,0:T(8,128)(2,1)S(1)} copy-done((bf16[512,2048]{1,0:T(8,128)(2,1)S(1)}, bf16[512,2048]{1,0:T(8,128)(2,1)}, u32[]{:S(2)}) %copy-start.2) | copy-done | bytes 2097176
  2.2 1.6 %copy-done.3 = bf16[512,2048]{1,0:T(8,128)(2,1)S(1)} copy-done((bf16[512,2048]{1,0:T(8,128)(2,1)S(1)}, bf16[512,2048]{1,0:T(8,128)(2,1)}, u32[]{:S(2)}) %copy-start.3) | copy-done | bytes 2097176
  3.8 0.8 %copy-done.5 = f32[16,512]{1,0:T(8,128)S(1)} copy-done((f32[16,512]{1,0:T(8,128)S(1)}, f32[16,512]{1,0:T(8,128)}, u32[]{:S(2)}) %copy-start.5) | copy-done | bytes 32792
  4.6 1.5 %shard_map.93 = (f32[16,512]{1,0:T(8,128)S(1)}, f32[16,512]{1,0:T(8,128)S(1)}, f32[16,512]{1,0:T(8,128)S(1)}, f32[3,16,128]{2,1,0:T(8,128)S(1)}, bf16[512,2048]{...) custom-call(f32[16,512]{1,0:T(8,128)S(1)} %copy-done.5, ...), custom_call_target="tpu_custom_call" | custom-call | flops 67108864 | tf_op jit(solution)/shard_map/pallas_call | solution.py:35
  6.1 0.5 collective-permute-start.1
  7.4 0.7 collective-permute-done.refs_1_.refs_9_
  8.9 2.9 %collective-permute-start.10 = (f32[256,128]{1,0:T(8,128)S(1)}, f32[256,128]{1,0:T(8,128)S(1)}, u32[]{:S(2)}, u32[]{:S(2)}) collective-permute-start(f32[256,128]{1,0:T(8,128)S(1)} %get-tuple-element.127.refs_4_.refs_1_), channel_id=1, source_target_pairs={{0,8},{4,12},{8,0},{12,4},{16,24},{20,28},{24,16},{28,20},{1,9},{5... | collective-permute-start | bytes 393224 | tf_op jit(solution)/shard_map/ppermute | solution.py:356
  11.7 1.5 %collective-permute-start.11 = (f32[256,128]{1,0:T(8,128)S(1)}, f32[256,128]{1,0:T(8,128)S(1)}, u32[]{:S(2)}, u32[]{:S(2)}) collective-permute-start(f32[256,128]{1,0:T(8,128)S(1)} %get-tuple-element.150.refs_3_), channel_id=1, source_target_pairs={{0,16},{4,20},{8,24},{12,28},{16,0},{20,4},{24,8},{28,12},{1,17},{... | collective-permute-start | bytes 393224 | tf_op jit(solution)/shard_map/ppermute | solution.py:356
  14.0 1.9 %collective-permute-start.5 = (f32[8,128]{1,0:T(8,128)S(1)}, f32[8,128]{1,0:T(8,128)S(1)}, u32[]{:S(2)}, u32[]{:S(2)}) collective-permute-start(f32[8,128]{1,0:T(8,128)S(1)} %slice_multiply_fusion), channel_id=1, source_target_pairs={{0,8},{4,12},{8,0},{12,4},{16,24},{20,28},{24,16},{28,20},{1,9},{5... | collective-permute-start | bytes 12296 | tf_op jit(solution)/shard_map/ppermute | solution.py:356
  16.2 1.4 %shard_map.105 = (f32[512,512]{1,0:T(8,128)S(1)}, bf16[512,512]{1,0:T(8,128)(2,1)S(1)}, bf16[512,512]{1,0:T(8,128)(2,1)S(1)}, bf16[512,512]{1,0:T(8,128)(2,1)S(1)}, bf16[512,512]{1,0:T(8,128)(2,1)S(1)}) custom-call(bf16[512,2048]{1,0:T(8,128)(2,1)S(1)} %copy-done.1, bf16[512,2048]{1,0:T(8,128)(2,1)S(1)} %get-tuple-element.120.refs_0_.refs_1_, ...), custom_call_target="tpu_custom_call" | custom-call | flops 536870912 | tf_op jit(solution)/shard_map/pallas_call | solution.py:35
  17.6 0.8 collective-permute-done.6
  18.4 1.2 %collective-permute-start.4 = (f32[256,128]{1,0:T(8,128)S(1)}, f32[256,128]{1,0:T(8,128)S(1)}, u32[]{:S(2)}, u32[]{:S(2)}) collective-permute-start(f32[256,128]{1,0:T(8,128)S(1)} %get-tuple-element.137.refs_3_), channel_id=1, source_target_pairs={{0,16},{4,20},{8,24},{12,28},{16,0},{20,4},{24,8},{28,12},{1,17},{... | collective-permute-start | bytes 393224 | tf_op jit(solution)/shard_map/ppermute | solution.py:356
  19.7 0.9 %collective-permute-start.12 = (f32[256,128]{1,0:T(8,128)S(1)}, f32[256,128]{1,0:T(8,128)S(1)}, u32[]{:S(2)}, u32[]{:S(2)}) collective-permute-start(f32[256,128]{1,0:T(8,128)S(1)} %get-tuple-element.151), channel_id=1, source_target_pairs={{0,16},{4,20},{8,24},{12,28},{16,0},{20,4},{24,8},{28,12},{1,17},{... | collective-permute-start | bytes 393224 | tf_op jit(solution)/shard_map/ppermute | solution.py:356
  20.6 1.2 %collective-permute-start.13 = (f32[256,128]{1,0:T(8,128)S(1)}, f32[256,128]{1,0:T(8,128)S(1)}, u32[]{:S(2)}, u32[]{:S(2)}) collective-permute-start(f32[256,128]{1,0:T(8,128)S(1)} %get-tuple-element.152), channel_id=1, source_target_pairs={{0,8},{4,12},{8,0},{12,4},{16,24},{20,28},{24,16},{28,20},{1,9},{5... | collective-permute-start | bytes 393224 | tf_op jit(solution)/shard_map/ppermute | solution.py:356
  21.8 1.4 %shard_map.101 = (f32[512,512]{1,0:T(8,128)S(1)}, bf16[512,512]{1,0:T(8,128)(2,1)S(1)}, bf16[512,512]{1,0:T(8,128)(2,1)S(1)}, bf16[512,512]{1,0:T(8,128)(2,1)S(1)}, bf16[512,512]{1,0:T(8,128)(2,1)S(1)}) custom-call(bf16[512,2048]{1,0:T(8,128)(2,1)S(1)} %copy-done.1, bf16[512,2048]{1,0:T(8,128)(2,1)S(1)} %get-tuple-element.120.refs_0_.refs_1_, ...), custom_call_target="tpu_custom_call" | custom-call | flops 536870912 | tf_op jit(solution)/shard_map/pallas_call | solution.py:35
  23.2 1.0 %collective-permute-done.4.refs_2_ = f32[256,128]{1,0:T(8,128)S(1)} collective-permute-done((f32[256,128]{1,0:T(8,128)S(1)}, f32[256,128]{1,0:T(8,128)S(1)}, u32[]{:S(2)}, u32[]{:S(2)}) %collective-permute-start.4) | collective-permute-done | bytes 131104 | tf_op jit(solution)/shard_map/ppermute | solution.py:356
  24.2 1.0 %collective-permute-start.7 = (f32[256,128]{1,0:T(8,128)S(1)}, f32[256,128]{1,0:T(8,128)S(1)}, u32[]{:S(2)}, u32[]{:S(2)}) collective-permute-start(f32[256,128]{1,0:T(8,128)S(1)} %get-tuple-element.140), channel_id=1, source_target_pairs={{0,16},{4,20},{8,24},{12,28},{16,0},{20,4},{24,8},{28,12},{1,17},{... | collective-permute-start | bytes 393224 | tf_op jit(solution)/shard_map/ppermute | solution.py:356
  25.3 1.7 %collective-permute-start.8 = (f32[256,128]{1,0:T(8,128)S(1)}, f32[256,128]{1,0:T(8,128)S(1)}, u32[]{:S(2)}, u32[]{:S(2)}) collective-permute-start(f32[256,128]{1,0:T(8,128)S(1)} %get-tuple-element.141), channel_id=1, source_target_pairs={{0,8},{4,12},{8,0},{12,4},{16,24},{20,28},{24,16},{28,20},{1,9},{5... | collective-permute-start | bytes 393224 | tf_op jit(solution)/shard_map/ppermute | solution.py:356
  27.0 1.4 %shard_map.100 = (f32[512,512]{1,0:T(8,128)S(1)}, bf16[512,512]{1,0:T(8,128)(2,1)S(1)}, bf16[512,512]{1,0:T(8,128)(2,1)S(1)}, bf16[512,512]{1,0:T(8,128)(2,1)S(1)}, bf16[512,512]{1,0:T(8,128)(2,1)S(1)}) custom-call(bf16[512,2048]{1,0:T(8,128)(2,1)S(1)} %copy-done.1, bf16[512,2048]{1,0:T(8,128)(2,1)S(1)} %get-tuple-element.120.refs_0_.refs_1_, ...), custom_call_target="tpu_custom_call" | custom-call | flops 536870912 | tf_op jit(solution)/shard_map/pallas_call | solution.py:35
  28.6 1.4 %shard_map.103 = (f32[512,512]{1,0:T(8,128)S(1)}, bf16[512,512]{1,0:T(8,128)(2,1)S(1)}, bf16[512,512]{1,0:T(8,128)(2,1)S(1)}, bf16[512,512]{1,0:T(8,128)(2,1)S(1)}, bf16[512,512]{1,0:T(8,128)(2,1)S(1)}) custom-call(bf16[512,2048]{1,0:T(8,128)(2,1)S(1)} %copy-done.1, bf16[512,2048]{1,0:T(8,128)(2,1)S(1)} %get-tuple-element.120.refs_0_.refs_1_, ...), custom_call_target="tpu_custom_call" | custom-call | flops 536870912 | tf_op jit(solution)/shard_map/pallas_call | solution.py:35
  30.8 0.9 %copy-done = bf16[512,2048]{1,0:T(8,128)(2,1)S(1)} copy-done((bf16[512,2048]{1,0:T(8,128)(2,1)S(1)}, bf16[512,2048]{1,0:T(8,128)(2,1)}, u32[]{:S(2)}) %copy-start) | copy-done | bytes 2097176
  32.6 0.5 shard_map.110
  33.6 0.5 shard_map.112
  34.1 1.6 %collective-permute-start.15 = (f32[8,512]{1,0:T(8,128)S(1)}, f32[8,512]{1,0:T(8,128)S(1)}, u32[]{:S(2)}, u32[]{:S(2)}) collective-permute-start(f32[8,512]{1,0:T(8,128)S(1)} %shard_map.112), channel_id=1, source_target_pairs={{0,1},{1,0},{2,3},{3,2},{4,5},{5,4},{6,7},{7,6},{8,9},{9,8},{10,11... | collective-permute-start | bytes 49160 | tf_op jit(solution)/shard_map/ppermute | solution.py:356
  35.7 2.2 %collective-permute-done.15 = f32[8,512]{1,0:T(8,128)S(1)} collective-permute-done((f32[8,512]{1,0:T(8,128)S(1)}, f32[8,512]{1,0:T(8,128)S(1)}, u32[]{:S(2)}, u32[]{:S(2)}) %collective-permute-start.15) | collective-permute-done | bytes 16416 | tf_op jit(solution)/shard_map/ppermute | solution.py:356
  37.9 2.6 %collective-permute-start.16 = (f32[8,512]{1,0:T(8,128)S(1)}, f32[8,512]{1,0:T(8,128)S(1)}, u32[]{:S(2)}, u32[]{:S(2)}) collective-permute-start(f32[8,512]{1,0:T(8,128)S(1)} %add.3.refs_0_), channel_id=1, source_target_pairs={{0,2},{1,3},{2,0},{3,1},{4,6},{5,7},{6,4},{7,5},{8,10},{9,11},{10,... | collective-permute-start | bytes 49160 | tf_op jit(solution)/shard_map/ppermute | solution.py:356
  40.5 2.0 %collective-permute-done.16.refs_1_ = f32[8,512]{1,0:T(8,128)S(1)} collective-permute-done((f32[8,512]{1,0:T(8,128)S(1)}, f32[8,512]{1,0:T(8,128)S(1)}, u32[]{:S(2)}, u32[]{:S(2)}) %collective-permute-start.16) | collective-permute-done | bytes 16416 | tf_op jit(solution)/shard_map/ppermute | solution.py:356
  43.3 0.7 shard_map.114
  44.0 0.8 %collective-permute-done.17.refs_1_.refs_9_ = f32[512,128]{1,0:T(8,128)S(1)} collective-permute-done((f32[512,128]{1,0:T(8,128)S(1)}, f32[512,128]{1,0:T(8,128)S(1)}, u32[]{:S(2)}, u32[]{:S(2)}) %collective-permute-start.17) | collective-permute-done | bytes 262176 | tf_op jit(solution)/shard_map/ppermute | solution.py:356
  44.9 0.5 shard_map.118
  45.6 0.6 collective-permute-start.24
  46.2 0.8 %collective-permute-start.25 = (f32[256,128]{1,0:T(8,128)S(1)}, f32[256,128]{1,0:T(8,128)S(1)}, u32[]{:S(2)}, u32[]{:S(2)}) collective-permute-start(f32[256,128]{1,0:T(8,128)S(1)} %get-tuple-element.218.refs_3_), channel_id=1, source_target_pairs={{0,16},{4,20},{8,24},{12,28},{16,0},{20,4},{24,8},{28,12},{1,17},{... | collective-permute-start | bytes 393224 | tf_op jit(solution)/shard_map/ppermute | solution.py:356
  47.0 0.5 shard_map.117
  47.6 1.2 %collective-permute-start.19 = (f32[256,128]{1,0:T(8,128)S(1)}, f32[256,128]{1,0:T(8,128)S(1)}, u32[]{:S(2)}, u32[]{:S(2)}) collective-permute-start(f32[256,128]{1,0:T(8,128)S(1)} %get-tuple-element.189.refs_11_.refs_13_.refs_1_), channel_id=1, source_target_pairs={{0,8},{4,12},{8,0},{12,4},{16,24},{20,28},{24,16},{28,20},{1,9},{5... | collective-permute-start | bytes 393224 | tf_op jit(solution)/shard_map/ppermute | solution.py:356
  48.8 1.5 %collective-permute-start.20 = (f32[256,128]{1,0:T(8,128)S(1)}, f32[256,128]{1,0:T(8,128)S(1)}, u32[]{:S(2)}, u32[]{:S(2)}) collective-permute-start(f32[256,128]{1,0:T(8,128)S(1)} %get-tuple-element.202.refs_3_), channel_id=1, source_target_pairs={{0,16},{4,20},{8,24},{12,28},{16,0},{20,4},{24,8},{28,12},{1,17},{... | collective-permute-start | bytes 393224 | tf_op jit(solution)/shard_map/ppermute | solution.py:356
  50.3 3.6 %shard_map.120 = (bf16[512,2048]{1,0:T(8,128)(2,1)}, bf16[512,2048]{1,0:T(8,128)(2,1)}, f32[512,512]{1,0:T(8,128)S(1)}, f32[512,512]{1,0:T(8,128)S(1)}) custom-call(bf16[512,2048]{1,0:T(8,128)(2,1)S(1)} %copy-done.1, bf16[512,2048]{1,0:T(8,128)(2,1)S(1)} %get-tuple-element.120.refs_0_.refs_1_, bf16[512,2048]{1,0:T(8,128)(2,1)S(1)} %get-tuple-element.121.refs_1_.refs_2_, ...), custom_call_target="tpu_custom_call" | custom-call | flops 1342177280 | tf_op jit(solution)/shard_map/pallas_call | solution.py:35
  54.0 0.6 collective-permute-start.26
  54.6 0.9 %collective-permute-start.27 = (f32[256,128]{1,0:T(8,128)S(1)}, f32[256,128]{1,0:T(8,128)S(1)}, u32[]{:S(2)}, u32[]{:S(2)}) collective-permute-start(f32[256,128]{1,0:T(8,128)S(1)} %get-tuple-element.220), channel_id=1, source_target_pairs={{0,8},{4,12},{8,0},{12,4},{16,24},{20,28},{24,16},{28,20},{1,9},{5... | collective-permute-start | bytes 393224 | tf_op jit(solution)/shard_map/ppermute | solution.py:356
  55.5 3.6 %shard_map.121 = (bf16[512,2048]{1,0:T(8,128)(2,1)}, bf16[512,2048]{1,0:T(8,128)(2,1)}, f32[512,512]{1,0:T(8,128)S(1)}, f32[512,512]{1,0:T(8,128)S(1)}) custom-call(bf16[512,2048]{1,0:T(8,128)(2,1)S(1)} %copy-done.1, bf16[512,2048]{1,0:T(8,128)(2,1)S(1)} %get-tuple-element.120.refs_0_.refs_1_, ...), custom_call_target="tpu_custom_call", output_to_operand_aliasing={{0}: (11, {}), {1}: (12, {})} | custom-call | flops 1342177280 | tf_op jit(solution)/shard_map/pallas_call | solution.py:35
  59.2 1.3 %collective-permute-start.21 = (f32[256,128]{1,0:T(8,128)S(1)}, f32[256,128]{1,0:T(8,128)S(1)}, u32[]{:S(2)}, u32[]{:S(2)}) collective-permute-start(f32[256,128]{1,0:T(8,128)S(1)} %get-tuple-element.204), channel_id=1, source_target_pairs={{0,16},{4,20},{8,24},{12,28},{16,0},{20,4},{24,8},{28,12},{1,17},{... | collective-permute-start | bytes 393224 | tf_op jit(solution)/shard_map/ppermute | solution.py:356
  60.4 1.5 %collective-permute-start.22 = (f32[256,128]{1,0:T(8,128)S(1)}, f32[256,128]{1,0:T(8,128)S(1)}, u32[]{:S(2)}, u32[]{:S(2)}) collective-permute-start(f32[256,128]{1,0:T(8,128)S(1)} %get-tuple-element.205), channel_id=1, source_target_pairs={{0,8},{4,12},{8,0},{12,4},{16,24},{20,28},{24,16},{28,20},{1,9},{5... | collective-permute-start | bytes 393224 | tf_op jit(solution)/shard_map/ppermute | solution.py:356
  61.9 3.6 %shard_map.122 = (bf16[512,2048]{1,0:T(8,128)(2,1)}, bf16[512,2048]{1,0:T(8,128)(2,1)}, f32[512,512]{1,0:T(8,128)S(1)}, f32[512,512]{1,0:T(8,128)S(1)}) custom-call(bf16[512,2048]{1,0:T(8,128)(2,1)S(1)} %copy-done.1, bf16[512,2048]{1,0:T(8,128)(2,1)S(1)} %get-tuple-element.120.refs_0_.refs_1_, ...), custom_call_target="tpu_custom_call", output_to_operand_aliasing={{0}: (11, {}), {1}: (12, {})} | custom-call | flops 1342177280 | tf_op jit(solution)/shard_map/pallas_call | solution.py:35
  65.7 3.8 %shard_map.123 = (bf16[512,2048]{1,0:T(8,128)(2,1)}, bf16[512,2048]{1,0:T(8,128)(2,1)}, f32[512,512]{1,0:T(8,128)S(1)}, f32[512,512]{1,0:T(8,128)S(1)}) custom-call(bf16[512,2048]{1,0:T(8,128)(2,1)S(1)} %copy-done.1, bf16[512,2048]{1,0:T(8,128)(2,1)S(1)} %get-tuple-element.120.refs_0_.refs_1_, ...), custom_call_target="tpu_custom_call", output_to_operand_aliasing={{0}: (11, {}), {1}: (12, {})} | custom-call | flops 1342177280 | tf_op jit(solution)/shard_map/pallas_call | solution.py:35
  69.7 0.6 collective-permute-start.23
  70.3 1.3 %shard_map.128 = (bf16[512,2048]{1,0:T(8,128)(2,1)}, bf16[512,2048]{1,0:T(8,128)(2,1)}) custom-call(bf16[512,512]{1,0:T(8,128)(2,1)S(1)} %get-tuple-element.223.refs_0_, bf16[512,512]{1,0:T(8,128)(2,1)S(1)} %get-tuple-element.224.refs_1_, f32[512,512]{1,0:T(8,128)S(1)} %get-tuple-element.203.refs_7_.refs_2_, f32[512,512]{1,0:T(8,128)S(1)} %get-tuple-element.225.refs_3_, ...), custom_call_target="tpu_custom_call" | custom-call | flops 134217728 | tf_op jit(solution)/shard_map/pallas_call | solution.py:35
  71.5 1.3 %shard_map.129 = (bf16[512,2048]{1,0:T(8,128)(2,1)}, bf16[512,2048]{1,0:T(8,128)(2,1)}) custom-call(bf16[512,512]{1,0:T(8,128)(2,1)S(1)} %get-tuple-element.214.refs_0_, bf16[512,512]{1,0:T(8,128)(2,1)S(1)} %get-tuple-element.215.refs_1_, f32[512,512]{1,0:T(8,128)S(1)} %get-tuple-element.216.refs_7_.refs_2_, ...), custom_call_target="tpu_custom_call", output_to_operand_aliasing={{0}: (7, {}), {1}: (8, {})} | custom-call | flops 134217728 | tf_op jit(solution)/shard_map/pallas_call | solution.py:35
  72.8 1.3 %shard_map.130 = (bf16[512,2048]{1,0:T(8,128)(2,1)}, bf16[512,2048]{1,0:T(8,128)(2,1)}) custom-call(bf16[512,512]{1,0:T(8,128)(2,1)S(1)} %get-tuple-element.209.refs_0_, bf16[512,512]{1,0:T(8,128)(2,1)S(1)} %get-tuple-element.210.refs_1_, f32[512,512]{1,0:T(8,128)S(1)} %get-tuple-element.206.refs_10_.refs_2_, ...), custom_call_target="tpu_custom_call", output_to_operand_aliasing={{0}: (7, {}), {1}: (8, {})} | custom-call | flops 134217728 | tf_op jit(solution)/shard_map/pallas_call | solution.py:35
  74.1 1.3 %shard_map.131 = (bf16[512,2048]{1,0:T(8,128)(2,1)}, bf16[512,2048]{1,0:T(8,128)(2,1)}) custom-call(bf16[512,512]{1,0:T(8,128)(2,1)S(1)} %get-tuple-element.198.refs_0_, bf16[512,512]{1,0:T(8,128)(2,1)S(1)} %get-tuple-element.199.refs_1_, f32[512,512]{1,0:T(8,128)S(1)} %get-tuple-element.200.refs_10_.refs_2_, ...), custom_call_target="tpu_custom_call", output_to_operand_aliasing={{0}: (7, {}), {1}: (8, {})} | custom-call | flops 134217728 | tf_op jit(solution)/shard_map/pallas_call | solution.py:35
  (69 shorter events, 6.5 us)
Async XLA Ops:
  0.6 1.6 %copy-start.2 = (bf16[512,2048]{1,0:T(8,128)(2,1)S(1)}, bf16[512,2048]{1,0:T(8,128)(2,1)}, u32[]{:S(2)}) copy-start(bf16[512,2048]{1,0:T(8,128)(2,1)} %refs_1_.1) | copy-start | bytes 6291460
  2.2 1.6 %copy-start.3 = (bf16[512,2048]{1,0:T(8,128)(2,1)S(1)}, bf16[512,2048]{1,0:T(8,128)(2,1)}, u32[]{:S(2)}) copy-start(bf16[512,2048]{1,0:T(8,128)(2,1)} %refs_2_.1) | copy-start | bytes 6291460
  3.8 0.8 %copy-start.5 = (f32[16,512]{1,0:T(8,128)S(1)}, f32[16,512]{1,0:T(8,128)}, u32[]{:S(2)}) copy-start(f32[16,512]{1,0:T(8,128)} %refs_0_.9) | copy-start | bytes 98308
  6.1 1.3 %collective-permute-start.1 = (f32[16,128]{1,0:T(8,128)S(1)}, f32[16,128]{1,0:T(8,128)S(1)}, u32[]{:S(2)}, u32[]{:S(2)}) collective-permute-start(f32[16,128]{1,0:T(8,128)S(1)} %slice_bitcast_fusion), channel_id=1, source_target_pairs={{0,4},{4,0},{8,12},{12,8},{16,20},{20,16},{24,28},{28,24},{1,5},{5... | collective-permute-start | bytes 24584 | tf_op jit(solution)/shard_map/ppermute | solution.py:356
  6.6 1.5 %collective-permute-start = (f32[512,128]{1,0:T(8,128)S(1)}, f32[512,128]{1,0:T(8,128)S(1)}, u32[]{:S(2)}, u32[]{:S(2)}) collective-permute-start(f32[512,128]{1,0:T(8,128)S(1)} %get-tuple-element.126), channel_id=1, source_target_pairs={{0,4},{4,0},{8,12},{12,8},{16,20},{20,16},{24,28},{28,24},{1,5},{5... | collective-permute-start | bytes 786440 | tf_op jit(solution)/shard_map/ppermute | solution.py:356
  8.7 5.1 %collective-permute-start.2 = (f32[512,128]{1,0:T(8,128)S(1)}, f32[512,128]{1,0:T(8,128)S(1)}, u32[]{:S(2)}, u32[]{:S(2)}) collective-permute-start(f32[512,128]{1,0:T(8,128)S(1)} %get-tuple-element.129), channel_id=1, source_target_pairs={{0,4},{4,0},{8,12},{12,8},{16,20},{20,16},{24,28},{28,24},{1,5},{5... | collective-permute-start | bytes 786440 | tf_op jit(solution)/shard_map/ppermute | solution.py:356
  8.9 10.7 %collective-permute-start.10 = (f32[256,128]{1,0:T(8,128)S(1)}, f32[256,128]{1,0:T(8,128)S(1)}, u32[]{:S(2)}, u32[]{:S(2)}) collective-permute-start(f32[256,128]{1,0:T(8,128)S(1)} %get-tuple-element.127.refs_4_.refs_1_), channel_id=1, source_target_pairs={{0,8},{4,12},{8,0},{12,4},{16,24},{20,28},{24,16},{28,20},{1,9},{5... | collective-permute-start | bytes 393224 | tf_op jit(solution)/shard_map/ppermute | solution.py:356
  11.7 4.5 %copy-start.1 = (bf16[512,2048]{1,0:T(8,128)(2,1)S(1)}, bf16[512,2048]{1,0:T(8,128)(2,1)}, u32[]{:S(2)}) copy-start(bf16[512,2048]{1,0:T(8,128)(2,1)} %refs_0_.17) | copy-start | bytes 6291460
  11.7 7.9 %collective-permute-start.11 = (f32[256,128]{1,0:T(8,128)S(1)}, f32[256,128]{1,0:T(8,128)S(1)}, u32[]{:S(2)}, u32[]{:S(2)}) collective-permute-start(f32[256,128]{1,0:T(8,128)S(1)} %get-tuple-element.150.refs_3_), channel_id=1, source_target_pairs={{0,16},{4,20},{8,24},{12,28},{16,0},{20,4},{24,8},{28,12},{1,17},{... | collective-permute-start | bytes 393224 | tf_op jit(solution)/shard_map/ppermute | solution.py:356
  13.8 4.6 %collective-permute-start.6 = (f32[8,128]{1,0:T(8,128)S(1)}, f32[8,128]{1,0:T(8,128)S(1)}, u32[]{:S(2)}, u32[]{:S(2)}) collective-permute-start(f32[8,128]{1,0:T(8,128)S(1)} %slice_multiply_fusion), channel_id=1, source_target_pairs={{0,24},{4,28},{8,16},{12,20},{16,8},{20,12},{24,0},{28,4},{1,25},{... | collective-permute-start | bytes 12296 | tf_op jit(solution)/shard_map/ppermute | solution.py:356
  14.0 5.6 %collective-permute-start.5 = (f32[8,128]{1,0:T(8,128)S(1)}, f32[8,128]{1,0:T(8,128)S(1)}, u32[]{:S(2)}, u32[]{:S(2)}) collective-permute-start(f32[8,128]{1,0:T(8,128)S(1)} %slice_multiply_fusion), channel_id=1, source_target_pairs={{0,8},{4,12},{8,0},{12,4},{16,24},{20,28},{24,16},{28,20},{1,9},{5... | collective-permute-start | bytes 12296 | tf_op jit(solution)/shard_map/ppermute | solution.py:356
  15.9 7.3 %collective-permute-start.3 = (f32[256,128]{1,0:T(8,128)S(1)}, f32[256,128]{1,0:T(8,128)S(1)}, u32[]{:S(2)}, u32[]{:S(2)}) collective-permute-start(f32[256,128]{1,0:T(8,128)S(1)} %get-tuple-element.130.refs_1_.refs_8_), channel_id=1, source_target_pairs={{0,8},{4,12},{8,0},{12,4},{16,24},{20,28},{24,16},{28,20},{1,9},{5... | collective-permute-start | bytes 393224 | tf_op jit(solution)/shard_map/ppermute | solution.py:356
  18.4 5.8 %collective-permute-start.4 = (f32[256,128]{1,0:T(8,128)S(1)}, f32[256,128]{1,0:T(8,128)S(1)}, u32[]{:S(2)}, u32[]{:S(2)}) collective-permute-start(f32[256,128]{1,0:T(8,128)S(1)} %get-tuple-element.137.refs_3_), channel_id=1, source_target_pairs={{0,16},{4,20},{8,24},{12,28},{16,0},{20,4},{24,8},{28,12},{1,17},{... | collective-permute-start | bytes 393224 | tf_op jit(solution)/shard_map/ppermute | solution.py:356
  19.7 8.7 %collective-permute-start.12 = (f32[256,128]{1,0:T(8,128)S(1)}, f32[256,128]{1,0:T(8,128)S(1)}, u32[]{:S(2)}, u32[]{:S(2)}) collective-permute-start(f32[256,128]{1,0:T(8,128)S(1)} %get-tuple-element.151), channel_id=1, source_target_pairs={{0,16},{4,20},{8,24},{12,28},{16,0},{20,4},{24,8},{28,12},{1,17},{... | collective-permute-start | bytes 393224 | tf_op jit(solution)/shard_map/ppermute | solution.py:356
  20.6 7.8 %collective-permute-start.13 = (f32[256,128]{1,0:T(8,128)S(1)}, f32[256,128]{1,0:T(8,128)S(1)}, u32[]{:S(2)}, u32[]{:S(2)}) collective-permute-start(f32[256,128]{1,0:T(8,128)S(1)} %get-tuple-element.152), channel_id=1, source_target_pairs={{0,8},{4,12},{8,0},{12,4},{16,24},{20,28},{24,16},{28,20},{1,9},{5... | collective-permute-start | bytes 393224 | tf_op jit(solution)/shard_map/ppermute | solution.py:356
  24.2 5.8 %collective-permute-start.7 = (f32[256,128]{1,0:T(8,128)S(1)}, f32[256,128]{1,0:T(8,128)S(1)}, u32[]{:S(2)}, u32[]{:S(2)}) collective-permute-start(f32[256,128]{1,0:T(8,128)S(1)} %get-tuple-element.140), channel_id=1, source_target_pairs={{0,16},{4,20},{8,24},{12,28},{16,0},{20,4},{24,8},{28,12},{1,17},{... | collective-permute-start | bytes 393224 | tf_op jit(solution)/shard_map/ppermute | solution.py:356
  25.3 5.0 %collective-permute-start.8 = (f32[256,128]{1,0:T(8,128)S(1)}, f32[256,128]{1,0:T(8,128)S(1)}, u32[]{:S(2)}, u32[]{:S(2)}) collective-permute-start(f32[256,128]{1,0:T(8,128)S(1)} %get-tuple-element.141), channel_id=1, source_target_pairs={{0,8},{4,12},{8,0},{12,4},{16,24},{20,28},{24,16},{28,20},{1,9},{5... | collective-permute-start | bytes 393224 | tf_op jit(solution)/shard_map/ppermute | solution.py:356
  28.5 3.6 %collective-permute-start.14 = (f32[512,128]{1,0:T(8,128)S(1)}, f32[512,128]{1,0:T(8,128)S(1)}, u32[]{:S(2)}, u32[]{:S(2)}) collective-permute-start(f32[512,128]{1,0:T(8,128)S(1)} %get-tuple-element.153), channel_id=1, source_target_pairs={{0,4},{4,0},{8,12},{12,8},{16,20},{20,16},{24,28},{28,24},{1,5},{5... | collective-permute-start | bytes 786440 | tf_op jit(solution)/shard_map/ppermute | solution.py:356
  30.0 1.6 %copy-start = (bf16[512,2048]{1,0:T(8,128)(2,1)S(1)}, bf16[512,2048]{1,0:T(8,128)(2,1)}, u32[]{:S(2)}) copy-start(bf16[512,2048]{1,0:T(8,128)(2,1)} %refs_5_.15) | copy-start | bytes 6291460
  30.1 1.6 %copy-start.4 = (f32[2048]{0:T(1024)S(1)}, f32[2048]{0:T(1024)}, u32[]{:S(2)}) copy-start(f32[2048]{0:T(1024)} %param.10) | copy-start | bytes 24580
  30.3 2.8 %collective-permute-start.9 = (f32[512,128]{1,0:T(8,128)S(1)}, f32[512,128]{1,0:T(8,128)S(1)}, u32[]{:S(2)}, u32[]{:S(2)}) collective-permute-start(f32[512,128]{1,0:T(8,128)S(1)} %get-tuple-element.143), channel_id=1, source_target_pairs={{0,4},{4,0},{8,12},{12,8},{16,20},{20,16},{24,28},{28,24},{1,5},{5... | collective-permute-start | bytes 786440 | tf_op jit(solution)/shard_map/ppermute | solution.py:356
  34.1 3.8 %collective-permute-start.15 = (f32[8,512]{1,0:T(8,128)S(1)}, f32[8,512]{1,0:T(8,128)S(1)}, u32[]{:S(2)}, u32[]{:S(2)}) collective-permute-start(f32[8,512]{1,0:T(8,128)S(1)} %shard_map.112), channel_id=1, source_target_pairs={{0,1},{1,0},{2,3},{3,2},{4,5},{5,4},{6,7},{7,6},{8,9},{9,8},{10,11... | collective-permute-start | bytes 49160 | tf_op jit(solution)/shard_map/ppermute | solution.py:356
  37.9 4.6 %collective-permute-start.16 = (f32[8,512]{1,0:T(8,128)S(1)}, f32[8,512]{1,0:T(8,128)S(1)}, u32[]{:S(2)}, u32[]{:S(2)}) collective-permute-start(f32[8,512]{1,0:T(8,128)S(1)} %add.3.refs_0_), channel_id=1, source_target_pairs={{0,2},{1,3},{2,0},{3,1},{4,6},{5,7},{6,4},{7,5},{8,10},{9,11},{10,... | collective-permute-start | bytes 49160 | tf_op jit(solution)/shard_map/ppermute | solution.py:356
  43.2 1.6 %collective-permute-start.17 = (f32[512,128]{1,0:T(8,128)S(1)}, f32[512,128]{1,0:T(8,128)S(1)}, u32[]{:S(2)}, u32[]{:S(2)}) collective-permute-start(f32[512,128]{1,0:T(8,128)S(1)} %get-tuple-element.175), channel_id=1, source_target_pairs={{0,4},{4,0},{8,12},{12,8},{16,20},{20,16},{24,28},{28,24},{1,5},{5... | collective-permute-start | bytes 786440 | tf_op jit(solution)/shard_map/ppermute | solution.py:356
  45.4 2.1 %collective-permute-start.18 = (f32[512,128]{1,0:T(8,128)S(1)}, f32[512,128]{1,0:T(8,128)S(1)}, u32[]{:S(2)}, u32[]{:S(2)}) collective-permute-start(f32[512,128]{1,0:T(8,128)S(1)} %get-tuple-element.188), channel_id=1, source_target_pairs={{0,4},{4,0},{8,12},{12,8},{16,20},{20,16},{24,28},{28,24},{1,5},{5... | collective-permute-start | bytes 786440 | tf_op jit(solution)/shard_map/ppermute | solution.py:356
  45.6 8.3 %collective-permute-start.24 = (f32[256,128]{1,0:T(8,128)S(1)}, f32[256,128]{1,0:T(8,128)S(1)}, u32[]{:S(2)}, u32[]{:S(2)}) collective-permute-start(f32[256,128]{1,0:T(8,128)S(1)} %get-tuple-element.176.refs_7_.refs_1_), channel_id=1, source_target_pairs={{0,8},{4,12},{8,0},{12,4},{16,24},{20,28},{24,16},{28,20},{1,9},{5... | collective-permute-start | bytes 393224 | tf_op jit(solution)/shard_map/ppermute | solution.py:356
  46.2 7.8 %collective-permute-start.25 = (f32[256,128]{1,0:T(8,128)S(1)}, f32[256,128]{1,0:T(8,128)S(1)}, u32[]{:S(2)}, u32[]{:S(2)}) collective-permute-start(f32[256,128]{1,0:T(8,128)S(1)} %get-tuple-element.218.refs_3_), channel_id=1, source_target_pairs={{0,16},{4,20},{8,24},{12,28},{16,0},{20,4},{24,8},{28,12},{1,17},{... | collective-permute-start | bytes 393224 | tf_op jit(solution)/shard_map/ppermute | solution.py:356
  47.6 11.5 %collective-permute-start.19 = (f32[256,128]{1,0:T(8,128)S(1)}, f32[256,128]{1,0:T(8,128)S(1)}, u32[]{:S(2)}, u32[]{:S(2)}) collective-permute-start(f32[256,128]{1,0:T(8,128)S(1)} %get-tuple-element.189.refs_11_.refs_13_.refs_1_), channel_id=1, source_target_pairs={{0,8},{4,12},{8,0},{12,4},{16,24},{20,28},{24,16},{28,20},{1,9},{5... | collective-permute-start | bytes 393224 | tf_op jit(solution)/shard_map/ppermute | solution.py:356
  48.8 10.3 %collective-permute-start.20 = (f32[256,128]{1,0:T(8,128)S(1)}, f32[256,128]{1,0:T(8,128)S(1)}, u32[]{:S(2)}, u32[]{:S(2)}) collective-permute-start(f32[256,128]{1,0:T(8,128)S(1)} %get-tuple-element.202.refs_3_), channel_id=1, source_target_pairs={{0,16},{4,20},{8,24},{12,28},{16,0},{20,4},{24,8},{28,12},{1,17},{... | collective-permute-start | bytes 393224 | tf_op jit(solution)/shard_map/ppermute | solution.py:356
  54.0 11.5 %collective-permute-start.26 = (f32[256,128]{1,0:T(8,128)S(1)}, f32[256,128]{1,0:T(8,128)S(1)}, u32[]{:S(2)}, u32[]{:S(2)}) collective-permute-start(f32[256,128]{1,0:T(8,128)S(1)} %get-tuple-element.219), channel_id=1, source_target_pairs={{0,16},{4,20},{8,24},{12,28},{16,0},{20,4},{24,8},{28,12},{1,17},{... | collective-permute-start | bytes 393224 | tf_op jit(solution)/shard_map/ppermute | solution.py:356
  54.6 10.9 %collective-permute-start.27 = (f32[256,128]{1,0:T(8,128)S(1)}, f32[256,128]{1,0:T(8,128)S(1)}, u32[]{:S(2)}, u32[]{:S(2)}) collective-permute-start(f32[256,128]{1,0:T(8,128)S(1)} %get-tuple-element.220), channel_id=1, source_target_pairs={{0,8},{4,12},{8,0},{12,4},{16,24},{20,28},{24,16},{28,20},{1,9},{5... | collective-permute-start | bytes 393224 | tf_op jit(solution)/shard_map/ppermute | solution.py:356
  59.2 10.4 %collective-permute-start.21 = (f32[256,128]{1,0:T(8,128)S(1)}, f32[256,128]{1,0:T(8,128)S(1)}, u32[]{:S(2)}, u32[]{:S(2)}) collective-permute-start(f32[256,128]{1,0:T(8,128)S(1)} %get-tuple-element.204), channel_id=1, source_target_pairs={{0,16},{4,20},{8,24},{12,28},{16,0},{20,4},{24,8},{28,12},{1,17},{... | collective-permute-start | bytes 393224 | tf_op jit(solution)/shard_map/ppermute | solution.py:356
  60.4 9.1 %collective-permute-start.22 = (f32[256,128]{1,0:T(8,128)S(1)}, f32[256,128]{1,0:T(8,128)S(1)}, u32[]{:S(2)}, u32[]{:S(2)}) collective-permute-start(f32[256,128]{1,0:T(8,128)S(1)} %get-tuple-element.205), channel_id=1, source_target_pairs={{0,8},{4,12},{8,0},{12,4},{16,24},{20,28},{24,16},{28,20},{1,9},{5... | collective-permute-start | bytes 393224 | tf_op jit(solution)/shard_map/ppermute | solution.py:356
  65.7 5.9 %collective-permute-start.28 = (f32[512,128]{1,0:T(8,128)S(1)}, f32[512,128]{1,0:T(8,128)S(1)}, u32[]{:S(2)}, u32[]{:S(2)}) collective-permute-start(f32[512,128]{1,0:T(8,128)S(1)} %get-tuple-element.221), channel_id=1, source_target_pairs={{0,4},{4,0},{8,12},{12,8},{16,20},{20,16},{24,28},{28,24},{1,5},{5... | collective-permute-start | bytes 786440 | tf_op jit(solution)/shard_map/ppermute | solution.py:356
  69.7 4.4 %collective-permute-start.23 = (f32[512,128]{1,0:T(8,128)S(1)}, f32[512,128]{1,0:T(8,128)S(1)}, u32[]{:S(2)}, u32[]{:S(2)}) collective-permute-start(f32[512,128]{1,0:T(8,128)S(1)} %get-tuple-element.207), channel_id=1, source_target_pairs={{0,4},{4,0},{8,12},{12,8},{16,20},{20,16},{24,28},{28,24},{1,5},{5... | collective-permute-start | bytes 786440 | tf_op jit(solution)/shard_map/ppermute | solution.py:356

commit v2 on v0

v2 whole, which is shorter than its diff:
```python
import functools

import jax
import jax.numpy as jnp
from jax import lax
from jax.experimental import pallas as pl
from jax.experimental.pallas import tpu as pltpu
from jax.sharding import PartitionSpec as P

E = 128
BLOCK = 512
CHUNK = 256
CHUNKS = BLOCK // CHUNK
EPSILON = 1e-05
GROUPS = 2

F32 = jnp.float32
BF16 = jnp.bfloat16
IN_VMEM = pl.BlockSpec(memory_space=pltpu.VMEM)
IN_HBM = pl.BlockSpec(memory_space=pltpu.HBM)
ANY = pl.BlockSpec(memory_space=pl.ANY)
MIB = 1 << 20


def call(kernel, outs, *args, anywhere=(), after=(), outs_anywhere=0, scratch=(), alias=None, limit=20):
    args = [pltpu.with_memory_space_constraint(x, pltpu.HBM) if n in anywhere else x for n, x in enumerate(args)]
    args += after
    skip = len(after)

    def body(*refs):
        kept = len(args) - skip
        kernel(*refs[:kept], *refs[len(args) :])

    in_specs = [IN_VMEM] * (len(args) - skip) + [ANY] * skip
    for operand in anywhere:
        in_specs[operand] = IN_HBM
    return pl.pallas_call(
        body,
        out_shape=[
            (pltpu.HBM if n < outs_anywhere else pltpu.VMEM)(shape, dtype) for n, (shape, dtype) in enumerate(outs)
        ],
        in_specs=in_specs,
        out_specs=[IN_HBM] * outs_anywhere + [IN_VMEM] * (len(outs) - outs_anywhere),
        scratch_shapes=scratch,
        input_output_aliases=alias or {},
        compiler_params=pltpu.CompilerParams(vmem_limit_bytes=limit * MIB),
        cost_estimate=pl.CostEstimate(flops=0, bytes_accessed=0, transcendentals=0),
    )(*args)


def dot(a, b, contract):
    return lax.dot_general(a, b, ((contract[:1], contract[1:]), ((), ())), preferred_element_type=F32)


def beside_copies(compute):
    pl.when(lax.axis_index("ctx") >= 0)(compute)


def span(i, n=1):
    return slice(i * E, (i + n) * E)


def chunk(c):
    return slice(c * CHUNK, (c + 1) * CHUNK)


def bits(reverse=False):
    me = lax.axis_index("ctx")
    if reverse:
        me = 7 - me
    return me & 1, (me >> 1) & 1, me >> 2


def columns(half, i, n=1):
    if half is None:
        return span(i, n)
    core = lax.axis_index("ctx") & 1
    base = core if i < half else 1 - core
    return pl.ds(pl.multiple_of(base * (half * E) + (i % half) * E, E), n * E)


def head_rows(half, i, n):
    core = lax.axis_index("ctx") & 1
    base = core if i < half else 1 - core
    return pl.ds(pl.multiple_of(base * half, half), n)


def contribution(index, keys, values, fall_row, factor, contrib, early):
    decayed = []
    for n, i in enumerate(index):
        turned = keys[:, span(n)].T.astype(F32)
        decayed.append((turned * fall_row[i : i + 1, :]).astype(BF16))
    news = [
        [dot(dec[:, chunk(c)], values[chunk(c), span(n)], (1, 0)) for c in range(CHUNKS)]
        for n, dec in enumerate(decayed)
    ]
    for n, i in enumerate(index):
        early[span(n), :] = news[n][0]
        contrib[span(n), :] = factor[1, i : i + 1, :] * news[n][0] + news[n][1]


def fetch(half, pieces, sources, outs, sems):
    made = []
    for m, index in enumerate(pieces):
        cols = columns(half, index[0], len(index))
        made.append([])
        for n, source in enumerate(sources):
            k = m * len(sources) + n
            made[-1].append(pltpu.make_async_copy(source.at[:, cols], outs[k], sems.at[k]))
            made[-1][-1].start()
    return made


def start_kernel(half, pieces, heads, log_decay, gain, keys, values, *refs):
    cum_row, rise_row, fall_row, factor, gain_out = refs[:5]
    rows, sems, more = refs[-3:]
    brought, (contrib, early) = refs[5:-5], refs[-5:-3]
    rows[...] = jnp.zeros_like(rows)
    moves = [pltpu.make_async_copy(gain, gain_out, more.at[2])]
    if half is None:
        moves.append(pltpu.make_async_copy(log_decay, rows.at[0:heads, :], more.at[0]))
    else:
        for n, i in enumerate((0, half)):
            source = log_decay.at[head_rows(half, i, half), :]
            moves.append(pltpu.make_async_copy(source, rows.at[i : i + half, :], more.at[n]))
    for move in moves:
        move.start()
    made = fetch(half, pieces, (keys, values), brought, sems)
    for move in moves:
        move.wait()
    @beside_copies
    def _():
        up_to = (
            lax.broadcasted_iota(jnp.int32, (CHUNK, CHUNK), 0)
            <= lax.broadcasted_iota(jnp.int32, (CHUNK, CHUNK), 1)
        ).astype(F32).astype(BF16)
        for c in range(CHUNKS):
            whole = rows[:, chunk(c)]
            high = whole.astype(BF16)
            rest = whole - high.astype(F32)
            middle = rest.astype(BF16)
            low = (rest - middle.astype(F32)).astype(BF16)
            cum = (dot(low, up_to, (1, 0)) + dot(middle, up_to, (1, 0))) + dot(high, up_to, (1, 0))
            total = cum[:, CHUNK - 1 : CHUNK]
            cum_row[:, chunk(c)] = cum
            rise_row[:, chunk(c)] = jnp.exp(cum)
            fall_row[:, chunk(c)] = jnp.exp(total - cum)
            factor[c] = jnp.broadcast_to(jnp.exp(total), (total.shape[0], E))
        whole = factor[0] * factor[1]
        factor[CHUNKS] = whole
        if half is not None:
            contrib[len(pieces[0]) * E :, :] = factor[CHUNKS, half : 2 * half]

    for move in made[0]:
        move.wait()
    beside_copies(functools.partial(contribution, pieces[0], *brought[:2], fall_row, factor, contrib, early))
    for moves in made[1:]:
        for move in moves:
            move.wait()


def contrib_kernel(index, keys, values, fall_row, factor, contrib, early):
    contribution(index, keys, values, fall_row, factor, contrib, early)


def column_kernel(cum_row, cum_col, rise_col, fall_col, rows):
    rows[...] = jnp.zeros_like(rows)
    rows[0 : cum_row.shape[0], :] = cum_row[...]
    col = rows[...].T
    cum_col[...] = col
    rise_col[...] = jnp.exp(col)
    for c in range(CHUNKS):
        fall_col[chunk(c), :] = jnp.exp(col[(c + 1) * CHUNK - 1 : (c + 1) * CHUNK, :] - col[chunk(c)])


def chip_kernel(count, reverse, kept, got, own_factor, other_factor, sums):
    if sums.shape[0] > count * E:
        sums[count * E :, :] = own_factor[...] * other_factor[...]
    lower = bits(reverse)[0] == 0
    for n in range(count):
        mine = jnp.where(lower, other_factor[n : n + 1, :], 1.0)
        theirs = jnp.where(lower, 1.0, own_factor[n : n + 1, :])
        sums[span(n), :] = mine * kept[span(n), :] + theirs * got[span(n), :]


def second_kernel(count, group, reverse, one, own, factor, factor_x, factor_d, send):
    _, x, y = bits(reverse)
    right, later = x == 1, y == 1
    for n in range(count):
        f, fx, fd = factor[n : n + 1, :], factor_x[n : n + 1, :], factor_d[n : n + 1, :]
        if group == 0:
            p = jnp.where(right, f, 1.0)
            q = jnp.where(right, 1.0, fx)
        else:
            p = jnp.where(later, jnp.where(right, 1.0, f * fd), 0.0)
            q = jnp.where(later, jnp.where(right, 0.0, jnp.ones_like(f)), 1.0)
        send[span(n), :] = p * one[span(n), :] + q * own[span(n), :]


def enter_kernel(count, group, reverse, one, two, factor_x, factor_d, own_factor, other_factor, kept, got, mine, send):
    core, x, y = bits(reverse)
    lower, right, later = core == 0, x == 1, y == 1
    for n in range(count):
        fx, fd = factor_x[n : n + 1, :], factor_d[n : n + 1, :]
        ones = jnp.ones_like(fx)
        if group == 0:
            w = jnp.where(right, ones, 0.0)
            u = jnp.where(later, jnp.where(right, fx, 1.0), 0.0)
        else:
            w = jnp.where(later, jnp.where(right, fx, fd), 0.0)
            u = jnp.where(later, ones, jnp.where(right, ones, 0.0))
        low = w * one[span(n), :] + u * two[span(n), :]
        f = jnp.where(lower, own_factor[n : n + 1, :], other_factor[n : n + 1, :])
        high = f * low + jnp.where(lower, kept[span(n), :], got[span(n), :])
        mine[span(n), :] = jnp.where(lower, low, high)
        send[span(n), :] = jnp.where(lower, high, low)


def intra_kernel(half, index, grad_out, queries, keys, values, cum_row, rise_row, cum_col, rise_col, fall_col, *refs):
    intra, query_dec, query_dec_t, key_dec, value_dec, grad_here, sems = refs
    made = fetch(half, [index], (grad_out,), (grad_here,), sems)
    @beside_copies
    def _():
        causal = lax.broadcasted_iota(jnp.int32, (CHUNK, CHUNK), 0) >= lax.broadcasted_iota(
            jnp.int32, (CHUNK, CHUNK), 1
        )
        scores, probs = [], []
        for n, i in enumerate(index):
            cols = columns(half, i)
            for c in range(CHUNKS):
                scores.append((n, i, c, dot(queries[chunk(c), cols], keys[chunk(c), span(n)], (1, 1))))
        for n, i, c, score in scores:
            at = chunk(c)
            spread = cum_col[at, i : i + 1] - cum_row[i : i + 1, at]
            weight = jnp.exp(jnp.where(causal, spread, -1e30))
            probs.append((n, i, c, (score * weight).astype(BF16)))
        for n, i, c, prob in probs:
            intra[chunk(c), span(n)] = dot(prob, values[chunk(c), span(n)], (1, 0))
        for n, i in enumerate(index):
            cols = columns(half, i)
            rise, fall = rise_col[:, i : i + 1], fall_col[:, i : i + 1]
            query_dec[:, span(n)] = (queries[:, cols].astype(F32) * rise).astype(BF16)
            query_dec_t[span(n), :] = (queries[:, cols].T.astype(F32) * rise_row[i : i + 1, :]).astype(BF16)
            key_dec[:, span(n)] = (keys[:, span(n)].astype(F32) * fall).astype(BF16)
            value_dec[:, span(n)] = (values[:, span(n)].astype(F32) * fall).astype(BF16)

    made[0][0].wait()


def attend_kernel(half, index, query_dec, intra, entering, early, factor, grad_out, gain, *refs):
    attended, state, squares, crossed = refs[-4:]
    states, inters = [], []
    for n, i in enumerate(index):
        now = entering[span(n), :]
        states.append((n, 0, now.astype(BF16)))
        states.append((n, 1, (factor[0, i : i + 1, :] * now + early[span(n), :]).astype(BF16)))
    for n, c, rounded in states:
        state[c, span(n), :] = rounded
        inters.append((n, c, dot(query_dec[chunk(c), span(n)], rounded, (1, 0))))
    totals, crosses = [0.0] * CHUNKS, [0.0] * CHUNKS
    for n, c, inter in inters:
        at, cols = chunk(c), columns(half, index[n])
        out = intra[at, span(n)] + inter
        attended[at, span(n)] = out
        totals[c] += out * out
        crosses[c] += (gain[:, cols] * grad_out[at, span(n)].astype(F32)) * out
    for c in range(CHUNKS):
        at = chunk(c)
        if len(refs) == 6:
            totals[c], crosses[c] = totals[c] + refs[0][at], crosses[c] + refs[1][at]
        squares[at, :] = totals[c]
        crossed[at, :] = crosses[c]


def sum_kernel(squares, crossed, sums):
    square = jnp.sum(squares[...].T, axis=0, keepdims=True)
    cross = jnp.sum(crossed[...].T, axis=0, keepdims=True)
    first = lax.broadcasted_iota(jnp.int32, (8, BLOCK), 0) == 0
    sums[...] = jnp.where(first, square, cross)


def scale_kernel(features, ours, theirs, inverse, coefficient):
    sums = ours[...] + theirs[...]
    inv = lax.rsqrt(sums[0:1, :] / features + EPSILON)
    coef = inv * inv * inv * sums[1:2, :] / features
    inverse[...] = jnp.broadcast_to(inv, (E, BLOCK)).T
    coefficient[...] = jnp.broadcast_to(coef, (E, BLOCK)).T


def outer_kernel(half, index, inverse, coefficient, attended, query_dec_t, factor, grad_out, gain, d_attended, flow, late):
    grads, news = [], []
    for n, i in enumerate(index):
        cols = columns(half, i)
        for c in range(CHUNKS):
            at = chunk(c)
            scaled = gain[:, cols] * grad_out[at, span(n)].astype(F32)
            grads.append((n, c, (inverse[at] * scaled - attended[at, span(n)] * coefficient[at]).astype(BF16)))
    for n, c, grad in grads:
        d_attended[chunk(c), span(n)] = grad
        news.append(dot(query_dec_t[span(n), chunk(c)], grad, (1, 0)))
    for n, i in enumerate(index):
        first, second = news[CHUNKS * n : CHUNKS * (n + 1)]
        late[span(n), :] = second
        flow[span(n), :] = factor[0, i : i + 1, :] * second + first


def flush(staged, outs, sems, half, index):
    made = []
    for m, out in enumerate(outs):
        cols = columns(half, index[0], len(index))
        made.append(pltpu.make_async_copy(staged.at[m], out.at[:, cols], sems.at[m]))
        made[-1].start()
    return made


def back_kernel(half, index, before, queries, keys, values, cum_row, cum_col, rise_col, d_attended, state, attended, inverse, gain, *refs):
    made = []
    if before is not None:
        made = flush(refs[0], refs[-6:-4], refs[-1], half, before)
    intra_k, intra_v, staged = refs[-4:-1]
    @beside_copies
    def _():
        causal = lax.broadcasted_iota(jnp.int32, (CHUNK, CHUNK), 0) <= lax.broadcasted_iota(
            jnp.int32, (CHUNK, CHUNK), 1
        )
        products, rounded = [], []
        for n, i in enumerate(index):
            cols = columns(half, i)
            for c in range(CHUNKS):
                at = chunk(c)
                grad = d_attended[at, span(n)]
                score = dot(keys[at, span(n)], queries[at, cols], (1, 1))
                d_prob = dot(values[at, span(n)], grad, (1, 1))
                products.append((n, i, c, score, d_prob, dot(grad, state[c, span(n), :], (1, 1))))
        for n, i, c, score, d_prob, inter in products:
            at = chunk(c)
            spread = cum_row[i : i + 1, at] - cum_col[at, i : i + 1]
            weight = jnp.exp(jnp.where(causal, spread, -1e30))
            rounded.append((n, i, c, (score * weight).astype(BF16), (d_prob * weight).astype(BF16), inter))
        for n, i, c, prob, d_score, inter in rounded:
            at, cols = chunk(c), columns(half, i)
            intra_v[at, span(n)] = dot(prob, d_attended[at, span(n)], (1, 0))
            intra_k[at, span(n)] = dot(d_score, queries[at, cols], (1, 0))
            staged[1, at, span(n)] = (dot(d_score, keys[at, span(n)], (0, 0)) + rise_col[at, i : i + 1] * inter).astype(BF16)
        for n, i in enumerate(index):
            staged[0, :, span(n)] = (gain[:, columns(half, i)] * attended[:, span(n)] * inverse[...]).astype(BF16)

    for copy in made:
        copy.wait()


def leave_kernel(half, index, before, last, split, value_dec, key_dec, intra_k, intra_v, leaving, late, factor, *refs):
    staged, sems, out_sems = refs[-3:]
    made = []
    if before is not None:
        made = flush(refs[0], refs[-7:-5] if split else refs[-5:-3], sems, half, before)
    @beside_copies
    def _():
        flows, products = [], []
        for n, i in enumerate(index):
            now = leaving[span(n), :]
            flows.append((n, 1, now.astype(BF16)))
            flows.append((n, 0, (factor[1, i : i + 1, :] * now + late[span(n), :]).astype(BF16)))
        for n, c, flow in flows:
            at = chunk(c)
            products.append((n, c, dot(value_dec[at, span(n)], flow, (1, 1)), dot(key_dec[at, span(n)], flow, (1, 0))))
        for n, c, of_key, of_value in products:
            at = chunk(c)
            staged[0, at, span(n)] = (intra_k[at, span(n)] + of_key).astype(BF16)
            staged[1, at, span(n)] = (intra_v[at, span(n)] + of_value).astype(BF16)

    if last:
        made += flush(staged, refs[-5:-3], out_sems, half, index)
    for copy in made:
        copy.wait()


def exchange(x, axis, bit):
    return lax.ppermute(x, axis, [(i, i ^ bit) for i in range(lax.axis_size(axis))])


def gathered(contrib, factor, reverse):
    devices, place = lax.axis_size("ctx"), lax.axis_index("ctx")
    all_contrib = lax.all_gather(contrib, "ctx")
    all_factor = lax.all_gather(factor, "ctx")

    def lap(step, state):
        at = devices - 1 - step if reverse else step
        reached = at > place if reverse else at < place
        new = (all_factor[at][:, None, :] * state.reshape(-1, E, E)).reshape(-1, E) + all_contrib[at]
        return jnp.where(reached, new, state)

    return lax.fori_loop(0, devices, lap, jnp.zeros_like(contrib))


def summed(x):
    devices = lax.axis_size("tp")
    if devices == 1 or devices & (devices - 1):
        return lax.psum(x, "tp"), jnp.zeros_like(x)
    bit = 1
    while True:
        other = exchange(x, "tp", bit)
        bit *= 2
        if bit == devices:
            return x, other
        x = x + other


def per_device(queries, keys, values, log_decay, gain, grad_out):
    heads, tokens = log_decay.shape
    assert tokens == BLOCK and CHUNKS == 2
    features = heads * E * lax.axis_size("tp")
    fast = lax.axis_size("ctx") == 8 and heads % 16 == 0
    half = heads // 2 if fast else None
    groups = GROUPS if fast else 1
    own = (half or heads) // groups
    gain = gain[None, :]
    rows = max(16, heads)

    sides = (1, 0) if fast else (0,)
    pieces = [(g, side) for g in range(groups) for side in sides]
    late_pieces = [(g, side) for g in range(groups) for side in reversed(sides)]
    index = {(g, side): [side * (half or 0) + g * own + i for i in range(own)] for g, side in pieces}
    tall, flat, wide = (own * E, E), (BLOCK, own * E), (BLOCK, E)
    staged_shape = ((2, BLOCK, own * E), BF16)
    bits_of = {0: (2, 4), 1: (4, 2)}

    def at(g):
        return slice(g * own, (g + 1) * own)

    n = len(pieces)
    cum_row, rise_row, fall_row, factor, gain, *made = call(
        functools.partial(start_kernel, half, [index[piece] for piece in pieces], heads),
        [((rows, BLOCK), F32)] * 3 + [((CHUNKS + 1, rows, E), F32), (gain.shape, F32)]
        + [(flat, BF16)] * (2 * n) + [((own * E + (half or 0), E), F32), (tall, F32)],
        log_decay, gain, keys, values, anywhere=(0, 1, 2, 3),
        scratch=[pltpu.VMEM((rows, BLOCK), F32), pltpu.SemaphoreType.DMA((2 * n,)), pltpu.SemaphoreType.DMA((3,))],
    )
    whole_factor = factor[CHUNKS]
    key, value = {}, {}
    for m, piece in enumerate(pieces):
        key[piece], value[piece] = made[2 * m : 2 * m + 2]
    contrib, early = {pieces[0]: made[-2]}, {pieces[0]: made[-1]}

    def contribute(piece):
        contrib[piece], early[piece] = call(
            functools.partial(contrib_kernel, index[piece]), [(tall, F32)] * 2,
            key[piece], value[piece], fall_row, factor,
        )

    def first_step(reverse, kept, got, g, after=()):
        more = half if g == 0 and not reverse else 0
        f, h = (own_factor, other_factor) if more else (own_factor[at(g)], other_factor[at(g)])
        (chip,) = call(
            functools.partial(chip_kernel, own, reverse), [((own * E + more, E), F32)], kept, got, f, h, after=after
        )
        return kept, got, chip, exchange(chip, "ctx", bits_of[g][0])

    def second_step(reverse, g, step, after):
        kept, got, chip, one = step
        (send,) = call(
            functools.partial(second_kernel, own, g, reverse), [(tall, F32)],
            one, chip, chip_factor[at(g)], factor_x[at(g)], (factor_d if g else factor_x)[at(g)], after=after,
        )
        return *step, exchange(send, "ctx", bits_of[g][1])

    def last_step(reverse, g, step, after):
        kept, got, chip, one, two = step
        enter, send = call(
            functools.partial(enter_kernel, own, g, reverse), [(tall, F32)] * 2,
            one, two, factor_x[at(g)], (factor_d if g else factor_x)[at(g)], own_factor[at(g)], other_factor[at(g)], kept, got,
            after=after,
        )
        return {(g, 0): enter, (g, 1): exchange(send, "ctx", 1)}

    steps, last = [], ()
    if fast:
        gots = [exchange(contrib[0, 1], "ctx", 1)]
        contribute((0, 0))
        for g in range(1, groups):
            contribute((g, 1))
            gots.append(exchange(contrib[g, 1], "ctx", 1))
        own_factor, other_factor = whole_factor[:half], gots[0][own * E : own * E + half]
        for g in range(groups):
            if g:
                contribute((g, 0))
            steps.append(first_step(False, contrib[g, 0], gots[g], g, [contrib[groups - 1, 1]]))
        chip_factor = steps[0][2][own * E :]
        factor_x = steps[0][3][own * E :]
        factor_d = exchange(chip_factor, "ctx", 6)
        last = [step[2] for step in steps]

    cum_col, rise_col, fall_col = call(
        column_kernel, [(wide, F32)] * 3, cum_row, scratch=[pltpu.VMEM((E, BLOCK), F32)], after=last
    )
    intra, query_dec, query_dec_t, key_dec, value_dec, grad_here = {}, {}, {}, {}, {}, {}
    for piece in pieces:
        made = call(
            functools.partial(intra_kernel, half, index[piece]),
            [(flat, F32), (flat, BF16), ((own * E, BLOCK), BF16)] + [(flat, BF16)] * 3,
            grad_out, queries, key[piece], value[piece], cum_row, rise_row, cum_col, rise_col, fall_col, after=last, anywhere=(0,), scratch=[pltpu.SemaphoreType.DMA((1,))],
        )
        intra[piece], query_dec[piece], query_dec_t[piece], key_dec[piece], value_dec[piece], grad_here[piece] = made
    attended, state, sums = {}, {}, []

    def attend(piece, sums):
        attended[piece], state[piece], *sums = call(
            functools.partial(attend_kernel, half, index[piece]),
            [(flat, F32), ((CHUNKS, *tall), BF16), (wide, F32), (wide, F32)],
            query_dec[piece], intra[piece], entering[piece], early[piece], factor, grad_here[piece], gain, *sums,
        )
        return sums

    entering = {}
    if fast:
        for g in range(groups):
            steps[g] = second_step(False, g, steps[g], [intra[pieces[g]], intra[pieces[1]]])
        for g in range(groups):
            entering |= last_step(False, g, steps[g], [intra[pieces[-1]], intra[pieces[-2]], *sums])
            if g == 0:
                sums = attend((0, 0), sums)
    else:
        entering[pieces[0]] = gathered(contrib[pieces[0]], whole_factor[:heads], False)
    for piece in late_pieces:
        if piece not in attended:
            sums = attend(piece, sums)
    (sums,) = call(sum_kernel, [((8, BLOCK), F32)], *sums)
    inverse, coefficient = call(functools.partial(scale_kernel, features), [(wide, F32)] * 2, *summed(sums))

    d_attended, flow, late = {}, {}, {}

    def outer(piece, after):
        d_attended[piece], flow[piece], late[piece] = call(
            functools.partial(outer_kernel, half, index[piece]), [(flat, BF16), (tall, F32), (tall, F32)],
            inverse, coefficient, attended[piece], query_dec_t[piece], factor, grad_here[piece], gain, after=after,
        )

    steps, last = [], ()
    outer(pieces[0], ())
    if fast:
        gots = [exchange(flow[0, 1], "ctx", 1)]
        outer((0, 0), ())
        for g in range(1, groups):
            outer((g, 1), ())
            gots.append(exchange(flow[g, 1], "ctx", 1))
        for g in range(groups):
            if g:
                outer((g, 0), ())
            steps.append(first_step(True, flow[g, 0], gots[g], g, [flow[groups - 1, 1]]))
        last = [step[2] for step in steps]

    full = (queries.shape, BF16)
    sems = pltpu.SemaphoreType.DMA((2,))
    results, before, staged, intra_k, intra_v = [], None, [], {}, {}
    for piece in pieces:
        args = [
            queries, key[piece], value[piece], cum_row, cum_col, rise_col,
            d_attended[piece], state[piece], attended[piece], inverse, gain, *staged, *results,
        ]
        where = (len(args) - 2, len(args) - 1) if results else ()
        *results, intra_k[piece], intra_v[piece], out = call(
            functools.partial(back_kernel, half, index[piece], before),
            [full] * 2 + [(flat, F32)] * 2 + [staged_shape],
            *args, anywhere=where, alias=dict(zip(where, (0, 1))), outs_anywhere=2,
            scratch=[sems], after=last,
        )
        before, staged = index[piece], [out]

    leaving, others = {}, []

    def leave(piece, before, staged, results, others):
        last = piece in late_pieces[-2:]
        first = piece == late_pieces[0]
        split = first and last
        held = results if first else others
        args = [
            value_dec[piece], key_dec[piece], intra_k[piece], intra_v[piece],
            leaving[piece], late[piece], factor, *staged, *held,
        ]
        where = (len(args) - 2, len(args) - 1) if held else ()
        outs = 4 if split else 2
        made = call(
            functools.partial(leave_kernel, half, index[piece], before, last, split),
            [full] * outs + [staged_shape] * (not last),
            *args, anywhere=where, alias=dict(zip(where, (0, 1))), outs_anywhere=outs,
            scratch=[pltpu.VMEM(*staged_shape)] * last + [sems, sems],
        )
        out = None if last else made[-1]
        made = made[:outs]
        if first:
            results, others = made[:2], made[2:]
        else:
            others = made
        return (None, [], results, others) if last else (index[piece], [out], results, others)

    carried = (before, staged, results, others)
    if fast:
        for g in range(groups):
            steps[g] = second_step(True, g, steps[g], [intra_k[pieces[1]]])
        for g in range(groups):
            leaving |= last_step(True, g, steps[g], [intra_k[pieces[-1]], *carried[1]])
            if g == 0:
                carried = leave((0, 0), *carried)
    else:
        leaving[pieces[0]] = gathered(flow[pieces[0]], whole_factor[:heads], True)
    for n, piece in enumerate(late_pieces):
        if n or not fast:
            carried = leave(piece, *carried)
    return *carried[2], *carried[3]


def solution(mesh):
    in_specs = (
        P("ctx", "tp"),
        P("ctx", "tp"),
        P("ctx", "tp"),
        P("tp", "ctx"),
        P("tp"),
        P("ctx", "tp"),
    )
    out_specs = (P("ctx", "tp"),) * 4
    return jax.shard_map(
        per_device, mesh=mesh, in_specs=in_specs, out_specs=out_specs, check_vma=False
    )
```

time: 224 us -> 59.3 us (0.26)
  matrix products: 69.7 us -> 0 us
  waiting for transfers between devices: 51.4 us -> 10.9 us
  other arithmetic: 34.4 us -> 0.01 us
  local copies, waits for them, and re-layouts: 30.5 us -> 0.03 us
  Pallas kernels: 0 us -> 27.8 us
  blocking collectives: 22.1 us -> 0 us
  starting transfers between devices: 0.08 us -> 19.2 us
  between operations: 14.2 us -> 1.14 us
    dot_general x12 -> x0, matrix products: 69.7 us -> none  [the longest x1 9.02 us: per_device(): jnp.einsum('nthe,nshe->nhts', query_blk, key_blk, preferred_element_type=...]
    all_gather x2 -> x0, waiting for transfers between devices: 51.3 us -> none  [prefix(): everything = jax.tree.map(lambda part: lax.all_gather(part, axis), shard)]
    pallas_call x0 -> x39, Pallas kernels: none -> 27.8 us  [call(): pl.pallas_call(body, out_shape=[(pltpu.HBM if n < outs_anywhere else pltp...]
    select_n x16 -> x0, other arithmetic: 23.4 us -> none  [lap(): return jax.tree.map(lambda a, b: jnp.where(reached, a, b), new, before)]
    ppermute x0 -> x19, starting transfers between devices: none -> 19.2 us  [exchange(): lax.ppermute(x, axis, [(i, i ^ bit) for i in range(lax.axis_size(axis))])]
    unnamed x19 -> x2, local copies, waits for them, and re-layouts: 13.9 us -> 0.01 us
    psum x1 -> x0, blocking collectives: 11.9 us -> none  [per_device(): square_total = lax.psum(squares, 'tp')]
    ppermute x0 -> x19, waiting for transfers between devices: none -> 10.9 us  [exchange(): lax.ppermute(x, axis, [(i, i ^ bit) for i in range(lax.axis_size(axis))])]
  transfers between devices with their start and end apart: 2 -> 19, of which waited for: 2 -> 11; matrix products, arithmetic and copies ran while one was open for 21% -> 0% of each run, Pallas kernels for 0% -> 38%
where the time goes in v2:
time: 59.3 us; the launch traced here: 59.1 us
  Pallas kernels  27.8 us (47%)
  starting transfers between devices  19.2 us (32%)
  waiting for transfers between devices  10.9 us (18%)
  between operations  1.14 us (2%)
    pallas_call x39, Pallas kernels, call(): pl.pallas_call(body, out_shape=[(pltpu.HBM if n < outs_anywhere else pltp...  27.8 us
    ppermute x19, starting transfers between devices, exchange(): lax.ppermute(x, axis, [(i, i ^ bit) for i in range(lax.axis_size(axis))])  19.2 us
    ppermute x19, waiting for transfers between devices, exchange(): lax.ppermute(x, axis, [(i, i ^ bit) for i in range(lax.axis_size(axis))])  10.9 us
  transfers between devices with their start and end apart: 19, of which 11 were waited for; matrix products, arithmetic and copies ran while one was open for 0% of the time, Pallas kernels for 38%

profile of v2, /device:TPU:0, one launch (start us, length us, event | category | flops | bytes accessed | tf_op | source)
XLA Modules:
  0.0 59.1 jit_solution(10904046449822026886)
XLA Ops:
  0.6 2.7 %shard_map.93 = (f32[16,512]{1,0:T(8,128)S(1)}, f32[16,512]{1,0:T(8,128)S(1)}, f32[16,512]{1,0:T(8,128)S(1)}, f32[3,16,128]{2,1,0:T(8,128)S(1)}, f32[1,2048]{1,0...) custom-call(f32[16,512]{1,0:T(8,128)} %refs_0_.9, ...), custom_call_target="tpu_custom_call" | custom-call | tf_op jit(solution)/shard_map/pallas_call | solution.py:37
  3.4 0.5 collective-permute-start
  3.8 0.3 shard_map.95
  4.4 0.3 shard_map.94
  4.7 0.4 shard_map.97
  5.2 3.0 %collective-permute-start.3 = (f32[520,128]{1,0:T(8,128)S(1)}, f32[520,128]{1,0:T(8,128)S(1)}, u32[]{:S(2)}, u32[]{:S(2)}) collective-permute-start(f32[520,128]{1,0:T(8,128)S(1)} %shard_map.96.refs_1_.refs_9_), channel_id=1, source_target_pairs={{0,8},{4,12},{8,0},{12,4},{16,24},{20,28},{24,16},{28,20},{1,9},{5... | collective-permute-start | bytes 798728 | tf_op jit(solution)/shard_map/ppermute | solution.py:379
  8.2 1.6 %collective-permute-start.2 = (f32[512,128]{1,0:T(8,128)S(1)}, f32[512,128]{1,0:T(8,128)S(1)}, u32[]{:S(2)}, u32[]{:S(2)}) collective-permute-start(f32[512,128]{1,0:T(8,128)S(1)} %shard_map.98.refs_2_.refs_10_.refs_1_), channel_id=1, source_target_pairs={{0,16},{4,20},{8,24},{12,28},{16,0},{20,4},{24,8},{28,12},{1,17},{... | collective-permute-start | bytes 786440 | tf_op jit(solution)/shard_map/ppermute | solution.py:379
  10.0 0.3 collective-permute-start.4
  10.3 1.4 %shard_map.100 = (f32[512,512]{1,0:T(8,128)S(1)}, bf16[512,512]{1,0:T(8,128)(2,1)S(1)}, bf16[512,512]{1,0:T(8,128)(2,1)S(1)}, bf16[512,512]{1,0:T(8,128)(2,1)S(1...) custom-call(bf16[512,2048]{1,0:T(8,128)(2,1)} %refs_0_.13, bf16[512,2048]{1,0:T(8,128)(2,1)S(1)} %copy-done, ...), custom_call_target="tpu_custom_call" | custom-call | tf_op jit(solution)/shard_map/pallas_call | solution.py:37
  11.6 1.4 %shard_map.104 = (f32[512,512]{1,0:T(8,128)S(1)}, bf16[512,512]{1,0:T(8,128)(2,1)S(1)}, bf16[512,512]{1,0:T(8,128)(2,1)S(1)}, bf16[512,512]{1,0:T(8,128)(2,1)S(1...) custom-call(bf16[512,2048]{1,0:T(8,128)(2,1)} %refs_0_.13, bf16[512,2048]{1,0:T(8,128)(2,1)S(1)} %copy-done, ...), custom_call_target="tpu_custom_call" | custom-call | tf_op jit(solution)/shard_map/pallas_call | solution.py:37
  13.0 1.8 %collective-permute-done.3.refs_0_ = f32[520,128]{1,0:T(8,128)S(1)} collective-permute-done((f32[520,128]{1,0:T(8,128)S(1)}, f32[520,128]{1,0:T(8,128)S(1)}, u32[]{:S(2)}, u32[]{:S(2)}) %collective-permute-start.3) | collective-permute-done | bytes 266272 | tf_op jit(solution)/shard_map/ppermute | solution.py:379
  14.8 1.8 %collective-permute-start.6 = (f32[512,128]{1,0:T(8,128)S(1)}, f32[512,128]{1,0:T(8,128)S(1)}, u32[]{:S(2)}, u32[]{:S(2)}) collective-permute-start(f32[512,128]{1,0:T(8,128)S(1)} %shard_map.105), channel_id=1, source_target_pairs={{0,16},{4,20},{8,24},{12,28},{16,0},{20,4},{24,8},{28,12},{1,17},{... | collective-permute-start | bytes 786440 | tf_op jit(solution)/shard_map/ppermute | solution.py:379
  16.8 1.6 %collective-permute-start.5 = (f32[512,128]{1,0:T(8,128)S(1)}, f32[512,128]{1,0:T(8,128)S(1)}, u32[]{:S(2)}, u32[]{:S(2)}) collective-permute-start(f32[512,128]{1,0:T(8,128)S(1)} %shard_map.102), channel_id=1, source_target_pairs={{0,8},{4,12},{8,0},{12,4},{16,24},{20,28},{24,16},{28,20},{1,9},{5... | collective-permute-start | bytes 786440 | tf_op jit(solution)/shard_map/ppermute | solution.py:379
  18.3 1.3 %shard_map.101 = (f32[512,512]{1,0:T(8,128)S(1)}, bf16[512,512]{1,0:T(8,128)(2,1)S(1)}, bf16[512,512]{1,0:T(8,128)(2,1)S(1)}, bf16[512,512]{1,0:T(8,128)(2,1)S(1...) custom-call(bf16[512,2048]{1,0:T(8,128)(2,1)} %refs_0_.13, bf16[512,2048]{1,0:T(8,128)(2,1)S(1)} %copy-done, ...), custom_call_target="tpu_custom_call" | custom-call | tf_op jit(solution)/shard_map/pallas_call | solution.py:37
  19.6 1.3 %shard_map.103 = (f32[512,512]{1,0:T(8,128)S(1)}, bf16[512,512]{1,0:T(8,128)(2,1)S(1)}, bf16[512,512]{1,0:T(8,128)(2,1)S(1)}, bf16[512,512]{1,0:T(8,128)(2,1)S(1...) custom-call(bf16[512,2048]{1,0:T(8,128)(2,1)} %refs_0_.13, bf16[512,2048]{1,0:T(8,128)(2,1)S(1)} %copy-done, ...), custom_call_target="tpu_custom_call" | custom-call | tf_op jit(solution)/shard_map/pallas_call | solution.py:37
  21.0 1.6 %collective-permute-done.6.refs_1_ = f32[512,128]{1,0:T(8,128)S(1)} collective-permute-done((f32[512,128]{1,0:T(8,128)S(1)}, f32[512,128]{1,0:T(8,128)S(1)}, u32[]{:S(2)}, u32[]{:S(2)}) %collective-permute-start.6) | collective-permute-done | bytes 262176 | tf_op jit(solution)/shard_map/ppermute | solution.py:379
  22.8 0.5 shard_map.107
  23.2 0.7 %collective-permute-done.5.refs_1_ = f32[512,128]{1,0:T(8,128)S(1)} collective-permute-done((f32[512,128]{1,0:T(8,128)S(1)}, f32[512,128]{1,0:T(8,128)S(1)}, u32[]{:S(2)}, u32[]{:S(2)}) %collective-permute-start.5) | collective-permute-done | bytes 262176 | tf_op jit(solution)/shard_map/ppermute | solution.py:379
  24.1 0.2 collective-permute-done.8.refs_2_
  24.3 0.5 shard_map.109
  24.8 0.5 shard_map.110
  25.3 0.3 collective-permute-done.7.refs_2_
  25.6 0.5 shard_map.111
  26.3 1.7 %collective-permute-start.9 = (f32[8,512]{1,0:T(8,128)S(1)}, f32[8,512]{1,0:T(8,128)S(1)}, u32[]{:S(2)}, u32[]{:S(2)}) collective-permute-start(f32[8,512]{1,0:T(8,128)S(1)} %shard_map.112), channel_id=1, source_target_pairs={{0,1},{1,0},{2,3},{3,2},{4,5},{5,4},{6,7},{7,6},{8,9},{9,8},{10,11... | collective-permute-start | bytes 49160 | tf_op jit(solution)/shard_map/ppermute | solution.py:379
  28.0 2.1 %collective-permute-done.9 = f32[8,512]{1,0:T(8,128)S(1)} collective-permute-done((f32[8,512]{1,0:T(8,128)S(1)}, f32[8,512]{1,0:T(8,128)S(1)}, u32[]{:S(2)}, u32[]{:S(2)}) %collective-permute-start.9) | collective-permute-done | bytes 16416 | tf_op jit(solution)/shard_map/ppermute | solution.py:379
  30.1 2.6 %collective-permute-start.10 = (f32[8,512]{1,0:T(8,128)S(1)}, f32[8,512]{1,0:T(8,128)S(1)}, u32[]{:S(2)}, u32[]{:S(2)}) collective-permute-start(f32[8,512]{1,0:T(8,128)S(1)} %add.3.refs_0_), channel_id=1, source_target_pairs={{0,2},{1,3},{2,0},{3,1},{4,6},{5,7},{6,4},{7,5},{8,10},{9,11},{10,... | collective-permute-start | bytes 49160 | tf_op jit(solution)/shard_map/ppermute | solution.py:379
  32.7 2.0 %collective-permute-done.10.refs_1_ = f32[8,512]{1,0:T(8,128)S(1)} collective-permute-done((f32[8,512]{1,0:T(8,128)S(1)}, f32[8,512]{1,0:T(8,128)S(1)}, u32[]{:S(2)}, u32[]{:S(2)}) %collective-permute-start.10) | collective-permute-done | bytes 16416 | tf_op jit(solution)/shard_map/ppermute | solution.py:379
  35.0 0.5 shard_map.115
  35.6 0.5 shard_map.116
  36.1 0.6 collective-permute-start.12
  36.6 0.5 shard_map.114
  37.2 1.6 %collective-permute-start.13 = (f32[512,128]{1,0:T(8,128)S(1)}, f32[512,128]{1,0:T(8,128)S(1)}, u32[]{:S(2)}, u32[]{:S(2)}) collective-permute-start(f32[512,128]{1,0:T(8,128)S(1)} %shard_map.117.refs_11_.refs_14_.refs_1_), channel_id=1, source_target_pairs={{0,8},{4,12},{8,0},{12,4},{16,24},{20,28},{24,16},{28,20},{1,9},{5... | collective-permute-start | bytes 786440 | tf_op jit(solution)/shard_map/ppermute | solution.py:379
  38.8 0.5 shard_map.118
  39.4 1.2 %collective-permute-start.15 = (f32[512,128]{1,0:T(8,128)S(1)}, f32[512,128]{1,0:T(8,128)S(1)}, u32[]{:S(2)}, u32[]{:S(2)}) collective-permute-start(f32[512,128]{1,0:T(8,128)S(1)} %shard_map.119.refs_12_.refs_15_.refs_1_), channel_id=1, source_target_pairs={{0,16},{4,20},{8,24},{12,28},{16,0},{20,4},{24,8},{28,12},{1,17},{... | collective-permute-start | bytes 786440 | tf_op jit(solution)/shard_map/ppermute | solution.py:379
  40.6 2.1 %shard_map.120 = (bf16[512,2048]{1,0:T(8,128)(2,1)}, bf16[512,2048]{1,0:T(8,128)(2,1)}, f32[512,512]{1,0:T(8,128)S(1)}, f32[512,512]{1,0:T(8,128)S(1)}, bf16[2,512,512]{2,1,0:T(8,128)(2,1)S(1)}) custom-call(bf16[512,2048]{1,0:T(8,128)(2,1)S(1)} %copy-done, bf16[512,512]{1,0:T(8,128)(2,1)S(1)} %get-tuple-element.144.refs_2_.refs_1_, ...), custom_call_target="tpu_custom_call" | custom-call | tf_op jit(solution)/shard_map/pallas_call | solution.py:37
  42.7 2.1 %shard_map.121 = (bf16[512,2048]{1,0:T(8,128)(2,1)}, bf16[512,2048]{1,0:T(8,128)(2,1)}, f32[512,512]{1,0:T(8,128)S(1)}, f32[512,512]{1,0:T(8,128)S(1)}, bf16[2,512,512]{2,1,0:T(8,128)(2,1)S(1)}) custom-call(bf16[512,2048]{1,0:T(8,128)(2,1)S(1)} %copy-done, ...), custom_call_target="tpu_custom_call", output_to_operand_aliasing={{0}: (12, {}), {1}: (13, {})} | custom-call | tf_op jit(solution)/shard_map/pallas_call | solution.py:37
  44.8 0.7 %collective-permute-done.13.refs_0_ = f32[512,128]{1,0:T(8,128)S(1)} collective-permute-done((f32[512,128]{1,0:T(8,128)S(1)}, f32[512,128]{1,0:T(8,128)S(1)}, u32[]{:S(2)}, u32[]{:S(2)}) %collective-permute-start.13) | collective-permute-done | bytes 262176 | tf_op jit(solution)/shard_map/ppermute | solution.py:379
  45.6 1.2 %collective-permute-start.14 = (f32[512,128]{1,0:T(8,128)S(1)}, f32[512,128]{1,0:T(8,128)S(1)}, u32[]{:S(2)}, u32[]{:S(2)}) collective-permute-start(f32[512,128]{1,0:T(8,128)S(1)} %shard_map.122), channel_id=1, source_target_pairs={{0,16},{4,20},{8,24},{12,28},{16,0},{20,4},{24,8},{28,12},{1,17},{... | collective-permute-start | bytes 786440 | tf_op jit(solution)/shard_map/ppermute | solution.py:379
  46.8 0.6 %collective-permute-done.15.refs_0_ = f32[512,128]{1,0:T(8,128)S(1)} collective-permute-done((f32[512,128]{1,0:T(8,128)S(1)}, f32[512,128]{1,0:T(8,128)S(1)}, u32[]{:S(2)}, u32[]{:S(2)}) %collective-permute-start.15) | collective-permute-done | bytes 262176 | tf_op jit(solution)/shard_map/ppermute | solution.py:379
  47.5 1.0 %collective-permute-start.16 = (f32[512,128]{1,0:T(8,128)S(1)}, f32[512,128]{1,0:T(8,128)S(1)}, u32[]{:S(2)}, u32[]{:S(2)}) collective-permute-start(f32[512,128]{1,0:T(8,128)S(1)} %shard_map.127), channel_id=1, source_target_pairs={{0,8},{4,12},{8,0},{12,4},{16,24},{20,28},{24,16},{28,20},{1,9},{5... | collective-permute-start | bytes 786440 | tf_op jit(solution)/shard_map/ppermute | solution.py:379
  48.4 2.0 %shard_map.123 = (bf16[512,2048]{1,0:T(8,128)(2,1)}, bf16[512,2048]{1,0:T(8,128)(2,1)}, f32[512,512]{1,0:T(8,128)S(1)}, f32[512,512]{1,0:T(8,128)S(1)}, bf16[2,512,512]{2,1,0:T(8,128)(2,1)S(1)}) custom-call(bf16[512,2048]{1,0:T(8,128)(2,1)S(1)} %copy-done, ...), custom_call_target="tpu_custom_call", output_to_operand_aliasing={{0}: (12, {}), {1}: (13, {})} | custom-call | tf_op jit(solution)/shard_map/pallas_call | solution.py:37
  50.5 2.1 %shard_map.124 = (bf16[512,2048]{1,0:T(8,128)(2,1)}, bf16[512,2048]{1,0:T(8,128)(2,1)}, f32[512,512]{1,0:T(8,128)S(1)}, f32[512,512]{1,0:T(8,128)S(1)}, bf16[2,512,512]{2,1,0:T(8,128)(2,1)S(1)}) custom-call(bf16[512,2048]{1,0:T(8,128)(2,1)S(1)} %copy-done, ...), custom_call_target="tpu_custom_call", output_to_operand_aliasing={{0}: (12, {}), {1}: (13, {})} | custom-call | tf_op jit(solution)/shard_map/pallas_call | solution.py:37
  52.6 0.5 collective-permute-done.14.refs_1_
  53.3 1.0 %shard_map.126 = (bf16[512,2048]{1,0:T(8,128)(2,1)}, bf16[512,2048]{1,0:T(8,128)(2,1)}, bf16[2,512,512]{2,1,0:T(8,128)(2,1)S(1)}) custom-call(bf16[512,512]{1,0:T(8,128)(2,1)S(1)} %get-tuple-element.137.refs_0_, bf16[512,512]{1,0:T(8,128)(2,1)S(1)} %get-tuple-element.138.refs_1_, ...), custom_call_target="tpu_custom_call", output_to_operand_aliasing={{0}: (8, {}), {1}: (9, {})} | custom-call | tf_op jit(solution)/shard_map/pallas_call | solution.py:37
  54.3 0.4 collective-permute-done.16.refs_1_
  55.0 1.0 %shard_map.129 = (bf16[512,2048]{1,0:T(8,128)(2,1)}, bf16[512,2048]{1,0:T(8,128)(2,1)}, bf16[2,512,512]{2,1,0:T(8,128)(2,1)S(1)}) custom-call(bf16[512,512]{1,0:T(8,128)(2,1)S(1)} %get-tuple-element.223.refs_0_, bf16[512,512]{1,0:T(8,128)(2,1)S(1)} %get-tuple-element.224.refs_1_, f32[512,512]{1,0:T(8,128)S(1)} %get-tuple-element.225.refs_2_, ...), custom_call_target="tpu_custom_call" | custom-call | tf_op jit(solution)/shard_map/pallas_call | solution.py:37
  56.0 1.5 %shard_map.130 = (bf16[512,2048]{1,0:T(8,128)(2,1)}, bf16[512,2048]{1,0:T(8,128)(2,1)}) custom-call(bf16[512,512]{1,0:T(8,128)(2,1)S(1)} %get-tuple-element.218.refs_0_, bf16[512,512]{1,0:T(8,128)(2,1)S(1)} %get-tuple-element.219.refs_1_, f32[512,512]{1,0:T(8,128)S(1)} %get-tuple-element.203.refs_8_.refs_2_, ...), custom_call_target="tpu_custom_call", output_to_operand_aliasing={{0}: (8, {}), {1}: (9, {})} | custom-call | tf_op jit(solution)/shard_map/pallas_call | solution.py:37
  57.4 1.5 %shard_map.131 = (bf16[512,2048]{1,0:T(8,128)(2,1)}, bf16[512,2048]{1,0:T(8,128)(2,1)}) custom-call(bf16[512,512]{1,0:T(8,128)(2,1)S(1)} %get-tuple-element.211.refs_0_, bf16[512,512]{1,0:T(8,128)(2,1)S(1)} %get-tuple-element.212.refs_1_, f32[512,512]{1,0:T(8,128)S(1)} %get-tuple-element.213.refs_2_, ...), custom_call_target="tpu_custom_call", output_to_operand_aliasing={{0}: (7, {}), {1}: (8, {})} | custom-call | tf_op jit(solution)/shard_map/pallas_call | solution.py:37
  (40 shorter events, 2.0 us)
Async XLA Ops:
  3.4 1.7 %collective-permute-start = (f32[520,128]{1,0:T(8,128)S(1)}, f32[520,128]{1,0:T(8,128)S(1)}, u32[]{:S(2)}, u32[]{:S(2)}) collective-permute-start(f32[520,128]{1,0:T(8,128)S(1)} %get-tuple-element.127), channel_id=1, source_target_pairs={{0,4},{4,0},{8,12},{12,8},{16,20},{20,16},{24,28},{28,24},{1,5},{5... | collective-permute-start | bytes 798728 | tf_op jit(solution)/shard_map/ppermute | solution.py:379
  4.2 4.0 %collective-permute-start.1 = (f32[512,128]{1,0:T(8,128)S(1)}, f32[512,128]{1,0:T(8,128)S(1)}, u32[]{:S(2)}, u32[]{:S(2)}) collective-permute-start(f32[512,128]{1,0:T(8,128)S(1)} %get-tuple-element.130.refs_4_), channel_id=1, source_target_pairs={{0,4},{4,0},{8,12},{12,8},{16,20},{20,16},{24,28},{28,24},{1,5},{5... | collective-permute-start | bytes 786440 | tf_op jit(solution)/shard_map/ppermute | solution.py:379
  4.7 5.6 %copy-start = (bf16[512,2048]{1,0:T(8,128)(2,1)S(1)}, bf16[512,2048]{1,0:T(8,128)(2,1)}, u32[]{:S(2)}) copy-start(bf16[512,2048]{1,0:T(8,128)(2,1)} %refs_0_.17) | copy-start | bytes 6291460
  5.2 9.6 %collective-permute-start.3 = (f32[520,128]{1,0:T(8,128)S(1)}, f32[520,128]{1,0:T(8,128)S(1)}, u32[]{:S(2)}, u32[]{:S(2)}) collective-permute-start(f32[520,128]{1,0:T(8,128)S(1)} %shard_map.96.refs_1_.refs_9_), channel_id=1, source_target_pairs={{0,8},{4,12},{8,0},{12,4},{16,24},{20,28},{24,16},{28,20},{1,9},{5... | collective-permute-start | bytes 798728 | tf_op jit(solution)/shard_map/ppermute | solution.py:379
  8.2 8.5 %collective-permute-start.2 = (f32[512,128]{1,0:T(8,128)S(1)}, f32[512,128]{1,0:T(8,128)S(1)}, u32[]{:S(2)}, u32[]{:S(2)}) collective-permute-start(f32[512,128]{1,0:T(8,128)S(1)} %shard_map.98.refs_2_.refs_10_.refs_1_), channel_id=1, source_target_pairs={{0,16},{4,20},{8,24},{12,28},{16,0},{20,4},{24,8},{28,12},{1,17},{... | collective-permute-start | bytes 786440 | tf_op jit(solution)/shard_map/ppermute | solution.py:379
  10.0 6.7 %collective-permute-start.4 = (f32[8,128]{1,0:T(8,128)S(1)}, f32[8,128]{1,0:T(8,128)S(1)}, u32[]{:S(2)}, u32[]{:S(2)}) collective-permute-start(f32[8,128]{1,0:T(8,128)S(1)} %slice.100), channel_id=1, source_target_pairs={{0,24},{4,28},{8,16},{12,20},{16,8},{20,12},{24,0},{28,4},{1,25},{... | collective-permute-start | bytes 12296 | tf_op jit(solution)/shard_map/ppermute | solution.py:379
  14.8 7.7 %collective-permute-start.6 = (f32[512,128]{1,0:T(8,128)S(1)}, f32[512,128]{1,0:T(8,128)S(1)}, u32[]{:S(2)}, u32[]{:S(2)}) collective-permute-start(f32[512,128]{1,0:T(8,128)S(1)} %shard_map.105), channel_id=1, source_target_pairs={{0,16},{4,20},{8,24},{12,28},{16,0},{20,4},{24,8},{28,12},{1,17},{... | collective-permute-start | bytes 786440 | tf_op jit(solution)/shard_map/ppermute | solution.py:379
  16.8 7.1 %collective-permute-start.5 = (f32[512,128]{1,0:T(8,128)S(1)}, f32[512,128]{1,0:T(8,128)S(1)}, u32[]{:S(2)}, u32[]{:S(2)}) collective-permute-start(f32[512,128]{1,0:T(8,128)S(1)} %shard_map.102), channel_id=1, source_target_pairs={{0,8},{4,12},{8,0},{12,4},{16,24},{20,28},{24,16},{28,20},{1,9},{5... | collective-permute-start | bytes 786440 | tf_op jit(solution)/shard_map/ppermute | solution.py:379
  22.7 1.6 %collective-permute-start.8 = (f32[512,128]{1,0:T(8,128)S(1)}, f32[512,128]{1,0:T(8,128)S(1)}, u32[]{:S(2)}, u32[]{:S(2)}) collective-permute-start(f32[512,128]{1,0:T(8,128)S(1)} %get-tuple-element.161), channel_id=1, source_target_pairs={{0,4},{4,0},{8,12},{12,8},{16,20},{20,16},{24,28},{28,24},{1,5},{5... | collective-permute-start | bytes 786440 | tf_op jit(solution)/shard_map/ppermute | solution.py:379
  24.0 1.6 %collective-permute-start.7 = (f32[512,128]{1,0:T(8,128)S(1)}, f32[512,128]{1,0:T(8,128)S(1)}, u32[]{:S(2)}, u32[]{:S(2)}) collective-permute-start(f32[512,128]{1,0:T(8,128)S(1)} %get-tuple-element.153), channel_id=1, source_target_pairs={{0,4},{4,0},{8,12},{12,8},{16,20},{20,16},{24,28},{28,24},{1,5},{5... | collective-permute-start | bytes 786440 | tf_op jit(solution)/shard_map/ppermute | solution.py:379
  26.3 3.8 %collective-permute-start.9 = (f32[8,512]{1,0:T(8,128)S(1)}, f32[8,512]{1,0:T(8,128)S(1)}, u32[]{:S(2)}, u32[]{:S(2)}) collective-permute-start(f32[8,512]{1,0:T(8,128)S(1)} %shard_map.112), channel_id=1, source_target_pairs={{0,1},{1,0},{2,3},{3,2},{4,5},{5,4},{6,7},{7,6},{8,9},{9,8},{10,11... | collective-permute-start | bytes 49160 | tf_op jit(solution)/shard_map/ppermute | solution.py:379
  30.1 4.6 %collective-permute-start.10 = (f32[8,512]{1,0:T(8,128)S(1)}, f32[8,512]{1,0:T(8,128)S(1)}, u32[]{:S(2)}, u32[]{:S(2)}) collective-permute-start(f32[8,512]{1,0:T(8,128)S(1)} %add.3.refs_0_), channel_id=1, source_target_pairs={{0,2},{1,3},{2,0},{3,1},{4,6},{5,7},{6,4},{7,5},{8,10},{9,11},{10,... | collective-permute-start | bytes 49160 | tf_op jit(solution)/shard_map/ppermute | solution.py:379
  35.5 1.7 %collective-permute-start.11 = (f32[512,128]{1,0:T(8,128)S(1)}, f32[512,128]{1,0:T(8,128)S(1)}, u32[]{:S(2)}, u32[]{:S(2)}) collective-permute-start(f32[512,128]{1,0:T(8,128)S(1)} %get-tuple-element.181), channel_id=1, source_target_pairs={{0,4},{4,0},{8,12},{12,8},{16,20},{20,16},{24,28},{28,24},{1,5},{5... | collective-permute-start | bytes 786440 | tf_op jit(solution)/shard_map/ppermute | solution.py:379
  36.1 3.2 %collective-permute-start.12 = (f32[512,128]{1,0:T(8,128)S(1)}, f32[512,128]{1,0:T(8,128)S(1)}, u32[]{:S(2)}, u32[]{:S(2)}) collective-permute-start(f32[512,128]{1,0:T(8,128)S(1)} %get-tuple-element.184.refs_4_), channel_id=1, source_target_pairs={{0,4},{4,0},{8,12},{12,8},{16,20},{20,16},{24,28},{28,24},{1,5},{5... | collective-permute-start | bytes 786440 | tf_op jit(solution)/shard_map/ppermute | solution.py:379
  37.2 8.3 %collective-permute-start.13 = (f32[512,128]{1,0:T(8,128)S(1)}, f32[512,128]{1,0:T(8,128)S(1)}, u32[]{:S(2)}, u32[]{:S(2)}) collective-permute-start(f32[512,128]{1,0:T(8,128)S(1)} %shard_map.117.refs_11_.refs_14_.refs_1_), channel_id=1, source_target_pairs={{0,8},{4,12},{8,0},{12,4},{16,24},{20,28},{24,16},{28,20},{1,9},{5... | collective-permute-start | bytes 786440 | tf_op jit(solution)/shard_map/ppermute | solution.py:379
  39.4 8.1 %collective-permute-start.15 = (f32[512,128]{1,0:T(8,128)S(1)}, f32[512,128]{1,0:T(8,128)S(1)}, u32[]{:S(2)}, u32[]{:S(2)}) collective-permute-start(f32[512,128]{1,0:T(8,128)S(1)} %shard_map.119.refs_12_.refs_15_.refs_1_), channel_id=1, source_target_pairs={{0,16},{4,20},{8,24},{12,28},{16,0},{20,4},{24,8},{28,12},{1,17},{... | collective-permute-start | bytes 786440 | tf_op jit(solution)/shard_map/ppermute | solution.py:379
  45.6 7.5 %collective-permute-start.14 = (f32[512,128]{1,0:T(8,128)S(1)}, f32[512,128]{1,0:T(8,128)S(1)}, u32[]{:S(2)}, u32[]{:S(2)}) collective-permute-start(f32[512,128]{1,0:T(8,128)S(1)} %shard_map.122), channel_id=1, source_target_pairs={{0,16},{4,20},{8,24},{12,28},{16,0},{20,4},{24,8},{28,12},{1,17},{... | collective-permute-start | bytes 786440 | tf_op jit(solution)/shard_map/ppermute | solution.py:379
  47.5 7.2 %collective-permute-start.16 = (f32[512,128]{1,0:T(8,128)S(1)}, f32[512,128]{1,0:T(8,128)S(1)}, u32[]{:S(2)}, u32[]{:S(2)}) collective-permute-start(f32[512,128]{1,0:T(8,128)S(1)} %shard_map.127), channel_id=1, source_target_pairs={{0,8},{4,12},{8,0},{12,4},{16,24},{20,28},{24,16},{28,20},{1,9},{5... | collective-permute-start | bytes 786440 | tf_op jit(solution)/shard_map/ppermute | solution.py:379
  53.2 1.8 %collective-permute-start.18 = (f32[512,128]{1,0:T(8,128)S(1)}, f32[512,128]{1,0:T(8,128)S(1)}, u32[]{:S(2)}, u32[]{:S(2)}) collective-permute-start(f32[512,128]{1,0:T(8,128)S(1)} %get-tuple-element.227), channel_id=1, source_target_pairs={{0,4},{4,0},{8,12},{12,8},{16,20},{20,16},{24,28},{28,24},{1,5},{5... | collective-permute-start | bytes 786440 | tf_op jit(solution)/shard_map/ppermute | solution.py:379
  54.8 2.7 %collective-permute-start.17 = (f32[512,128]{1,0:T(8,128)S(1)}, f32[512,128]{1,0:T(8,128)S(1)}, u32[]{:S(2)}, u32[]{:S(2)}) collective-permute-start(f32[512,128]{1,0:T(8,128)S(1)} %get-tuple-element.216), channel_id=1, source_target_pairs={{0,4},{4,0},{8,12},{12,8},{16,20},{20,16},{24,28},{28,24},{1,5},{5... | collective-permute-start | bytes 786440 | tf_op jit(solution)/shard_map/ppermute | solution.py:379

commit v3 on v2

--- a/solution.py
+++ b/solution.py
@@ -185,30 +185,27 @@
 
 def second_kernel(count, group, reverse, one, own, factor, factor_x, factor_d, send):
     _, x, y = bits(reverse)
-    right, later = x == 1, y == 1
+    over_x, right, later = (bits()[0] if group is None else group) == 0, x == 1, y == 1
     for n in range(count):
         f, fx, fd = factor[n : n + 1, :], factor_x[n : n + 1, :], factor_d[n : n + 1, :]
-        if group == 0:
-            p = jnp.where(right, f, 1.0)
-            q = jnp.where(right, 1.0, fx)
-        else:
-            p = jnp.where(later, jnp.where(right, 1.0, f * fd), 0.0)
-            q = jnp.where(later, jnp.where(right, 0.0, jnp.ones_like(f)), 1.0)
+        ones = jnp.ones_like(f)
+        p = jnp.where(over_x, jnp.where(right, f, 1.0), jnp.where(later, jnp.where(right, 1.0, f * fd), 0.0))
+        q = jnp.where(over_x, jnp.where(right, 1.0, fx), jnp.where(later, jnp.where(right, 0.0, ones), 1.0))
         send[span(n), :] = p * one[span(n), :] + q * own[span(n), :]
 
 
 def enter_kernel(count, group, reverse, one, two, factor_x, factor_d, own_factor, other_factor, kept, got, mine, send):
     core, x, y = bits(reverse)
-    lower, right, later = core == 0, x == 1, y == 1
+    over_x, lower, right, later = (bits()[0] if group is None else group) == 0, core == 0, x == 1, y == 1
     for n in range(count):
         fx, fd = factor_x[n : n + 1, :], factor_d[n : n + 1, :]
         ones = jnp.ones_like(fx)
-        if group == 0:
-            w = jnp.where(right, ones, 0.0)
-            u = jnp.where(later, jnp.where(right, fx, 1.0), 0.0)
-        else:
-            w = jnp.where(later, jnp.where(right, fx, fd), 0.0)
-            u = jnp.where(later, ones, jnp.where(right, ones, 0.0))
+        w = jnp.where(over_x, jnp.where(right, ones, 0.0), jnp.where(later, jnp.where(right, fx, fd), 0.0))
+        u = jnp.where(
+            over_x,
+            jnp.where(later, jnp.where(right, fx, 1.0), 0.0),
+            jnp.where(later, ones, jnp.where(right, ones, 0.0)),
+        )
         low = w * one[span(n), :] + u * two[span(n), :]
         f = jnp.where(lower, own_factor[n : n + 1, :], other_factor[n : n + 1, :])
         high = f * low + jnp.where(lower, kept[span(n), :], got[span(n), :])
@@ -275,16 +272,18 @@
 def sum_kernel(squares, crossed, sums):
     square = jnp.sum(squares[...].T, axis=0, keepdims=True)
     cross = jnp.sum(crossed[...].T, axis=0, keepdims=True)
-    first = lax.broadcasted_iota(jnp.int32, (8, BLOCK), 0) == 0
-    sums[...] = jnp.where(first, square, cross)
+    for n in range(BLOCK // E):
+        sums[n : n + 1, :] = square[:, span(n)]
+        sums[n + 4 : n + 5, :] = cross[:, span(n)]
 
 
 def scale_kernel(features, ours, theirs, inverse, coefficient):
     sums = ours[...] + theirs[...]
-    inv = lax.rsqrt(sums[0:1, :] / features + EPSILON)
-    coef = inv * inv * inv * sums[1:2, :] / features
-    inverse[...] = jnp.broadcast_to(inv, (E, BLOCK)).T
-    coefficient[...] = jnp.broadcast_to(coef, (E, BLOCK)).T
+    inv = lax.rsqrt(sums[0:4, :] / features + EPSILON)
+    coef = inv * inv * inv * sums[4:8, :] / features
+    for n in range(BLOCK // E):
+        inverse[span(n), :] = jnp.broadcast_to(inv[n : n + 1, :], (E, E)).T
+        coefficient[span(n), :] = jnp.broadcast_to(coef[n : n + 1, :], (E, E)).T
 
 
 def outer_kernel(half, index, inverse, coefficient, attended, query_dec_t, factor, grad_out, gain, d_attended, flow, late):
@@ -349,34 +348,50 @@
         copy.wait()
 
 
-def leave_kernel(half, index, before, last, split, value_dec, key_dec, intra_k, intra_v, leaving, late, factor, *refs):
-    staged, sems, out_sems = refs[-3:]
-    made = []
-    if before is not None:
-        made = flush(refs[0], refs[-7:-5] if split else refs[-5:-3], sems, half, before)
-    @beside_copies
-    def _():
-        flows, products = [], []
-        for n, i in enumerate(index):
-            now = leaving[span(n), :]
-            flows.append((n, 1, now.astype(BF16)))
-            flows.append((n, 0, (factor[1, i : i + 1, :] * now + late[span(n), :]).astype(BF16)))
-        for n, c, flow in flows:
-            at = chunk(c)
-            products.append((n, c, dot(value_dec[at, span(n)], flow, (1, 1)), dot(key_dec[at, span(n)], flow, (1, 0))))
-        for n, c, of_key, of_value in products:
-            at = chunk(c)
-            staged[0, at, span(n)] = (intra_k[at, span(n)] + of_key).astype(BF16)
-            staged[1, at, span(n)] = (intra_v[at, span(n)] + of_value).astype(BF16)
-
-    if last:
-        made += flush(staged, refs[-5:-3], out_sems, half, index)
+def leave_part(index, start, value_dec, key_dec, intra_k, intra_v, leaving, late, factor, staged):
+    flows, products = [], []
+    for n, i in enumerate(index, start):
+        now = leaving[span(n), :]
+        flows.append((n, 1, now.astype(BF16)))
+        flows.append((n, 0, (factor[1, i : i + 1, :] * now + late[span(n), :]).astype(BF16)))
+    for n, c, flow in flows:
+        at = chunk(c)
+        products.append((n, c, dot(value_dec[at, span(n)], flow, (1, 1)), dot(key_dec[at, span(n)], flow, (1, 0))))
+    for n, c, of_key, of_value in products:
+        at = chunk(c)
+        staged[0, at, span(n)] = (intra_k[at, span(n)] + of_key).astype(BF16)
+        staged[1, at, span(n)] = (intra_v[at, span(n)] + of_value).astype(BF16)
+
+
+def leave_kernel(half, before, parts, last, counts, factor, *refs):
+    held, aliased, targets = counts
+    sources, refs = refs[: 6 * len(parts)], refs[6 * len(parts) :]
+    outs = refs[held + aliased : held + aliased + targets]
+    staged, sems = refs[-1 - len(parts) : -1], refs[-1]
+    if not last:
+        staged = (*staged[1:], staged[0])
+    made = flush(refs[0], outs[:2], sems.at[0], half, before) if held else []
+    for n, index in enumerate(parts):
+        part = sources[6 * n : 6 * n + 6]
+        final = last and n == len(parts) - 1
+        cuts = 2 if final and len(index) % 2 == 0 else 1
+        size = len(index) // cuts
+        for k in range(cuts):
+            some = index[k * size : (k + 1) * size]
+            beside_copies(functools.partial(leave_part, some, k * size, *part, factor, staged[n]))
+            if final or n < len(parts) - 1:
+                ready = staged[n].at[:, :, span(k * size, size)]
+                made += flush(ready, outs[-2:], sems.at[1 + n + k], half, some)
     for copy in made:
         copy.wait()
 
 
 def exchange(x, axis, bit):
     return lax.ppermute(x, axis, [(i, i ^ bit) for i in range(lax.axis_size(axis))])
+
+
+def crossing(x, group, step):
+    return lax.ppermute(x, "ctx", [(i, i ^ (2 if (i % 2 if group is None else group) == step else 4)) for i in range(8)])
 
 
 def gathered(contrib, factor, reverse):
@@ -423,7 +438,6 @@
     index = {(g, side): [side * (half or 0) + g * own + i for i in range(own)] for g, side in pieces}
     tall, flat, wide = (own * E, E), (BLOCK, own * E), (BLOCK, E)
     staged_shape = ((2, BLOCK, own * E), BF16)
-    bits_of = {0: (2, 4), 1: (4, 2)}
 
     def at(g):
         return slice(g * own, (g + 1) * own)
@@ -454,21 +468,21 @@
         (chip,) = call(
             functools.partial(chip_kernel, own, reverse), [((own * E + more, E), F32)], kept, got, f, h, after=after
         )
-        return kept, got, chip, exchange(chip, "ctx", bits_of[g][0])
+        return kept, got, chip, crossing(chip, None if reverse else g, 0)
 
     def second_step(reverse, g, step, after):
         kept, got, chip, one = step
         (send,) = call(
-            functools.partial(second_kernel, own, g, reverse), [(tall, F32)],
-            one, chip, chip_factor[at(g)], factor_x[at(g)], (factor_d if g else factor_x)[at(g)], after=after,
-        )
-        return *step, exchange(send, "ctx", bits_of[g][1])
+            functools.partial(second_kernel, own, None if reverse else g, reverse), [(tall, F32)],
+            one, chip, chip_factor[at(g)], factor_x[at(g)], (factor_d if g or reverse else factor_x)[at(g)], after=after,
+        )
+        return *step, send, crossing(send, None if reverse else g, 1)
 
     def last_step(reverse, g, step, after):
-        kept, got, chip, one, two = step
+        kept, got, chip, one, _, two = step
         enter, send = call(
-            functools.partial(enter_kernel, own, g, reverse), [(tall, F32)] * 2,
-            one, two, factor_x[at(g)], (factor_d if g else factor_x)[at(g)], own_factor[at(g)], other_factor[at(g)], kept, got,
+            functools.partial(enter_kernel, own, None if reverse else g, reverse), [(tall, F32)] * 2,
+            one, two, factor_x[at(g)], (factor_d if g or reverse else factor_x)[at(g)], own_factor[at(g)], other_factor[at(g)], kept, got,
             after=after,
         )
         return {(g, 0): enter, (g, 1): exchange(send, "ctx", 1)}
@@ -524,7 +538,7 @@
     for piece in late_pieces:
         if piece not in attended:
             sums = attend(piece, sums)
-    (sums,) = call(sum_kernel, [((8, BLOCK), F32)], *sums)
+    (sums,) = call(sum_kernel, [((8, E), F32)], *sums)
     inverse, coefficient = call(functools.partial(scale_kernel, features), [(wide, F32)] * 2, *summed(sums))
 
     d_attended, flow, late = {}, {}, {}
@@ -566,47 +580,37 @@
         )
         before, staged = index[piece], [out]
 
-    leaving, others = {}, []
-
-    def leave(piece, before, staged, results, others):
-        last = piece in late_pieces[-2:]
-        first = piece == late_pieces[0]
-        split = first and last
-        held = results if first else others
-        args = [
-            value_dec[piece], key_dec[piece], intra_k[piece], intra_v[piece],
-            leaving[piece], late[piece], factor, *staged, *held,
-        ]
-        where = (len(args) - 2, len(args) - 1) if held else ()
-        outs = 4 if split else 2
-        made = call(
-            functools.partial(leave_kernel, half, index[piece], before, last, split),
-            [full] * outs + [staged_shape] * (not last),
-            *args, anywhere=where, alias=dict(zip(where, (0, 1))), outs_anywhere=outs,
-            scratch=[pltpu.VMEM(*staged_shape)] * last + [sems, sems],
-        )
-        out = None if last else made[-1]
-        made = made[:outs]
-        if first:
-            results, others = made[:2], made[2:]
-        else:
-            others = made
-        return (None, [], results, others) if last else (index[piece], [out], results, others)
-
-    carried = (before, staged, results, others)
+    def leave(group, last, before, held, aliased, targets):
+        args = [factor]
+        for piece in group:
+            args += [value_dec[piece], key_dec[piece], intra_k[piece], intra_v[piece], leaving[piece], late[piece]]
+        args += [*held, *aliased]
+        where = tuple(range(len(args) - len(aliased), len(args)))
+        inside = len(group) if last else len(group) - 1
+        return call(
+            functools.partial(
+                leave_kernel, half, before, [index[piece] for piece in group], last, (len(held), len(aliased), targets)
+            ),
+            [full] * targets + [staged_shape] * (not last),
+            *args, anywhere=where, alias={n: m for m, n in enumerate(where)}, outs_anywhere=targets,
+            scratch=[pltpu.VMEM(*staged_shape)] * inside + [pltpu.SemaphoreType.DMA((2 + len(group), 2))],
+        )
+
+    leaving, tail = {}, []
     if fast:
         for g in range(groups):
-            steps[g] = second_step(True, g, steps[g], [intra_k[pieces[1]]])
+            steps[g] = second_step(True, g, steps[g], [intra_k[pieces[1 + g]], *steps[0][4:5]])
         for g in range(groups):
-            leaving |= last_step(True, g, steps[g], [intra_k[pieces[-1]], *carried[1]])
+            leaving |= last_step(True, g, steps[g], [intra_k[pieces[-1]], *tail])
             if g == 0:
-                carried = leave((0, 0), *carried)
+                normed, grad_q, out = leave([(0, 0)], False, before, staged, results, 2)
+                tail = [out]
+        *results, out = leave([(0, 1), (1, 0)], False, index[0, 0], [out], [], 2)
+        grad_k, grad_v = leave([(1, 1)], True, index[1, 0], [out], results, 2)
     else:
         leaving[pieces[0]] = gathered(flow[pieces[0]], whole_factor[:heads], True)
-    for n, piece in enumerate(late_pieces):
-        if n or not fast:
-            carried = leave(piece, *carried)
-    return *carried[2], *carried[3]
+        normed, grad_q, grad_k, grad_v = leave([pieces[0]], True, before, staged, results, 4)
+    return normed, grad_q, grad_k, grad_v
 
 
 def solution(mesh):

time: 59.3 us -> 57.2 us (0.965)
  Pallas kernels: 27.8 us -> 26.7 us
  starting transfers between devices: 19.2 us -> 18.4 us
    ppermute x19 -> x11, starting transfers between devices: 19.2 us -> 6.09 us  [exchange(): lax.ppermute(x, axis, [(i, i ^ bit) for i in range(lax.axis_size(axis))])]
    ppermute x0 -> x8, starting transfers between devices: none -> 12.3 us  [crossing(): lax.ppermute(x, 'ctx', [(i, i ^ (2 if (i % 2 if group is None else group)...]
    ppermute x19 -> x11, waiting for transfers between devices: 10.9 us -> 4.47 us  [exchange(): lax.ppermute(x, axis, [(i, i ^ bit) for i in range(lax.axis_size(axis))])]
    ppermute x0 -> x8, waiting for transfers between devices: none -> 6.25 us  [crossing(): lax.ppermute(x, 'ctx', [(i, i ^ (2 if (i % 2 if group is None else group)...]
    pallas_call x39 -> x38, Pallas kernels: 27.8 us -> 26.7 us  [call(): pl.pallas_call(body, out_shape=[(pltpu.HBM if n < outs_anywhere else pltp...]
  transfers between devices with their start and end apart: 19 -> 19, of which waited for: 11 -> 9; matrix products, arithmetic and copies ran while one was open for 0% -> 0% of each run, Pallas kernels for 38% -> 37%
where the time goes in v3:
time: 57.2 us; the launch traced here: 57 us
  Pallas kernels  26.7 us (47%)
  starting transfers between devices  18.4 us (32%)
  waiting for transfers between devices  10.7 us (19%)
  between operations  1.17 us (2%)
    pallas_call x38, Pallas kernels, call(): pl.pallas_call(body, out_shape=[(pltpu.HBM if n < outs_anywhere else pltp...  26.7 us
    ppermute x8, starting transfers between devices, crossing(): lax.ppermute(x, 'ctx', [(i, i ^ (2 if (i % 2 if group is None else group)...  12.3 us
    ppermute x8, waiting for transfers between devices, crossing(): lax.ppermute(x, 'ctx', [(i, i ^ (2 if (i % 2 if group is None else group)...  6.25 us
    ppermute x11, starting transfers between devices, exchange(): lax.ppermute(x, axis, [(i, i ^ bit) for i in range(lax.axis_size(axis))])  6.09 us
    ppermute x11, waiting for transfers between devices, exchange(): lax.ppermute(x, axis, [(i, i ^ bit) for i in range(lax.axis_size(axis))])  4.47 us
  transfers between devices with their start and end apart: 19, of which 9 were waited for; matrix products, arithmetic and copies ran while one was open for 0% of the time, Pallas kernels for 37%

profile of v3, /device:TPU:0, one launch (start us, length us, event | category | flops | bytes accessed | tf_op | source)
XLA Modules:
  0.0 57.0 jit_solution(10431248267443191535)
XLA Ops:
  0.6 2.7 %shard_map.93 = (f32[16,512]{1,0:T(8,128)S(1)}, f32[16,512]{1,0:T(8,128)S(1)}, f32[16,512]{1,0:T(8,128)S(1)}, f32[3,16,128]{2,1,0:T(8,128)S(1)}, f32[1,2048]{1,0...) custom-call(f32[16,512]{1,0:T(8,128)} %refs_0_.9, ...), custom_call_target="tpu_custom_call" | custom-call | tf_op jit(solution)/shard_map/pallas_call | solution.py:37
  3.4 0.5 collective-permute-start
  3.8 0.3 shard_map.95
  4.2 0.2 collective-permute-start.1
  4.4 0.3 shard_map.94
  4.7 0.4 shard_map.97
  5.2 3.0 %collective-permute-start.3 = (f32[520,128]{1,0:T(8,128)S(1)}, f32[520,128]{1,0:T(8,128)S(1)}, u32[]{:S(2)}, u32[]{:S(2)}) collective-permute-start(f32[520,128]{1,0:T(8,128)S(1)} %shard_map.96.refs_1_.refs_9_), channel_id=1, source_target_pairs={{0,8},{4,12},{8,0},{12,4},{16,24},{20,28},{24,16},{28,20},{1,9},{5... | collective-permute-start | bytes 798728 | tf_op jit(solution)/shard_map/ppermute | solution.py:394
  8.2 1.6 %collective-permute-start.2 = (f32[512,128]{1,0:T(8,128)S(1)}, f32[512,128]{1,0:T(8,128)S(1)}, u32[]{:S(2)}, u32[]{:S(2)}) collective-permute-start(f32[512,128]{1,0:T(8,128)S(1)} %shard_map.98.refs_2_.refs_10_.refs_1_), channel_id=1, source_target_pairs={{0,16},{4,20},{8,24},{12,28},{16,0},{20,4},{24,8},{28,12},{1,17},{... | collective-permute-start | bytes 786440 | tf_op jit(solution)/shard_map/ppermute | solution.py:394
  9.8 0.2 shard_map.99
  10.0 0.3 collective-permute-start.4
  10.3 1.4 %shard_map.100 = (f32[512,512]{1,0:T(8,128)S(1)}, bf16[512,512]{1,0:T(8,128)(2,1)S(1)}, bf16[512,512]{1,0:T(8,128)(2,1)S(1)}, bf16[512,512]{1,0:T(8,128)(2,1)S(1...) custom-call(bf16[512,2048]{1,0:T(8,128)(2,1)} %refs_0_.13, bf16[512,2048]{1,0:T(8,128)(2,1)S(1)} %copy-done, ...), custom_call_target="tpu_custom_call" | custom-call | tf_op jit(solution)/shard_map/pallas_call | solution.py:37
  11.6 1.4 %shard_map.104 = (f32[512,512]{1,0:T(8,128)S(1)}, bf16[512,512]{1,0:T(8,128)(2,1)S(1)}, bf16[512,512]{1,0:T(8,128)(2,1)S(1)}, bf16[512,512]{1,0:T(8,128)(2,1)S(1...) custom-call(bf16[512,2048]{1,0:T(8,128)(2,1)} %refs_0_.13, bf16[512,2048]{1,0:T(8,128)(2,1)S(1)} %copy-done, ...), custom_call_target="tpu_custom_call" | custom-call | tf_op jit(solution)/shard_map/pallas_call | solution.py:37
  13.0 1.8 %collective-permute-done.3.refs_0_ = f32[520,128]{1,0:T(8,128)S(1)} collective-permute-done((f32[520,128]{1,0:T(8,128)S(1)}, f32[520,128]{1,0:T(8,128)S(1)}, u32[]{:S(2)}, u32[]{:S(2)}) %collective-permute-start.3) | collective-permute-done | bytes 266272 | tf_op jit(solution)/shard_map/ppermute | solution.py:394
  14.8 1.8 %collective-permute-start.6 = (f32[512,128]{1,0:T(8,128)S(1)}, f32[512,128]{1,0:T(8,128)S(1)}, u32[]{:S(2)}, u32[]{:S(2)}) collective-permute-start(f32[512,128]{1,0:T(8,128)S(1)} %shard_map.105), channel_id=1, source_target_pairs={{0,16},{4,20},{8,24},{12,28},{16,0},{20,4},{24,8},{28,12},{1,17},{... | collective-permute-start | bytes 786440 | tf_op jit(solution)/shard_map/ppermute | solution.py:394
  16.8 1.6 %collective-permute-start.5 = (f32[512,128]{1,0:T(8,128)S(1)}, f32[512,128]{1,0:T(8,128)S(1)}, u32[]{:S(2)}, u32[]{:S(2)}) collective-permute-start(f32[512,128]{1,0:T(8,128)S(1)} %shard_map.102), channel_id=1, source_target_pairs={{0,8},{4,12},{8,0},{12,4},{16,24},{20,28},{24,16},{28,20},{1,9},{5... | collective-permute-start | bytes 786440 | tf_op jit(solution)/shard_map/ppermute | solution.py:394
  18.3 1.3 %shard_map.101 = (f32[512,512]{1,0:T(8,128)S(1)}, bf16[512,512]{1,0:T(8,128)(2,1)S(1)}, bf16[512,512]{1,0:T(8,128)(2,1)S(1)}, bf16[512,512]{1,0:T(8,128)(2,1)S(1...) custom-call(bf16[512,2048]{1,0:T(8,128)(2,1)} %refs_0_.13, bf16[512,2048]{1,0:T(8,128)(2,1)S(1)} %copy-done, ...), custom_call_target="tpu_custom_call" | custom-call | tf_op jit(solution)/shard_map/pallas_call | solution.py:37
  19.6 1.3 %shard_map.103 = (f32[512,512]{1,0:T(8,128)S(1)}, bf16[512,512]{1,0:T(8,128)(2,1)S(1)}, bf16[512,512]{1,0:T(8,128)(2,1)S(1)}, bf16[512,512]{1,0:T(8,128)(2,1)S(1...) custom-call(bf16[512,2048]{1,0:T(8,128)(2,1)} %refs_0_.13, bf16[512,2048]{1,0:T(8,128)(2,1)S(1)} %copy-done, ...), custom_call_target="tpu_custom_call" | custom-call | tf_op jit(solution)/shard_map/pallas_call | solution.py:37
  21.0 1.6 %collective-permute-done.6.refs_1_ = f32[512,128]{1,0:T(8,128)S(1)} collective-permute-done((f32[512,128]{1,0:T(8,128)S(1)}, f32[512,128]{1,0:T(8,128)S(1)}, u32[]{:S(2)}, u32[]{:S(2)}) %collective-permute-start.6) | collective-permute-done | bytes 262176 | tf_op jit(solution)/shard_map/ppermute | solution.py:394
  22.8 0.5 shard_map.107
  23.2 0.6 %collective-permute-done.5.refs_1_ = f32[512,128]{1,0:T(8,128)S(1)} collective-permute-done((f32[512,128]{1,0:T(8,128)S(1)}, f32[512,128]{1,0:T(8,128)S(1)}, u32[]{:S(2)}, u32[]{:S(2)}) %collective-permute-start.5) | collective-permute-done | bytes 262176 | tf_op jit(solution)/shard_map/ppermute | solution.py:394
  24.1 0.2 collective-permute-done.8.refs_2_
  24.3 0.5 shard_map.109
  24.8 0.5 shard_map.110
  25.3 0.3 collective-permute-done.7.refs_2_
  25.6 0.5 shard_map.111
  26.1 0.2 shard_map.112
  26.3 1.7 %collective-permute-start.9 = (f32[8,128]{1,0:T(8,128)S(1)}, f32[8,128]{1,0:T(8,128)S(1)}, u32[]{:S(2)}, u32[]{:S(2)}) collective-permute-start(f32[8,128]{1,0:T(8,128)S(1)} %shard_map.112), channel_id=1, source_target_pairs={{0,1},{1,0},{2,3},{3,2},{4,5},{5,4},{6,7},{7,6},{8,9},{9,8},{10,11... | collective-permute-start | bytes 12296 | tf_op jit(solution)/shard_map/ppermute | solution.py:390
  28.0 2.0 %collective-permute-done.9 = f32[8,128]{1,0:T(8,128)S(1)} collective-permute-done((f32[8,128]{1,0:T(8,128)S(1)}, f32[8,128]{1,0:T(8,128)S(1)}, u32[]{:S(2)}, u32[]{:S(2)}) %collective-permute-start.9) | collective-permute-done | bytes 4128 | tf_op jit(solution)/shard_map/ppermute | solution.py:390
  30.0 2.6 %collective-permute-start.10 = (f32[8,128]{1,0:T(8,128)S(1)}, f32[8,128]{1,0:T(8,128)S(1)}, u32[]{:S(2)}, u32[]{:S(2)}) collective-permute-start(f32[8,128]{1,0:T(8,128)S(1)} %add.3.refs_0_), channel_id=1, source_target_pairs={{0,2},{1,3},{2,0},{3,1},{4,6},{5,7},{6,4},{7,5},{8,10},{9,11},{10,... | collective-permute-start | bytes 12296 | tf_op jit(solution)/shard_map/ppermute | solution.py:390
  32.6 1.9 %collective-permute-done.10.refs_1_ = f32[8,128]{1,0:T(8,128)S(1)} collective-permute-done((f32[8,128]{1,0:T(8,128)S(1)}, f32[8,128]{1,0:T(8,128)S(1)}, u32[]{:S(2)}, u32[]{:S(2)}) %collective-permute-start.10) | collective-permute-done | bytes 4128 | tf_op jit(solution)/shard_map/ppermute | solution.py:390
  34.5 0.2 shard_map.113
  34.7 0.5 shard_map.115
  35.3 0.5 shard_map.116
  35.8 0.6 collective-permute-start.12
  36.3 0.5 shard_map.114
  36.9 1.6 %collective-permute-start.13 = (f32[512,128]{1,0:T(8,128)S(1)}, f32[512,128]{1,0:T(8,128)S(1)}, u32[]{:S(2)}, u32[]{:S(2)}) collective-permute-start(f32[512,128]{1,0:T(8,128)S(1)} %shard_map.117.refs_11_.refs_14_.refs_1_), channel_id=1, source_target_pairs={{0,8},{4,20},{8,0},{12,28},{16,24},{20,4},{24,16},{28,12},{1,9},{5... | collective-permute-start | bytes 786440 | tf_op jit(solution)/shard_map/ppermute | solution.py:394
  38.5 0.5 shard_map.118
  39.1 0.6 %collective-permute-start.15 = (f32[512,128]{1,0:T(8,128)S(1)}, f32[512,128]{1,0:T(8,128)S(1)}, u32[]{:S(2)}, u32[]{:S(2)}) collective-permute-start(f32[512,128]{1,0:T(8,128)S(1)} %shard_map.119.refs_12_.refs_15_.refs_1_), channel_id=1, source_target_pairs={{0,8},{4,20},{8,0},{12,28},{16,24},{20,4},{24,16},{28,12},{1,9},{5... | collective-permute-start | bytes 786440 | tf_op jit(solution)/shard_map/ppermute | solution.py:394
  39.7 2.0 %shard_map.120 = (bf16[512,2048]{1,0:T(8,128)(2,1)}, bf16[512,2048]{1,0:T(8,128)(2,1)}, f32[512,512]{1,0:T(8,128)S(1)}, f32[512,512]{1,0:T(8,128)S(1)}, bf16[2,512,512]{2,1,0:T(8,128)(2,1)S(1)}) custom-call(bf16[512,2048]{1,0:T(8,128)(2,1)S(1)} %copy-done, bf16[512,512]{1,0:T(8,128)(2,1)S(1)} %get-tuple-element.142.refs_2_.refs_1_, ...), custom_call_target="tpu_custom_call" | custom-call | tf_op jit(solution)/shard_map/pallas_call | solution.py:37
  41.7 2.1 %shard_map.121 = (bf16[512,2048]{1,0:T(8,128)(2,1)}, bf16[512,2048]{1,0:T(8,128)(2,1)}, f32[512,512]{1,0:T(8,128)S(1)}, f32[512,512]{1,0:T(8,128)S(1)}, bf16[2,512,512]{2,1,0:T(8,128)(2,1)S(1)}) custom-call(bf16[512,2048]{1,0:T(8,128)(2,1)S(1)} %copy-done, ...), custom_call_target="tpu_custom_call", output_to_operand_aliasing={{0}: (12, {}), {1}: (13, {})} | custom-call | tf_op jit(solution)/shard_map/pallas_call | solution.py:37
  43.9 1.2 %collective-permute-start.14 = (f32[512,128]{1,0:T(8,128)S(1)}, f32[512,128]{1,0:T(8,128)S(1)}, u32[]{:S(2)}, u32[]{:S(2)}) collective-permute-start(f32[512,128]{1,0:T(8,128)S(1)} %shard_map.122.refs_6_), channel_id=1, source_target_pairs={{0,16},{4,12},{8,24},{12,4},{16,0},{20,28},{24,8},{28,20},{1,17},{... | collective-permute-start | bytes 786440 | tf_op jit(solution)/shard_map/ppermute | solution.py:394
  45.1 2.0 %shard_map.123 = (bf16[512,2048]{1,0:T(8,128)(2,1)}, bf16[512,2048]{1,0:T(8,128)(2,1)}, f32[512,512]{1,0:T(8,128)S(1)}, f32[512,512]{1,0:T(8,128)S(1)}, bf16[2,512,512]{2,1,0:T(8,128)(2,1)S(1)}) custom-call(bf16[512,2048]{1,0:T(8,128)(2,1)S(1)} %copy-done, ...), custom_call_target="tpu_custom_call", output_to_operand_aliasing={{0}: (12, {}), {1}: (13, {})} | custom-call | tf_op jit(solution)/shard_map/pallas_call | solution.py:37
  47.2 0.9 %collective-permute-start.16 = (f32[512,128]{1,0:T(8,128)S(1)}, f32[512,128]{1,0:T(8,128)S(1)}, u32[]{:S(2)}, u32[]{:S(2)}) collective-permute-start(f32[512,128]{1,0:T(8,128)S(1)} %shard_map.127), channel_id=1, source_target_pairs={{0,16},{4,12},{8,24},{12,4},{16,0},{20,28},{24,8},{28,20},{1,17},{... | collective-permute-start | bytes 786440 | tf_op jit(solution)/shard_map/ppermute | solution.py:394
  48.1 2.0 %shard_map.124 = (bf16[512,2048]{1,0:T(8,128)(2,1)}, bf16[512,2048]{1,0:T(8,128)(2,1)}, f32[512,512]{1,0:T(8,128)S(1)}, f32[512,512]{1,0:T(8,128)S(1)}, bf16[2,512,512]{2,1,0:T(8,128)(2,1)S(1)}) custom-call(bf16[512,2048]{1,0:T(8,128)(2,1)S(1)} %copy-done, ...), custom_call_target="tpu_custom_call", output_to_operand_aliasing={{0}: (12, {}), {1}: (13, {})} | custom-call | tf_op jit(solution)/shard_map/pallas_call | solution.py:37
  50.5 1.0 %shard_map.126 = (bf16[512,2048]{1,0:T(8,128)(2,1)}, bf16[512,2048]{1,0:T(8,128)(2,1)}, bf16[2,512,512]{2,1,0:T(8,128)(2,1)S(1)}) custom-call(f32[3,16,128]{2,1,0:T(8,128)S(1)} %get-tuple-element.118.refs_3_.refs_4_.refs_0_, bf16[512,512]{1,0:T(8,128)(2,1)S(1)} %get-tuple-element.135.refs_1_, ...), custom_call_target="tpu_custom_call", output_to_operand_aliasing={{0}: (8, {}), {1}: (9, {})} | custom-call | tf_op jit(solution)/shard_map/pallas_call | solution.py:37
  51.5 2.1 %collective-permute-done.16.refs_1_ = f32[512,128]{1,0:T(8,128)S(1)} collective-permute-done((f32[512,128]{1,0:T(8,128)S(1)}, f32[512,128]{1,0:T(8,128)S(1)}, u32[]{:S(2)}, u32[]{:S(2)}) %collective-permute-start.16) | collective-permute-done | bytes 262176 | tf_op jit(solution)/shard_map/ppermute | solution.py:394
  53.9 1.5 %shard_map.129 = (bf16[512,2048]{1,0:T(8,128)(2,1)}, bf16[512,2048]{1,0:T(8,128)(2,1)}, bf16[2,512,512]{2,1,0:T(8,128)(2,1)S(1)}) custom-call(f32[3,16,128]{2,1,0:T(8,128)S(1)} %get-tuple-element.118.refs_3_.refs_4_.refs_0_, bf16[512,512]{1,0:T(8,128)(2,1)S(1)} %get-tuple-element.216.refs_1_, bf16[512,512]{1,0:T(8,128)(2,1)S(1)} %get-tuple-element.217.refs_2_, ...), custom_call_target="tpu_custom_call" | custom-call | tf_op jit(solution)/shard_map/pallas_call | solution.py:37
  55.4 1.4 %shard_map.130 = (bf16[512,2048]{1,0:T(8,128)(2,1)}, bf16[512,2048]{1,0:T(8,128)(2,1)}) custom-call(f32[3,16,128]{2,1,0:T(8,128)S(1)} %get-tuple-element.118.refs_3_.refs_4_.refs_0_, bf16[512,512]{1,0:T(8,128)(2,1)S(1)} %get-tuple-element.209.refs_1_, bf16[512,512]{1,0:T(8,128)(2,1)S(1)} %get-tuple-element.210.refs_2_, ...), custom_call_target="tpu_custom_call", output_to_operand_aliasing={{0}: (8, {}), {1}: (9, {})} | custom-call | tf_op jit(solution)/shard_map/pallas_call | solution.py:37
  (39 shorter events, 1.3 us)
Async XLA Ops:
  3.4 1.7 %collective-permute-start = (f32[520,128]{1,0:T(8,128)S(1)}, f32[520,128]{1,0:T(8,128)S(1)}, u32[]{:S(2)}, u32[]{:S(2)}) collective-permute-start(f32[520,128]{1,0:T(8,128)S(1)} %get-tuple-element.125), channel_id=1, source_target_pairs={{0,4},{4,0},{8,12},{12,8},{16,20},{20,16},{24,28},{28,24},{1,5},{5... | collective-permute-start | bytes 798728 | tf_op jit(solution)/shard_map/ppermute | solution.py:390
  4.2 4.0 %collective-permute-start.1 = (f32[512,128]{1,0:T(8,128)S(1)}, f32[512,128]{1,0:T(8,128)S(1)}, u32[]{:S(2)}, u32[]{:S(2)}) collective-permute-start(f32[512,128]{1,0:T(8,128)S(1)} %get-tuple-element.128.refs_4_), channel_id=1, source_target_pairs={{0,4},{4,0},{8,12},{12,8},{16,20},{20,16},{24,28},{28,24},{1,5},{5... | collective-permute-start | bytes 786440 | tf_op jit(solution)/shard_map/ppermute | solution.py:390
  4.7 5.6 %copy-start = (bf16[512,2048]{1,0:T(8,128)(2,1)S(1)}, bf16[512,2048]{1,0:T(8,128)(2,1)}, u32[]{:S(2)}) copy-start(bf16[512,2048]{1,0:T(8,128)(2,1)} %refs_0_.17) | copy-start | bytes 6291460
  5.2 9.6 %collective-permute-start.3 = (f32[520,128]{1,0:T(8,128)S(1)}, f32[520,128]{1,0:T(8,128)S(1)}, u32[]{:S(2)}, u32[]{:S(2)}) collective-permute-start(f32[520,128]{1,0:T(8,128)S(1)} %shard_map.96.refs_1_.refs_9_), channel_id=1, source_target_pairs={{0,8},{4,12},{8,0},{12,4},{16,24},{20,28},{24,16},{28,20},{1,9},{5... | collective-permute-start | bytes 798728 | tf_op jit(solution)/shard_map/ppermute | solution.py:394
  8.2 8.5 %collective-permute-start.2 = (f32[512,128]{1,0:T(8,128)S(1)}, f32[512,128]{1,0:T(8,128)S(1)}, u32[]{:S(2)}, u32[]{:S(2)}) collective-permute-start(f32[512,128]{1,0:T(8,128)S(1)} %shard_map.98.refs_2_.refs_10_.refs_1_), channel_id=1, source_target_pairs={{0,16},{4,20},{8,24},{12,28},{16,0},{20,4},{24,8},{28,12},{1,17},{... | collective-permute-start | bytes 786440 | tf_op jit(solution)/shard_map/ppermute | solution.py:394
  10.0 6.7 %collective-permute-start.4 = (f32[8,128]{1,0:T(8,128)S(1)}, f32[8,128]{1,0:T(8,128)S(1)}, u32[]{:S(2)}, u32[]{:S(2)}) collective-permute-start(f32[8,128]{1,0:T(8,128)S(1)} %slice.103), channel_id=1, source_target_pairs={{0,24},{4,28},{8,16},{12,20},{16,8},{20,12},{24,0},{28,4},{1,25},{... | collective-permute-start | bytes 12296 | tf_op jit(solution)/shard_map/ppermute | solution.py:390
  14.8 7.7 %collective-permute-start.6 = (f32[512,128]{1,0:T(8,128)S(1)}, f32[512,128]{1,0:T(8,128)S(1)}, u32[]{:S(2)}, u32[]{:S(2)}) collective-permute-start(f32[512,128]{1,0:T(8,128)S(1)} %shard_map.105), channel_id=1, source_target_pairs={{0,16},{4,20},{8,24},{12,28},{16,0},{20,4},{24,8},{28,12},{1,17},{... | collective-permute-start | bytes 786440 | tf_op jit(solution)/shard_map/ppermute | solution.py:394
  16.8 7.1 %collective-permute-start.5 = (f32[512,128]{1,0:T(8,128)S(1)}, f32[512,128]{1,0:T(8,128)S(1)}, u32[]{:S(2)}, u32[]{:S(2)}) collective-permute-start(f32[512,128]{1,0:T(8,128)S(1)} %shard_map.102), channel_id=1, source_target_pairs={{0,8},{4,12},{8,0},{12,4},{16,24},{20,28},{24,16},{28,20},{1,9},{5... | collective-permute-start | bytes 786440 | tf_op jit(solution)/shard_map/ppermute | solution.py:394
  22.7 1.6 %collective-permute-start.8 = (f32[512,128]{1,0:T(8,128)S(1)}, f32[512,128]{1,0:T(8,128)S(1)}, u32[]{:S(2)}, u32[]{:S(2)}) collective-permute-start(f32[512,128]{1,0:T(8,128)S(1)} %get-tuple-element.159), channel_id=1, source_target_pairs={{0,4},{4,0},{8,12},{12,8},{16,20},{20,16},{24,28},{28,24},{1,5},{5... | collective-permute-start | bytes 786440 | tf_op jit(solution)/shard_map/ppermute | solution.py:390
  24.0 1.6 %collective-permute-start.7 = (f32[512,128]{1,0:T(8,128)S(1)}, f32[512,128]{1,0:T(8,128)S(1)}, u32[]{:S(2)}, u32[]{:S(2)}) collective-permute-start(f32[512,128]{1,0:T(8,128)S(1)} %get-tuple-element.151), channel_id=1, source_target_pairs={{0,4},{4,0},{8,12},{12,8},{16,20},{20,16},{24,28},{28,24},{1,5},{5... | collective-permute-start | bytes 786440 | tf_op jit(solution)/shard_map/ppermute | solution.py:390
  26.3 3.7 %collective-permute-start.9 = (f32[8,128]{1,0:T(8,128)S(1)}, f32[8,128]{1,0:T(8,128)S(1)}, u32[]{:S(2)}, u32[]{:S(2)}) collective-permute-start(f32[8,128]{1,0:T(8,128)S(1)} %shard_map.112), channel_id=1, source_target_pairs={{0,1},{1,0},{2,3},{3,2},{4,5},{5,4},{6,7},{7,6},{8,9},{9,8},{10,11... | collective-permute-start | bytes 12296 | tf_op jit(solution)/shard_map/ppermute | solution.py:390
  30.0 4.5 %collective-permute-start.10 = (f32[8,128]{1,0:T(8,128)S(1)}, f32[8,128]{1,0:T(8,128)S(1)}, u32[]{:S(2)}, u32[]{:S(2)}) collective-permute-start(f32[8,128]{1,0:T(8,128)S(1)} %add.3.refs_0_), channel_id=1, source_target_pairs={{0,2},{1,3},{2,0},{3,1},{4,6},{5,7},{6,4},{7,5},{8,10},{9,11},{10,... | collective-permute-start | bytes 12296 | tf_op jit(solution)/shard_map/ppermute | solution.py:390
  35.2 1.6 %collective-permute-start.11 = (f32[512,128]{1,0:T(8,128)S(1)}, f32[512,128]{1,0:T(8,128)S(1)}, u32[]{:S(2)}, u32[]{:S(2)}) collective-permute-start(f32[512,128]{1,0:T(8,128)S(1)} %get-tuple-element.179), channel_id=1, source_target_pairs={{0,4},{4,0},{8,12},{12,8},{16,20},{20,16},{24,28},{28,24},{1,5},{5... | collective-permute-start | bytes 786440 | tf_op jit(solution)/shard_map/ppermute | solution.py:390
  35.8 3.3 %collective-permute-start.12 = (f32[512,128]{1,0:T(8,128)S(1)}, f32[512,128]{1,0:T(8,128)S(1)}, u32[]{:S(2)}, u32[]{:S(2)}) collective-permute-start(f32[512,128]{1,0:T(8,128)S(1)} %get-tuple-element.182.refs_4_), channel_id=1, source_target_pairs={{0,4},{4,0},{8,12},{12,8},{16,20},{20,16},{24,28},{28,24},{1,5},{5... | collective-permute-start | bytes 786440 | tf_op jit(solution)/shard_map/ppermute | solution.py:390
  36.9 6.9 %collective-permute-start.13 = (f32[512,128]{1,0:T(8,128)S(1)}, f32[512,128]{1,0:T(8,128)S(1)}, u32[]{:S(2)}, u32[]{:S(2)}) collective-permute-start(f32[512,128]{1,0:T(8,128)S(1)} %shard_map.117.refs_11_.refs_14_.refs_1_), channel_id=1, source_target_pairs={{0,8},{4,20},{8,0},{12,28},{16,24},{20,4},{24,16},{28,12},{1,9},{5... | collective-permute-start | bytes 786440 | tf_op jit(solution)/shard_map/ppermute | solution.py:394
  39.1 8.1 %collective-permute-start.15 = (f32[512,128]{1,0:T(8,128)S(1)}, f32[512,128]{1,0:T(8,128)S(1)}, u32[]{:S(2)}, u32[]{:S(2)}) collective-permute-start(f32[512,128]{1,0:T(8,128)S(1)} %shard_map.119.refs_12_.refs_15_.refs_1_), channel_id=1, source_target_pairs={{0,8},{4,20},{8,0},{12,28},{16,24},{20,4},{24,16},{28,12},{1,9},{5... | collective-permute-start | bytes 786440 | tf_op jit(solution)/shard_map/ppermute | solution.py:394
  43.9 6.4 %collective-permute-start.14 = (f32[512,128]{1,0:T(8,128)S(1)}, f32[512,128]{1,0:T(8,128)S(1)}, u32[]{:S(2)}, u32[]{:S(2)}) collective-permute-start(f32[512,128]{1,0:T(8,128)S(1)} %shard_map.122.refs_6_), channel_id=1, source_target_pairs={{0,16},{4,12},{8,24},{12,4},{16,0},{20,28},{24,8},{28,20},{1,17},{... | collective-permute-start | bytes 786440 | tf_op jit(solution)/shard_map/ppermute | solution.py:394
  47.2 6.4 %collective-permute-start.16 = (f32[512,128]{1,0:T(8,128)S(1)}, f32[512,128]{1,0:T(8,128)S(1)}, u32[]{:S(2)}, u32[]{:S(2)}) collective-permute-start(f32[512,128]{1,0:T(8,128)S(1)} %shard_map.127), channel_id=1, source_target_pairs={{0,16},{4,12},{8,24},{12,4},{16,0},{20,28},{24,8},{28,20},{1,17},{... | collective-permute-start | bytes 786440 | tf_op jit(solution)/shard_map/ppermute | solution.py:394
  50.4 3.5 %collective-permute-start.18 = (f32[512,128]{1,0:T(8,128)S(1)}, f32[512,128]{1,0:T(8,128)S(1)}, u32[]{:S(2)}, u32[]{:S(2)}) collective-permute-start(f32[512,128]{1,0:T(8,128)S(1)} %get-tuple-element.220), channel_id=1, source_target_pairs={{0,4},{4,0},{8,12},{12,8},{16,20},{20,16},{24,28},{28,24},{1,5},{5... | collective-permute-start | bytes 786440 | tf_op jit(solution)/shard_map/ppermute | solution.py:390
  53.8 1.6 %collective-permute-start.17 = (f32[512,128]{1,0:T(8,128)S(1)}, f32[512,128]{1,0:T(8,128)S(1)}, u32[]{:S(2)}, u32[]{:S(2)}) collective-permute-start(f32[512,128]{1,0:T(8,128)S(1)} %get-tuple-element.214), channel_id=1, source_target_pairs={{0,4},{4,0},{8,12},{12,8},{16,20},{20,16},{24,28},{28,24},{1,5},{5... | collective-permute-start | bytes 786440 | tf_op jit(solution)/shard_map/ppermute | solution.py:390

commit v4 on v3

--- a/solution.py
+++ b/solution.py
@@ -244,8 +244,13 @@
     made[0][0].wait()
 
 
-def attend_kernel(half, index, query_dec, intra, entering, early, factor, grad_out, gain, *refs):
-    attended, state, squares, crossed = refs[-4:]
+def attend_kernel(half, index, last, query_dec, intra, entering, early, factor, grad_out, gain, *refs):
+    if last:
+        attended, state, sums = refs[-3:]
+        before = refs[:-3]
+    else:
+        attended, state, squares, crossed = refs[-4:]
+        before = refs[:-4]
     states, inters = [], []
     for n, i in enumerate(index):
         now = entering[span(n), :]
@@ -263,18 +268,22 @@
         crosses[c] += (gain[:, cols] * grad_out[at, span(n)].astype(F32)) * out
     for c in range(CHUNKS):
         at = chunk(c)
-        if len(refs) == 6:
-            totals[c], crosses[c] = totals[c] + refs[0][at], crosses[c] + refs[1][at]
-        squares[at, :] = totals[c]
-        crossed[at, :] = crosses[c]
-
-
-def sum_kernel(squares, crossed, sums):
-    square = jnp.sum(squares[...].T, axis=0, keepdims=True)
-    cross = jnp.sum(crossed[...].T, axis=0, keepdims=True)
-    for n in range(BLOCK // E):
-        sums[n : n + 1, :] = square[:, span(n)]
-        sums[n + 4 : n + 5, :] = cross[:, span(n)]
+        if before:
+            totals[c], crosses[c] = totals[c] + before[0][at], crosses[c] + before[1][at]
+        if not last:
+            squares[at, :] = totals[c]
+            crossed[at, :] = crosses[c]
+    if last:
+        sum_rows(totals, crosses, sums)
+
+
+def sum_rows(squares, crosses, sums):
+    for c in range(CHUNKS):
+        for m, terms in enumerate((squares[c], crosses[c])):
+            row = jnp.sum(terms.T, axis=0, keepdims=True)
+            for n in range(CHUNK // E):
+                at = m * (BLOCK // E) + c * (CHUNK // E) + n
+                sums[at : at + 1, :] = row[:, span(n)]
 
 
 def scale_kernel(features, ours, theirs, inverse, coefficient):
@@ -519,8 +528,9 @@
 
     def attend(piece, sums):
         attended[piece], state[piece], *sums = call(
-            functools.partial(attend_kernel, half, index[piece]),
-            [(flat, F32), ((CHUNKS, *tall), BF16), (wide, F32), (wide, F32)],
+            functools.partial(attend_kernel, half, index[piece], piece == late_pieces[-1]),
+            [(flat, F32), ((CHUNKS, *tall), BF16)]
+            + ([((8, E), F32)] if piece == late_pieces[-1] else [(wide, F32)] * 2),
             query_dec[piece], intra[piece], entering[piece], early[piece], factor, grad_here[piece], gain, *sums,
         )
         return sums
@@ -538,7 +548,7 @@
     for piece in late_pieces:
         if piece not in attended:
             sums = attend(piece, sums)
-    (sums,) = call(sum_kernel, [((8, E), F32)], *sums)
+    (sums,) = sums
     inverse, coefficient = call(functools.partial(scale_kernel, features), [(wide, F32)] * 2, *summed(sums))
 
     d_attended, flow, late = {}, {}, {}
@@ -560,7 +570,7 @@
         for g in range(groups):
             if g:
                 outer((g, 0), ())
-            steps.append(first_step(True, flow[g, 0], gots[g], g, [flow[groups - 1, 1]]))
+            steps.append(first_step(True, flow[g, 0], gots[g], g))
         last = [step[2] for step in steps]
 
     full = (queries.shape, BF16)

time: 57.2 us -> 57.2 us (level)
    pallas_call x38 -> x37, Pallas kernels: 26.7 us -> 26.7 us  [call(): pl.pallas_call(body, out_shape=[(pltpu.HBM if n < outs_anywhere else pltp...]
where the time goes in v4:
time: 57.2 us; the launch traced here: 57 us
  Pallas kernels  26.7 us (47%)
  starting transfers between devices  18.4 us (32%)
  waiting for transfers between devices  10.7 us (19%)
  between operations  1.16 us (2%)
    pallas_call x37, Pallas kernels, call(): pl.pallas_call(body, out_shape=[(pltpu.HBM if n < outs_anywhere else pltp...  26.7 us
    ppermute x8, starting transfers between devices, crossing(): lax.ppermute(x, 'ctx', [(i, i ^ (2 if (i % 2 if group is None else group)...  12.3 us
    ppermute x8, waiting for transfers between devices, crossing(): lax.ppermute(x, 'ctx', [(i, i ^ (2 if (i % 2 if group is None else group)...  6.25 us
    ppermute x11, starting transfers between devices, exchange(): lax.ppermute(x, axis, [(i, i ^ bit) for i in range(lax.axis_size(axis))])  6.09 us
    ppermute x11, waiting for transfers between devices, exchange(): lax.ppermute(x, axis, [(i, i ^ bit) for i in range(lax.axis_size(axis))])  4.46 us
  transfers between devices with their start and end apart: 19, of which 9 were waited for; matrix products, arithmetic and copies ran while one was open for 0% of the time, Pallas kernels for 37%

profile of v4, /device:TPU:0, one launch (start us, length us, event | category | flops | bytes accessed | tf_op | source)
XLA Modules:
  0.0 57.0 jit_solution(14656474090707016958)
XLA Ops:
  0.6 2.7 %shard_map.93 = (f32[16,512]{1,0:T(8,128)S(1)}, f32[16,512]{1,0:T(8,128)S(1)}, f32[16,512]{1,0:T(8,128)S(1)}, f32[3,16,128]{2,1,0:T(8,128)S(1)}, f32[1,2048]{1,0...) custom-call(f32[16,512]{1,0:T(8,128)} %refs_0_.9, ...), custom_call_target="tpu_custom_call" | custom-call | tf_op jit(solution)/shard_map/pallas_call | solution.py:37
  3.4 0.5 collective-permute-start
  3.8 0.3 shard_map.95
  4.2 0.2 collective-permute-start.1
  4.4 0.3 shard_map.94
  4.7 0.4 shard_map.97
  5.2 3.0 %collective-permute-start.3 = (f32[520,128]{1,0:T(8,128)S(1)}, f32[520,128]{1,0:T(8,128)S(1)}, u32[]{:S(2)}, u32[]{:S(2)}) collective-permute-start(f32[520,128]{1,0:T(8,128)S(1)} %shard_map.96.refs_1_.refs_9_), channel_id=1, source_target_pairs={{0,8},{4,12},{8,0},{12,4},{16,24},{20,28},{24,16},{28,20},{1,9},{5... | collective-permute-start | bytes 798728 | tf_op jit(solution)/shard_map/ppermute | solution.py:403
  8.2 1.6 %collective-permute-start.2 = (f32[512,128]{1,0:T(8,128)S(1)}, f32[512,128]{1,0:T(8,128)S(1)}, u32[]{:S(2)}, u32[]{:S(2)}) collective-permute-start(f32[512,128]{1,0:T(8,128)S(1)} %shard_map.98.refs_2_.refs_10_.refs_1_), channel_id=1, source_target_pairs={{0,16},{4,20},{8,24},{12,28},{16,0},{20,4},{24,8},{28,12},{1,17},{... | collective-permute-start | bytes 786440 | tf_op jit(solution)/shard_map/ppermute | solution.py:403
  9.8 0.2 shard_map.99
  10.0 0.3 collective-permute-start.4
  10.3 1.4 %shard_map.100 = (f32[512,512]{1,0:T(8,128)S(1)}, bf16[512,512]{1,0:T(8,128)(2,1)S(1)}, bf16[512,512]{1,0:T(8,128)(2,1)S(1)}, bf16[512,512]{1,0:T(8,128)(2,1)S(1...) custom-call(bf16[512,2048]{1,0:T(8,128)(2,1)} %refs_0_.13, bf16[512,2048]{1,0:T(8,128)(2,1)S(1)} %copy-done, ...), custom_call_target="tpu_custom_call" | custom-call | tf_op jit(solution)/shard_map/pallas_call | solution.py:37
  11.6 1.4 %shard_map.104 = (f32[512,512]{1,0:T(8,128)S(1)}, bf16[512,512]{1,0:T(8,128)(2,1)S(1)}, bf16[512,512]{1,0:T(8,128)(2,1)S(1)}, bf16[512,512]{1,0:T(8,128)(2,1)S(1...) custom-call(bf16[512,2048]{1,0:T(8,128)(2,1)} %refs_0_.13, bf16[512,2048]{1,0:T(8,128)(2,1)S(1)} %copy-done, ...), custom_call_target="tpu_custom_call" | custom-call | tf_op jit(solution)/shard_map/pallas_call | solution.py:37
  13.0 1.8 %collective-permute-done.3.refs_0_ = f32[520,128]{1,0:T(8,128)S(1)} collective-permute-done((f32[520,128]{1,0:T(8,128)S(1)}, f32[520,128]{1,0:T(8,128)S(1)}, u32[]{:S(2)}, u32[]{:S(2)}) %collective-permute-start.3) | collective-permute-done | bytes 266272 | tf_op jit(solution)/shard_map/ppermute | solution.py:403
  14.8 1.8 %collective-permute-start.6 = (f32[512,128]{1,0:T(8,128)S(1)}, f32[512,128]{1,0:T(8,128)S(1)}, u32[]{:S(2)}, u32[]{:S(2)}) collective-permute-start(f32[512,128]{1,0:T(8,128)S(1)} %shard_map.105), channel_id=1, source_target_pairs={{0,16},{4,20},{8,24},{12,28},{16,0},{20,4},{24,8},{28,12},{1,17},{... | collective-permute-start | bytes 786440 | tf_op jit(solution)/shard_map/ppermute | solution.py:403
  16.8 1.6 %collective-permute-start.5 = (f32[512,128]{1,0:T(8,128)S(1)}, f32[512,128]{1,0:T(8,128)S(1)}, u32[]{:S(2)}, u32[]{:S(2)}) collective-permute-start(f32[512,128]{1,0:T(8,128)S(1)} %shard_map.102), channel_id=1, source_target_pairs={{0,8},{4,12},{8,0},{12,4},{16,24},{20,28},{24,16},{28,20},{1,9},{5... | collective-permute-start | bytes 786440 | tf_op jit(solution)/shard_map/ppermute | solution.py:403
  18.3 1.3 %shard_map.101 = (f32[512,512]{1,0:T(8,128)S(1)}, bf16[512,512]{1,0:T(8,128)(2,1)S(1)}, bf16[512,512]{1,0:T(8,128)(2,1)S(1)}, bf16[512,512]{1,0:T(8,128)(2,1)S(1...) custom-call(bf16[512,2048]{1,0:T(8,128)(2,1)} %refs_0_.13, bf16[512,2048]{1,0:T(8,128)(2,1)S(1)} %copy-done, ...), custom_call_target="tpu_custom_call" | custom-call | tf_op jit(solution)/shard_map/pallas_call | solution.py:37
  19.6 1.3 %shard_map.103 = (f32[512,512]{1,0:T(8,128)S(1)}, bf16[512,512]{1,0:T(8,128)(2,1)S(1)}, bf16[512,512]{1,0:T(8,128)(2,1)S(1)}, bf16[512,512]{1,0:T(8,128)(2,1)S(1...) custom-call(bf16[512,2048]{1,0:T(8,128)(2,1)} %refs_0_.13, bf16[512,2048]{1,0:T(8,128)(2,1)S(1)} %copy-done, ...), custom_call_target="tpu_custom_call" | custom-call | tf_op jit(solution)/shard_map/pallas_call | solution.py:37
  21.0 1.6 %collective-permute-done.6.refs_1_ = f32[512,128]{1,0:T(8,128)S(1)} collective-permute-done((f32[512,128]{1,0:T(8,128)S(1)}, f32[512,128]{1,0:T(8,128)S(1)}, u32[]{:S(2)}, u32[]{:S(2)}) %collective-permute-start.6) | collective-permute-done | bytes 262176 | tf_op jit(solution)/shard_map/ppermute | solution.py:403
  22.8 0.5 shard_map.107
  23.2 0.6 %collective-permute-done.5.refs_1_ = f32[512,128]{1,0:T(8,128)S(1)} collective-permute-done((f32[512,128]{1,0:T(8,128)S(1)}, f32[512,128]{1,0:T(8,128)S(1)}, u32[]{:S(2)}, u32[]{:S(2)}) %collective-permute-start.5) | collective-permute-done | bytes 262176 | tf_op jit(solution)/shard_map/ppermute | solution.py:403
  24.1 0.2 collective-permute-done.8.refs_2_
  24.3 0.5 shard_map.109
  24.8 0.5 shard_map.110
  25.3 0.3 collective-permute-done.7.refs_2_
  25.6 0.7 %shard_map.111 = (f32[512,512]{1,0:T(8,128)S(1)}, bf16[2,512,128]{2,1,0:T(8,128)(2,1)S(1)}, f32[8,128]{1,0:T(8,128)S(1)}) custom-call(bf16[512,512]{1,0:T(8,128)(2,1)S(1)} %get-tuple-element.136.refs_0_, f32[512,512]{1,0:T(8,128)S(1)} %get-tuple-element.137.refs_9_.refs_1_, f32[512,128]{1,0:T(8,128)S(1)} %collective-permute-done.7.refs_2_, ...), custom_call_target="tpu_custom_call" | custom-call | tf_op jit(solution)/shard_map/pallas_call | solution.py:37
  26.3 1.7 %collective-permute-start.9 = (f32[8,128]{1,0:T(8,128)S(1)}, f32[8,128]{1,0:T(8,128)S(1)}, u32[]{:S(2)}, u32[]{:S(2)}) collective-permute-start(f32[8,128]{1,0:T(8,128)S(1)} %get-tuple-element.165), channel_id=1, source_target_pairs={{0,1},{1,0},{2,3},{3,2},{4,5},{5,4},{6,7},{7,6},{8,9},{9,8},{10,11... | collective-permute-start | bytes 12296 | tf_op jit(solution)/shard_map/ppermute | solution.py:399
  27.9 2.0 %collective-permute-done.9 = f32[8,128]{1,0:T(8,128)S(1)} collective-permute-done((f32[8,128]{1,0:T(8,128)S(1)}, f32[8,128]{1,0:T(8,128)S(1)}, u32[]{:S(2)}, u32[]{:S(2)}) %collective-permute-start.9) | collective-permute-done | bytes 4128 | tf_op jit(solution)/shard_map/ppermute | solution.py:399
  30.0 2.6 %collective-permute-start.10 = (f32[8,128]{1,0:T(8,128)S(1)}, f32[8,128]{1,0:T(8,128)S(1)}, u32[]{:S(2)}, u32[]{:S(2)}) collective-permute-start(f32[8,128]{1,0:T(8,128)S(1)} %add.3.refs_0_), channel_id=1, source_target_pairs={{0,2},{1,3},{2,0},{3,1},{4,6},{5,7},{6,4},{7,5},{8,10},{9,11},{10,... | collective-permute-start | bytes 12296 | tf_op jit(solution)/shard_map/ppermute | solution.py:399
  32.6 1.9 %collective-permute-done.10.refs_1_ = f32[8,128]{1,0:T(8,128)S(1)} collective-permute-done((f32[8,128]{1,0:T(8,128)S(1)}, f32[8,128]{1,0:T(8,128)S(1)}, u32[]{:S(2)}, u32[]{:S(2)}) %collective-permute-start.10) | collective-permute-done | bytes 4128 | tf_op jit(solution)/shard_map/ppermute | solution.py:399
  34.5 0.2 shard_map.112
  34.7 0.5 shard_map.114
  35.2 0.5 shard_map.117
  35.7 0.6 collective-permute-start.12
  36.3 0.5 shard_map.113
  36.9 1.6 %collective-permute-start.13 = (f32[512,128]{1,0:T(8,128)S(1)}, f32[512,128]{1,0:T(8,128)S(1)}, u32[]{:S(2)}, u32[]{:S(2)}) collective-permute-start(f32[512,128]{1,0:T(8,128)S(1)} %shard_map.115.refs_11_.refs_14_.refs_1_), channel_id=1, source_target_pairs={{0,8},{4,20},{8,0},{12,28},{16,24},{20,4},{24,16},{28,12},{1,9},{5... | collective-permute-start | bytes 786440 | tf_op jit(solution)/shard_map/ppermute | solution.py:403
  38.4 0.5 shard_map.116
  39.0 0.6 %collective-permute-start.15 = (f32[512,128]{1,0:T(8,128)S(1)}, f32[512,128]{1,0:T(8,128)S(1)}, u32[]{:S(2)}, u32[]{:S(2)}) collective-permute-start(f32[512,128]{1,0:T(8,128)S(1)} %shard_map.118.refs_12_.refs_15_.refs_1_), channel_id=1, source_target_pairs={{0,8},{4,20},{8,0},{12,28},{16,24},{20,4},{24,16},{28,12},{1,9},{5... | collective-permute-start | bytes 786440 | tf_op jit(solution)/shard_map/ppermute | solution.py:403
  39.6 2.0 %shard_map.119 = (bf16[512,2048]{1,0:T(8,128)(2,1)}, bf16[512,2048]{1,0:T(8,128)(2,1)}, f32[512,512]{1,0:T(8,128)S(1)}, f32[512,512]{1,0:T(8,128)S(1)}, bf16[2,512,512]{2,1,0:T(8,128)(2,1)S(1)}) custom-call(bf16[512,2048]{1,0:T(8,128)(2,1)S(1)} %copy-done, bf16[512,512]{1,0:T(8,128)(2,1)S(1)} %get-tuple-element.141.refs_2_.refs_1_, ...), custom_call_target="tpu_custom_call" | custom-call | tf_op jit(solution)/shard_map/pallas_call | solution.py:37
  41.7 2.1 %shard_map.120 = (bf16[512,2048]{1,0:T(8,128)(2,1)}, bf16[512,2048]{1,0:T(8,128)(2,1)}, f32[512,512]{1,0:T(8,128)S(1)}, f32[512,512]{1,0:T(8,128)S(1)}, bf16[2,512,512]{2,1,0:T(8,128)(2,1)S(1)}) custom-call(bf16[512,2048]{1,0:T(8,128)(2,1)S(1)} %copy-done, ...), custom_call_target="tpu_custom_call", output_to_operand_aliasing={{0}: (12, {}), {1}: (13, {})} | custom-call | tf_op jit(solution)/shard_map/pallas_call | solution.py:37
  43.8 1.2 %collective-permute-start.14 = (f32[512,128]{1,0:T(8,128)S(1)}, f32[512,128]{1,0:T(8,128)S(1)}, u32[]{:S(2)}, u32[]{:S(2)}) collective-permute-start(f32[512,128]{1,0:T(8,128)S(1)} %shard_map.121.refs_6_), channel_id=1, source_target_pairs={{0,16},{4,12},{8,24},{12,4},{16,0},{20,28},{24,8},{28,20},{1,17},{... | collective-permute-start | bytes 786440 | tf_op jit(solution)/shard_map/ppermute | solution.py:403
  45.1 2.0 %shard_map.122 = (bf16[512,2048]{1,0:T(8,128)(2,1)}, bf16[512,2048]{1,0:T(8,128)(2,1)}, f32[512,512]{1,0:T(8,128)S(1)}, f32[512,512]{1,0:T(8,128)S(1)}, bf16[2,512,512]{2,1,0:T(8,128)(2,1)S(1)}) custom-call(bf16[512,2048]{1,0:T(8,128)(2,1)S(1)} %copy-done, ...), custom_call_target="tpu_custom_call", output_to_operand_aliasing={{0}: (12, {}), {1}: (13, {})} | custom-call | tf_op jit(solution)/shard_map/pallas_call | solution.py:37
  47.2 0.9 %collective-permute-start.16 = (f32[512,128]{1,0:T(8,128)S(1)}, f32[512,128]{1,0:T(8,128)S(1)}, u32[]{:S(2)}, u32[]{:S(2)}) collective-permute-start(f32[512,128]{1,0:T(8,128)S(1)} %shard_map.126), channel_id=1, source_target_pairs={{0,16},{4,12},{8,24},{12,4},{16,0},{20,28},{24,8},{28,20},{1,17},{... | collective-permute-start | bytes 786440 | tf_op jit(solution)/shard_map/ppermute | solution.py:403
  48.1 2.0 %shard_map.123 = (bf16[512,2048]{1,0:T(8,128)(2,1)}, bf16[512,2048]{1,0:T(8,128)(2,1)}, f32[512,512]{1,0:T(8,128)S(1)}, f32[512,512]{1,0:T(8,128)S(1)}, bf16[2,512,512]{2,1,0:T(8,128)(2,1)S(1)}) custom-call(bf16[512,2048]{1,0:T(8,128)(2,1)S(1)} %copy-done, ...), custom_call_target="tpu_custom_call", output_to_operand_aliasing={{0}: (12, {}), {1}: (13, {})} | custom-call | tf_op jit(solution)/shard_map/pallas_call | solution.py:37
  50.4 1.0 %shard_map.125 = (bf16[512,2048]{1,0:T(8,128)(2,1)}, bf16[512,2048]{1,0:T(8,128)(2,1)}, bf16[2,512,512]{2,1,0:T(8,128)(2,1)S(1)}) custom-call(f32[3,16,128]{2,1,0:T(8,128)S(1)} %get-tuple-element.117.refs_3_.refs_4_.refs_0_, bf16[512,512]{1,0:T(8,128)(2,1)S(1)} %get-tuple-element.134.refs_1_, ...), custom_call_target="tpu_custom_call", output_to_operand_aliasing={{0}: (8, {}), {1}: (9, {})} | custom-call | tf_op jit(solution)/shard_map/pallas_call | solution.py:37
  51.5 2.1 %collective-permute-done.16.refs_1_ = f32[512,128]{1,0:T(8,128)S(1)} collective-permute-done((f32[512,128]{1,0:T(8,128)S(1)}, f32[512,128]{1,0:T(8,128)S(1)}, u32[]{:S(2)}, u32[]{:S(2)}) %collective-permute-start.16) | collective-permute-done | bytes 262176 | tf_op jit(solution)/shard_map/ppermute | solution.py:403
  53.6 0.1 shard_map.127
  53.8 1.5 %shard_map.128 = (bf16[512,2048]{1,0:T(8,128)(2,1)}, bf16[512,2048]{1,0:T(8,128)(2,1)}, bf16[2,512,512]{2,1,0:T(8,128)(2,1)S(1)}) custom-call(f32[3,16,128]{2,1,0:T(8,128)S(1)} %get-tuple-element.117.refs_3_.refs_4_.refs_0_, bf16[512,512]{1,0:T(8,128)(2,1)S(1)} %get-tuple-element.214.refs_1_, bf16[512,512]{1,0:T(8,128)(2,1)S(1)} %get-tuple-element.215.refs_2_, ...), custom_call_target="tpu_custom_call" | custom-call | tf_op jit(solution)/shard_map/pallas_call | solution.py:37
  55.4 1.4 %shard_map.129 = (bf16[512,2048]{1,0:T(8,128)(2,1)}, bf16[512,2048]{1,0:T(8,128)(2,1)}) custom-call(f32[3,16,128]{2,1,0:T(8,128)S(1)} %get-tuple-element.117.refs_3_.refs_4_.refs_0_, bf16[512,512]{1,0:T(8,128)(2,1)S(1)} %get-tuple-element.207.refs_1_, bf16[512,512]{1,0:T(8,128)(2,1)S(1)} %get-tuple-element.208.refs_2_, ...), custom_call_target="tpu_custom_call", output_to_operand_aliasing={{0}: (8, {}), {1}: (9, {})} | custom-call | tf_op jit(solution)/shard_map/pallas_call | solution.py:37
  (38 shorter events, 1.2 us)
Async XLA Ops:
  3.4 1.7 %collective-permute-start = (f32[520,128]{1,0:T(8,128)S(1)}, f32[520,128]{1,0:T(8,128)S(1)}, u32[]{:S(2)}, u32[]{:S(2)}) collective-permute-start(f32[520,128]{1,0:T(8,128)S(1)} %get-tuple-element.124), channel_id=1, source_target_pairs={{0,4},{4,0},{8,12},{12,8},{16,20},{20,16},{24,28},{28,24},{1,5},{5... | collective-permute-start | bytes 798728 | tf_op jit(solution)/shard_map/ppermute | solution.py:399
  4.2 4.0 %collective-permute-start.1 = (f32[512,128]{1,0:T(8,128)S(1)}, f32[512,128]{1,0:T(8,128)S(1)}, u32[]{:S(2)}, u32[]{:S(2)}) collective-permute-start(f32[512,128]{1,0:T(8,128)S(1)} %get-tuple-element.127.refs_4_), channel_id=1, source_target_pairs={{0,4},{4,0},{8,12},{12,8},{16,20},{20,16},{24,28},{28,24},{1,5},{5... | collective-permute-start | bytes 786440 | tf_op jit(solution)/shard_map/ppermute | solution.py:399
  4.7 5.6 %copy-start = (bf16[512,2048]{1,0:T(8,128)(2,1)S(1)}, bf16[512,2048]{1,0:T(8,128)(2,1)}, u32[]{:S(2)}) copy-start(bf16[512,2048]{1,0:T(8,128)(2,1)} %refs_0_.17) | copy-start | bytes 6291460
  5.2 9.6 %collective-permute-start.3 = (f32[520,128]{1,0:T(8,128)S(1)}, f32[520,128]{1,0:T(8,128)S(1)}, u32[]{:S(2)}, u32[]{:S(2)}) collective-permute-start(f32[520,128]{1,0:T(8,128)S(1)} %shard_map.96.refs_1_.refs_9_), channel_id=1, source_target_pairs={{0,8},{4,12},{8,0},{12,4},{16,24},{20,28},{24,16},{28,20},{1,9},{5... | collective-permute-start | bytes 798728 | tf_op jit(solution)/shard_map/ppermute | solution.py:403
  8.2 8.5 %collective-permute-start.2 = (f32[512,128]{1,0:T(8,128)S(1)}, f32[512,128]{1,0:T(8,128)S(1)}, u32[]{:S(2)}, u32[]{:S(2)}) collective-permute-start(f32[512,128]{1,0:T(8,128)S(1)} %shard_map.98.refs_2_.refs_10_.refs_1_), channel_id=1, source_target_pairs={{0,16},{4,20},{8,24},{12,28},{16,0},{20,4},{24,8},{28,12},{1,17},{... | collective-permute-start | bytes 786440 | tf_op jit(solution)/shard_map/ppermute | solution.py:403
  10.0 6.7 %collective-permute-start.4 = (f32[8,128]{1,0:T(8,128)S(1)}, f32[8,128]{1,0:T(8,128)S(1)}, u32[]{:S(2)}, u32[]{:S(2)}) collective-permute-start(f32[8,128]{1,0:T(8,128)S(1)} %slice.103), channel_id=1, source_target_pairs={{0,24},{4,28},{8,16},{12,20},{16,8},{20,12},{24,0},{28,4},{1,25},{... | collective-permute-start | bytes 12296 | tf_op jit(solution)/shard_map/ppermute | solution.py:399
  14.8 7.7 %collective-permute-start.6 = (f32[512,128]{1,0:T(8,128)S(1)}, f32[512,128]{1,0:T(8,128)S(1)}, u32[]{:S(2)}, u32[]{:S(2)}) collective-permute-start(f32[512,128]{1,0:T(8,128)S(1)} %shard_map.105), channel_id=1, source_target_pairs={{0,16},{4,20},{8,24},{12,28},{16,0},{20,4},{24,8},{28,12},{1,17},{... | collective-permute-start | bytes 786440 | tf_op jit(solution)/shard_map/ppermute | solution.py:403
  16.8 7.1 %collective-permute-start.5 = (f32[512,128]{1,0:T(8,128)S(1)}, f32[512,128]{1,0:T(8,128)S(1)}, u32[]{:S(2)}, u32[]{:S(2)}) collective-permute-start(f32[512,128]{1,0:T(8,128)S(1)} %shard_map.102), channel_id=1, source_target_pairs={{0,8},{4,12},{8,0},{12,4},{16,24},{20,28},{24,16},{28,20},{1,9},{5... | collective-permute-start | bytes 786440 | tf_op jit(solution)/shard_map/ppermute | solution.py:403
  22.7 1.6 %collective-permute-start.8 = (f32[512,128]{1,0:T(8,128)S(1)}, f32[512,128]{1,0:T(8,128)S(1)}, u32[]{:S(2)}, u32[]{:S(2)}) collective-permute-start(f32[512,128]{1,0:T(8,128)S(1)} %get-tuple-element.158), channel_id=1, source_target_pairs={{0,4},{4,0},{8,12},{12,8},{16,20},{20,16},{24,28},{28,24},{1,5},{5... | collective-permute-start | bytes 786440 | tf_op jit(solution)/shard_map/ppermute | solution.py:399
  24.0 1.6 %collective-permute-start.7 = (f32[512,128]{1,0:T(8,128)S(1)}, f32[512,128]{1,0:T(8,128)S(1)}, u32[]{:S(2)}, u32[]{:S(2)}) collective-permute-start(f32[512,128]{1,0:T(8,128)S(1)} %get-tuple-element.150), channel_id=1, source_target_pairs={{0,4},{4,0},{8,12},{12,8},{16,20},{20,16},{24,28},{28,24},{1,5},{5... | collective-permute-start | bytes 786440 | tf_op jit(solution)/shard_map/ppermute | solution.py:399
  26.3 3.7 %collective-permute-start.9 = (f32[8,128]{1,0:T(8,128)S(1)}, f32[8,128]{1,0:T(8,128)S(1)}, u32[]{:S(2)}, u32[]{:S(2)}) collective-permute-start(f32[8,128]{1,0:T(8,128)S(1)} %get-tuple-element.165), channel_id=1, source_target_pairs={{0,1},{1,0},{2,3},{3,2},{4,5},{5,4},{6,7},{7,6},{8,9},{9,8},{10,11... | collective-permute-start | bytes 12296 | tf_op jit(solution)/shard_map/ppermute | solution.py:399
  30.0 4.5 %collective-permute-start.10 = (f32[8,128]{1,0:T(8,128)S(1)}, f32[8,128]{1,0:T(8,128)S(1)}, u32[]{:S(2)}, u32[]{:S(2)}) collective-permute-start(f32[8,128]{1,0:T(8,128)S(1)} %add.3.refs_0_), channel_id=1, source_target_pairs={{0,2},{1,3},{2,0},{3,1},{4,6},{5,7},{6,4},{7,5},{8,10},{9,11},{10,... | collective-permute-start | bytes 12296 | tf_op jit(solution)/shard_map/ppermute | solution.py:399
  35.2 1.6 %collective-permute-start.11 = (f32[512,128]{1,0:T(8,128)S(1)}, f32[512,128]{1,0:T(8,128)S(1)}, u32[]{:S(2)}, u32[]{:S(2)}) collective-permute-start(f32[512,128]{1,0:T(8,128)S(1)} %get-tuple-element.177), channel_id=1, source_target_pairs={{0,4},{4,0},{8,12},{12,8},{16,20},{20,16},{24,28},{28,24},{1,5},{5... | collective-permute-start | bytes 786440 | tf_op jit(solution)/shard_map/ppermute | solution.py:399
  35.7 3.2 %collective-permute-start.12 = (f32[512,128]{1,0:T(8,128)S(1)}, f32[512,128]{1,0:T(8,128)S(1)}, u32[]{:S(2)}, u32[]{:S(2)}) collective-permute-start(f32[512,128]{1,0:T(8,128)S(1)} %get-tuple-element.183), channel_id=1, source_target_pairs={{0,4},{4,0},{8,12},{12,8},{16,20},{20,16},{24,28},{28,24},{1,5},{5... | collective-permute-start | bytes 786440 | tf_op jit(solution)/shard_map/ppermute | solution.py:399
  36.9 6.9 %collective-permute-start.13 = (f32[512,128]{1,0:T(8,128)S(1)}, f32[512,128]{1,0:T(8,128)S(1)}, u32[]{:S(2)}, u32[]{:S(2)}) collective-permute-start(f32[512,128]{1,0:T(8,128)S(1)} %shard_map.115.refs_11_.refs_14_.refs_1_), channel_id=1, source_target_pairs={{0,8},{4,20},{8,0},{12,28},{16,24},{20,4},{24,16},{28,12},{1,9},{5... | collective-permute-start | bytes 786440 | tf_op jit(solution)/shard_map/ppermute | solution.py:403
  39.0 8.1 %collective-permute-start.15 = (f32[512,128]{1,0:T(8,128)S(1)}, f32[512,128]{1,0:T(8,128)S(1)}, u32[]{:S(2)}, u32[]{:S(2)}) collective-permute-start(f32[512,128]{1,0:T(8,128)S(1)} %shard_map.118.refs_12_.refs_15_.refs_1_), channel_id=1, source_target_pairs={{0,8},{4,20},{8,0},{12,28},{16,24},{20,4},{24,16},{28,12},{1,9},{5... | collective-permute-start | bytes 786440 | tf_op jit(solution)/shard_map/ppermute | solution.py:403
  43.8 6.4 %collective-permute-start.14 = (f32[512,128]{1,0:T(8,128)S(1)}, f32[512,128]{1,0:T(8,128)S(1)}, u32[]{:S(2)}, u32[]{:S(2)}) collective-permute-start(f32[512,128]{1,0:T(8,128)S(1)} %shard_map.121.refs_6_), channel_id=1, source_target_pairs={{0,16},{4,12},{8,24},{12,4},{16,0},{20,28},{24,8},{28,20},{1,17},{... | collective-permute-start | bytes 786440 | tf_op jit(solution)/shard_map/ppermute | solution.py:403
  47.2 6.4 %collective-permute-start.16 = (f32[512,128]{1,0:T(8,128)S(1)}, f32[512,128]{1,0:T(8,128)S(1)}, u32[]{:S(2)}, u32[]{:S(2)}) collective-permute-start(f32[512,128]{1,0:T(8,128)S(1)} %shard_map.126), channel_id=1, source_target_pairs={{0,16},{4,12},{8,24},{12,4},{16,0},{20,28},{24,8},{28,20},{1,17},{... | collective-permute-start | bytes 786440 | tf_op jit(solution)/shard_map/ppermute | solution.py:403
  50.4 3.5 %collective-permute-start.18 = (f32[512,128]{1,0:T(8,128)S(1)}, f32[512,128]{1,0:T(8,128)S(1)}, u32[]{:S(2)}, u32[]{:S(2)}) collective-permute-start(f32[512,128]{1,0:T(8,128)S(1)} %get-tuple-element.218), channel_id=1, source_target_pairs={{0,4},{4,0},{8,12},{12,8},{16,20},{20,16},{24,28},{28,24},{1,5},{5... | collective-permute-start | bytes 786440 | tf_op jit(solution)/shard_map/ppermute | solution.py:399
  53.7 1.6 %collective-permute-start.17 = (f32[512,128]{1,0:T(8,128)S(1)}, f32[512,128]{1,0:T(8,128)S(1)}, u32[]{:S(2)}, u32[]{:S(2)}) collective-permute-start(f32[512,128]{1,0:T(8,128)S(1)} %get-tuple-element.212), channel_id=1, source_target_pairs={{0,4},{4,0},{8,12},{12,8},{16,20},{20,16},{24,28},{28,24},{1,5},{5... | collective-permute-start | bytes 786440 | tf_op jit(solution)/shard_map/ppermute | solution.py:399
